TPU v7x, 32 devices: a whole 2x2x4 slice. The times are simulated.
32 devices in a mesh: dp: 8 (over z, x), tensor: 4 (over y, core).
Axes of the slice: x: 2, y: 2, z: 4, core: 2. Of those that a mesh axis runs over, the one named last changes fastest.
Arguments:
- hidden_first: bfloat16 [1024, 2048], P('dp', 'tensor'), may hold values from -6 to 6
- hidden_second: bfloat16 [1024, 2048], P('dp', 'tensor'), may hold values from -6 to 6
- cotangent: bfloat16 [1024, 2048], P('dp', 'tensor'), may hold values from -6 to 6
- depths: int32 [1024], P('dp'), may hold values from 0 to 2, as said below
- norm_gain: float32 [2048], replicated, may hold values from 0.5 to 1.5
- router: float32 [2, 2048], replicated, may hold values from -0.125 to 0.125
- w_gate: bfloat16 [2048, 4096], P(None, 'tensor'), may hold values from -0.125 to 0.125
- w_up: bfloat16 [2048, 4096], P(None, 'tensor'), may hold values from -0.125 to 0.125
- w_down: bfloat16 [4096, 2048], P('tensor'), may hold values from -0.09375 to 0.09375
Outputs:
- grad_first: bfloat16 [1024, 2048], P('dp', 'tensor')
Inputs may be any that keep to these rules, and one draw needn't show every extreme that they name: `depths`: exactly 512 tokens have depth 1 or more and exactly 256 have depth 2; the active tokens are unevenly spread over the tokens of one dp index.
All inputs are finite; a program needn't handle non-finite values.
Results may differ from a plain program's by a relative error of at most 0.02.
Values may be sent and summed in bfloat16 or wider, within the bound.
No kernel may reach another device: no remote copies, remote signals or barrier semaphores. Data moves between devices by JAX's collectives and lax.ppermute only.
A program may use at most 64 MiB of HBM per device.

v0:
```python
import jax
import jax.numpy as jnp
from jax import lax
from jax.sharding import PartitionSpec as P

epsilon = 1e-06


def contract_first(left, right):
    return lax.dot_general(
        left, right, (((0,), (0,)), ((), ())), preferred_element_type=jnp.float32
    )


def contract_last(left, right):
    return lax.dot_general(
        left, right, (((1,), (1,)), ((), ())), preferred_element_type=jnp.float32
    )


def block_grad(x_slice, cot_slice, row_mask, router_row, norm_gain, w_gate, w_up, w_down):
    feat = x_slice.shape[1]
    start = lax.axis_index("tensor") * feat
    full_x, full_cot = (
        lax.all_gather(x_slice, "tensor", axis=1, tiled=True),
        lax.all_gather(cot_slice, "tensor", axis=1, tiled=True),
    )
    wide = full_x.shape[1]
    x_float = full_x.astype(jnp.float32)
    inv_rms = lax.rsqrt(jnp.mean(x_float * x_float, axis=1, keepdims=True) + epsilon)
    normed = (x_float * inv_rms * norm_gain).astype(jnp.bfloat16)
    gate_pre = jnp.dot(normed, w_gate, preferred_element_type=jnp.float32)
    up_pre = jnp.dot(normed, w_up, preferred_element_type=jnp.float32)
    sigma = jax.nn.sigmoid(gate_pre)
    silu_val = gate_pre * sigma
    hidden_act = (silu_val * up_pre).astype(jnp.bfloat16)
    score = jax.nn.sigmoid(jnp.dot(x_float, router_row, precision=lax.Precision.HIGHEST))
    back_hidden = contract_last(full_cot, w_down)
    score_part = jnp.sum(hidden_act.astype(jnp.float32) * back_hidden, axis=1)
    scaled = score[:, None] * back_hidden
    grad_gate = (scaled * up_pre * sigma * (1.0 + gate_pre * (1.0 - sigma))).astype(jnp.bfloat16)
    grad_up = (scaled * silu_val).astype(jnp.bfloat16)
    norm_part = contract_last(grad_gate, w_gate) + contract_last(grad_up, w_up)
    router_slice = lax.dynamic_slice_in_dim(router_row, start, feat)
    x_own = x_slice.astype(jnp.float32)
    grad_norm, score_grad = (
        lax.psum(norm_part.astype(jnp.bfloat16), "tensor").astype(jnp.float32),
        lax.psum(score_part.astype(jnp.bfloat16), "tensor").astype(jnp.float32),
    )
    scaled_grad = grad_norm * norm_gain
    row_dot = jnp.sum(x_float * scaled_grad, axis=1)
    own_grad = lax.dynamic_slice_in_dim(scaled_grad, start, feat, 1)
    logit_grad = score_grad * score * (1.0 - score)
    delta = (
        inv_rms * own_grad
        - x_own * inv_rms**3 * (row_dot / wide)[:, None]
        + logit_grad[:, None] * router_slice[None, :]
    )
    return (cot_slice.astype(jnp.float32) + row_mask[:, None] * delta).astype(jnp.bfloat16)


def route_tables(active, all_counts, column, quota):
    count_rows = active.shape[0]
    groups = lax.axis_size("dp")
    capacity = -(-count_rows // groups)
    my_index = lax.axis_index("dp")
    column_counts = all_counts[:, column]
    column_prefix = jnp.cumsum(column_counts) - column_counts
    group_ids = jnp.arange(groups, dtype=jnp.int32)
    start_mine = jnp.sum(jnp.where(group_ids == my_index, column_prefix, 0))
    total_mine = jnp.sum(jnp.where(group_ids == my_index, column_counts, 0))
    act_int = active.astype(jnp.int32)
    local_rank = jnp.cumsum(act_int) - act_int
    slot_ids = jnp.arange(groups * capacity, dtype=jnp.int32)
    peer_ids = slot_ids // capacity
    within = slot_ids % capacity
    send_pos = jnp.mod(peer_ids - start_mine, groups) + within * groups
    send_valid = send_pos < total_mine
    send_table = (
        send_valid[:, None] & active[None, :] & (local_rank[None, :] == send_pos[:, None])
    ).astype(jnp.bfloat16)
    peer_match = peer_ids[:, None] == group_ids[None, :]
    peer_prefix = jnp.sum(jnp.where(peer_match, column_prefix[None, :], 0), axis=1)
    peer_count = jnp.sum(jnp.where(peer_match, column_counts[None, :], 0), axis=1)
    recv_pos = jnp.mod(my_index - peer_prefix, groups) + within * groups
    recv_valid = recv_pos < peer_count
    recv_place = (peer_prefix + recv_pos - my_index) // groups
    places = jnp.arange(quota, dtype=jnp.int32)
    recv_table = (recv_valid[None, :] & (recv_place[None, :] == places[:, None])).astype(
        jnp.bfloat16
    )
    return (send_table, recv_table)


def spread_pass(
    x_home, cot_home, active, all_counts, column, quota, router_row, norm_gain, w_gate, w_up, w_down
):
    send_table, recv_table = route_tables(active, all_counts, column, quota)
    send_x = jnp.dot(send_table, x_home, preferred_element_type=jnp.float32).astype(jnp.bfloat16)
    send_cot = jnp.dot(send_table, cot_home, preferred_element_type=jnp.float32).astype(
        jnp.bfloat16
    )
    recv_x, recv_cot = (
        lax.all_to_all(send_x, "dp", split_axis=0, concat_axis=0, tiled=True),
        lax.all_to_all(send_cot, "dp", split_axis=0, concat_axis=0, tiled=True),
    )
    packed_x = jnp.dot(recv_table, recv_x, preferred_element_type=jnp.float32).astype(jnp.bfloat16)
    packed_cot = jnp.dot(recv_table, recv_cot, preferred_element_type=jnp.float32).astype(
        jnp.bfloat16
    )
    packed_grad = block_grad(
        packed_x,
        packed_cot,
        jnp.ones((quota,), jnp.float32),
        router_row,
        norm_gain,
        w_gate,
        w_up,
        w_down,
    )
    back_rows = contract_first(recv_table, packed_grad).astype(jnp.bfloat16)
    returned = lax.all_to_all(back_rows, "dp", split_axis=0, concat_axis=0, tiled=True)
    home_rows = contract_first(send_table, returned).astype(jnp.bfloat16)
    return jnp.where(active[:, None], home_rows, cot_home)


def body(hidden_first, hidden_second, cotangent, depths, norm_gain, router, w_gate, w_up, w_down):
    act_first = depths >= 1
    act_second = depths >= 2
    count_rows = hidden_first.shape[0]
    local_counts = jnp.stack(
        [jnp.sum(act_first.astype(jnp.int32)), jnp.sum(act_second.astype(jnp.int32))]
    )
    all_counts = lax.all_gather(local_counts[None, :], "dp", axis=0, tiled=True)
    grad_second = spread_pass(
        hidden_second,
        cotangent,
        act_second,
        all_counts,
        1,
        count_rows // 4,
        router[1],
        norm_gain,
        w_gate,
        w_up,
        w_down,
    )
    grad_first = spread_pass(
        hidden_first,
        grad_second,
        act_first,
        all_counts,
        0,
        count_rows // 2,
        router[0],
        norm_gain,
        w_gate,
        w_up,
        w_down,
    )
    return grad_first


def solution(mesh):
    in_specs = (
        P("dp", "tensor"),
        P("dp", "tensor"),
        P("dp", "tensor"),
        P("dp"),
        P(),
        P(),
        P(None, "tensor"),
        P(None, "tensor"),
        P("tensor", None),
    )
    out_specs = P("dp", "tensor")
    return jax.shard_map(body, mesh=mesh, in_specs=in_specs, out_specs=out_specs, check_vma=False)
```

profile of v0, /device:TPU:0, one launch (start us, length us, event | category | flops | bytes accessed | tf_op | source)
XLA Modules:
  0.0 217.5 jit_solution(5544220817420190145)
XLA Ops:
  9.9 1.4 convert_subtract_fusion.1
  11.3 1.5 add_dynamic-update-slice_fusion
  12.8 13.1 %all-reduce = s32[16]{0:T(128)S(1)} all-reduce(s32[16]{0:T(128)S(1)} %add_dynamic-update-slice_fusion), channel_id=2, replica_groups=mesh['dp'=8,'tensor'=4] {'dp'}, use_global_device_ids=true, to_apply=%add | all-reduce | flops 16 | bytes 128
  27.7 1.4 broadcast_compare_fusion
  29.9 3.4 %all-to-all-start.1 = ((bf16[8,16,512]{2,1,0:T(8,128)(2,1)}), bf16[8,16,512]{2,1,0:T(8,128)(2,1)S(1)}, u32[]{:S(2)}, u32[]{:S(2)}) async-start(bf16[8,16,512]{2,1,0:T(8,128)(2,1)} %bitcast.7), calls=%async_computation.1 | async-start | bytes 262144 | tf_op jit(solution)/shard_map/all_to_all | solution.py:104
  35.7 1.3 broadcast_compare_fusion.1
  37.1 1.8 convolution_convert_fusion.5
  38.9 1.8 convolution_convert_fusion.1
  40.7 5.9 %all-to-all-start = ((bf16[8,16,512]{2,1,0:T(8,128)(2,1)}), bf16[8,16,512]{2,1,0:T(8,128)(2,1)S(1)}, u32[]{:S(2)}, u32[]{:S(2)}) async-start(bf16[8,16,512]{2,1,0:T(8,128)(2,1)} %bitcast.5), calls=%async_computation | async-start | bytes 262144 | tf_op jit(solution)/shard_map/all_to_all | solution.py:105
  46.7 5.6 %all_gather.16 = bf16[32,2048]{1,0:T(8,128)(2,1)S(1)} all-gather(bf16[32,512]{1,0:T(8,128)(2,1)S(1)} %convolution_convert_fusion.10), channel_id=1, replica_groups=mesh['dp'=8,'tensor'=4] {'tensor'}, dimensions={1}, use_global_device_ids=true | all-gather | bytes 163840 | tf_op jit(solution)/shard_map/all_gather | solution.py:25
  52.4 3.1 %fusion.40 = f32[32,1024]{1,0:T(8,128)S(1)} fusion(bf16[2048,1024]{1,0:T(8,128)(2,1)} %param.15, bf16[32,2048]{1,0:T(8,128)(2,1)S(1)} %all_gather.16, f32[2048]{0:T(1024)} %param.13, f32[32]{0:T(128)S(1)} %get-tuple-element.41), kind=kOutput, calls=%fused_computation.75 | convolution fusion | flops 134479872 | bytes 4464768 | tf_op jit(solution)/shard_map/dot_general | solution.py:32
  56.4 6.0 %all-to-all-start.4 = ((bf16[8,16,512]{2,1,0:T(8,128)(2,1)}), bf16[8,16,512]{2,1,0:T(8,128)(2,1)S(1)}, u32[]{:S(2)}, u32[]{:S(2)}) async-start(bf16[8,16,512]{2,1,0:T(8,128)(2,1)} %bitcast.17), calls=%async_computation.4 | async-start | bytes 262144 | tf_op jit(solution)/shard_map/all_to_all | solution.py:104
  62.6 5.4 %all_gather.17 = bf16[32,2048]{1,0:T(8,128)(2,1)S(1)} all-gather(bf16[32,512]{1,0:T(8,128)(2,1)S(1)} %convolution_convert_fusion.11), channel_id=1, replica_groups=mesh['dp'=8,'tensor'=4] {'tensor'}, dimensions={1}, use_global_device_ids=true | all-gather | bytes 163840 | tf_op jit(solution)/shard_map/all_gather | solution.py:26
  68.0 3.6 %multiply_reduce_fusion.1 = (bf16[32]{0:T(256)(128)(2,1)S(1)}, f32[32,1024]{1,0:T(8,128)S(1)}) fusion(f32[32,1024]{1,0:T(8,128)S(1)} %fusion.42, f32[32,1024]{1,0:T(8,128)S(1)} %fusion.40, bf16[32,2048]{1,0:T(8,128)(2,1)S(1)} %all_gather.17, bf16[1024,2048]{1,0:T(8,128)(2,1)} %param.17), kind=kOutput, calls=%fused_computation.55 | convolution fusion | flops 134512608 | bytes 4718656 | tf_op jit(solution)/shard_map/dot_general | solution.py:16
  71.7 7.1 %psum.29 = bf16[32]{0:T(256)(128)(2,1)S(1)} all-reduce(bf16[32]{0:T(256)(128)(2,1)S(1)} %get-tuple-element.43), channel_id=1, replica_groups=mesh['dp'=8,'tensor'=4] {'tensor'}, use_global_device_ids=true, to_apply=%region_18.19 | all-reduce | flops 32 | bytes 128 | tf_op jit(solution)/shard_map/psum | solution.py:48
  79.0 3.7 %fusion.30 = f32[32,2048]{1,0:T(8,128)S(1)} fusion(bf16[2048,1024]{1,0:T(8,128)(2,1)} %param.15, f32[32,1024]{1,0:T(8,128)S(1)} %fusion.40, f32[32,1024]{1,0:T(8,128)S(1)} %fusion.42, f32[32,1024]{1,0:T(8,128)S(1)} %get-tuple-element.44, f32[32]{0:T(128)S(1)} %get-tuple-element.46), kind=kOutput, calls=%fused_computation.63 | convolution fusion | flops 134578176 | bytes 4849792 | tf_op jit(solution)/shard_map/dot_general | solution.py:16
  82.8 2.0 fusion.1
  85.0 5.8 %all_gather.18 = bf16[64,2048]{1,0:T(8,128)(2,1)S(1)} all-gather(bf16[64,512]{1,0:T(8,128)(2,1)S(1)} %convolution_convert_fusion.8), channel_id=1, replica_groups=mesh['dp'=8,'tensor'=4] {'tensor'}, dimensions={1}, use_global_device_ids=true | all-gather | bytes 327680 | tf_op jit(solution)/shard_map/all_gather | solution.py:25
  90.9 25.9 %all-reduce.4.cloned.1.call-done = bf16[32,2048]{1,0:T(8,128)(2,1)} async-done(((bf16[32,2048]{1,0:T(8,128)(2,1)}), bf16[32,2048]{1,0:T(8,128)(2,1)}) %all-reduce.4.cloned.1.call-update) | async-done | bytes 131088 | tf_op jit(solution)/shard_map/psum | solution.py:47
  118.8 5.5 %all-to-all-start.2 = ((bf16[8,16,512]{2,1,0:T(8,128)(2,1)}), bf16[8,16,512]{2,1,0:T(8,128)(2,1)S(1)}, u32[]{:S(2)}, u32[]{:S(2)}) async-start(bf16[8,16,512]{2,1,0:T(8,128)(2,1)} %bitcast.13), calls=%async_computation.2 | async-start | bytes 262144 | tf_op jit(solution)/shard_map/all_to_all | solution.py:122
  124.3 3.1 %fusion.26 = f32[64,1024]{1,0:T(8,128)S(1)} fusion(bf16[2048,1024]{1,0:T(8,128)(2,1)} %param.15, bf16[64,2048]{1,0:T(8,128)(2,1)S(1)} %all_gather.18, f32[2048]{0:T(1024)S(1)} %copy-done.5, f32[64]{0:T(128)S(1)} %get-tuple-element.30), kind=kOutput, calls=%fused_computation.61 | convolution fusion | flops 268959744 | bytes 4727040 | tf_op jit(solution)/shard_map/dot_general | solution.py:32
  127.4 4.3 %all-to-all-done.2 = bf16[8,16,512]{2,1,0:T(8,128)(2,1)S(1)} async-done(((bf16[8,16,512]{2,1,0:T(8,128)(2,1)}), bf16[8,16,512]{2,1,0:T(8,128)(2,1)S(1)}, u32[]{:S(2)}, u32[]{:S(2)}) %all-to-all-start.2) | async-done | bytes 131104 | tf_op jit(solution)/shard_map/all_to_all | solution.py:122
  132.9 3.4 %all-to-all-start.3 = ((bf16[8,16,512]{2,1,0:T(8,128)(2,1)}), bf16[8,16,512]{2,1,0:T(8,128)(2,1)S(1)}, u32[]{:S(2)}, u32[]{:S(2)}) async-start(bf16[8,16,512]{2,1,0:T(8,128)(2,1)} %bitcast.15), calls=%async_computation.3 | async-start | bytes 262144 | tf_op jit(solution)/shard_map/all_to_all | solution.py:105
  136.3 3.1 %fusion.28 = f32[64,1024]{1,0:T(8,128)S(1)} fusion(bf16[2048,1024]{1,0:T(8,128)(2,1)} %param.16, bf16[64,2048]{1,0:T(8,128)(2,1)S(1)} %all_gather.18, f32[2048]{0:T(1024)S(1)} %copy-done.5, f32[64]{0:T(128)S(1)} %get-tuple-element.30), kind=kOutput, calls=%fused_computation.62 | convolution fusion | flops 268959744 | bytes 4727040 | tf_op jit(solution)/shard_map/dot_general | solution.py:33
  139.4 4.1 %all-to-all-done.3 = bf16[8,16,512]{2,1,0:T(8,128)(2,1)S(1)} async-done(((bf16[8,16,512]{2,1,0:T(8,128)(2,1)}), bf16[8,16,512]{2,1,0:T(8,128)(2,1)S(1)}, u32[]{:S(2)}, u32[]{:S(2)}) %all-to-all-start.3) | async-done | bytes 131104 | tf_op jit(solution)/shard_map/all_to_all | solution.py:105
  143.7 5.8 %all_gather.19 = bf16[64,2048]{1,0:T(8,128)(2,1)S(1)} all-gather(bf16[64,512]{1,0:T(8,128)(2,1)S(1)} %convolution_convert_fusion.9), channel_id=1, replica_groups=mesh['dp'=8,'tensor'=4] {'tensor'}, dimensions={1}, use_global_device_ids=true | all-gather | bytes 327680 | tf_op jit(solution)/shard_map/all_gather | solution.py:26
  149.5 3.7 %multiply_reduce_fusion = (bf16[64]{0:T(256)(128)(2,1)S(1)}, f32[64,1024]{1,0:T(8,128)S(1)}) fusion(f32[64,1024]{1,0:T(8,128)S(1)} %fusion.28, f32[64,1024]{1,0:T(8,128)S(1)} %fusion.26, bf16[64,2048]{1,0:T(8,128)(2,1)S(1)} %all_gather.19, bf16[1024,2048]{1,0:T(8,128)(2,1)} %param.17), kind=kOutput, calls=%fused_computation.43 | convolution fusion | flops 269025216 | bytes 5243008 | tf_op jit(solution)/shard_map/dot_general | solution.py:16
  153.2 6.3 %psum.31 = bf16[64]{0:T(256)(128)(2,1)S(1)} all-reduce(bf16[64]{0:T(256)(128)(2,1)S(1)} %get-tuple-element.47), channel_id=1, replica_groups=mesh['dp'=8,'tensor'=4] {'tensor'}, use_global_device_ids=true, to_apply=%region_23.24 | all-reduce | flops 64 | bytes 256 | tf_op jit(solution)/shard_map/psum | solution.py:48
  159.8 3.8 %fusion.21 = f32[64,2048]{1,0:T(8,128)S(1)} fusion(bf16[2048,1024]{1,0:T(8,128)(2,1)} %param.15, f32[64,1024]{1,0:T(8,128)S(1)} %fusion.26, f32[64,1024]{1,0:T(8,128)S(1)} %fusion.28, f32[64,1024]{1,0:T(8,128)S(1)} %get-tuple-element.48, f32[64]{0:T(128)S(1)} %get-tuple-element.50), kind=kOutput, calls=%fused_computation.50 | convolution fusion | flops 269156352 | bytes 5505280 | tf_op jit(solution)/shard_map/dot_general | solution.py:16
  163.6 2.1 fusion
  165.8 29.9 %all-reduce.6.cloned.1.call-done = bf16[64,2048]{1,0:T(8,128)(2,1)} async-done(((bf16[64,2048]{1,0:T(8,128)(2,1)}), bf16[64,2048]{1,0:T(8,128)(2,1)}) %all-reduce.6.cloned.1.call-update) | async-done | bytes 262160 | tf_op jit(solution)/shard_map/psum | solution.py:47
  197.1 12.7 %all_to_all.72 = bf16[8,16,512]{2,1,0:T(8,128)(2,1)S(1)} all-to-all(bf16[8,16,512]{2,1,0:T(8,128)(2,1)S(1)} %bitcast.83), channel_id=1, replica_groups=mesh['dp'=8,'tensor'=4] {'dp'}, dimensions={0} | all-to-all | bytes 262144 | tf_op jit(solution)/shard_map/all_to_all | solution.py:122
  (69 shorter events, 15.8 us)
Async XLA Ops:
  6.5 22.5 %copy-start = (bf16[128,512]{1,0:T(8,128)(2,1)S(1)}, bf16[128,512]{1,0:T(8,128)(2,1)}, u32[]{:S(2)}) copy-start(bf16[128,512]{1,0:T(8,128)(2,1)} %param.10) | copy-start | bytes 393220
  6.5 49.0 %copy-start.5 = (f32[2048]{0:T(1024)S(1)}, f32[2048]{0:T(1024)}, u32[]{:S(2)}) copy-start(f32[2048]{0:T(1024)} %param.13) | copy-start | bytes 24580
  29.9 10.8 %all-to-all-start.1 = ((bf16[8,16,512]{2,1,0:T(8,128)(2,1)}), bf16[8,16,512]{2,1,0:T(8,128)(2,1)S(1)}, u32[]{:S(2)}, u32[]{:S(2)}) async-start(bf16[8,16,512]{2,1,0:T(8,128)(2,1)} %bitcast.7), calls=%async_computation.1 | async-start | bytes 262144 | tf_op jit(solution)/shard_map/all_to_all | solution.py:104
  40.7 15.8 %all-to-all-start = ((bf16[8,16,512]{2,1,0:T(8,128)(2,1)}), bf16[8,16,512]{2,1,0:T(8,128)(2,1)S(1)}, u32[]{:S(2)}, u32[]{:S(2)}) async-start(bf16[8,16,512]{2,1,0:T(8,128)(2,1)} %bitcast.5), calls=%async_computation | async-start | bytes 262144 | tf_op jit(solution)/shard_map/all_to_all | solution.py:105
  46.6 8.9 %copy-start.1 = (bf16[2048,1024]{1,0:T(8,128)(2,1)S(1)}, bf16[2048,1024]{1,0:T(8,128)(2,1)}, u32[]{:S(2)}) copy-start(bf16[2048,1024]{1,0:T(8,128)(2,1)} %param.16) | copy-start | bytes 12582916
  55.6 23.3 %copy-start.6 = (f32[2,2048]{1,0:T(2,128)S(1)}, f32[2,2048]{1,0:T(2,128)}, u32[]{:S(2)}) copy-start(f32[2,2048]{1,0:T(2,128)} %param.14) | copy-start | bytes 49156
  56.4 28.4 %all-to-all-start.4 = ((bf16[8,16,512]{2,1,0:T(8,128)(2,1)}), bf16[8,16,512]{2,1,0:T(8,128)(2,1)S(1)}, u32[]{:S(2)}, u32[]{:S(2)}) async-start(bf16[8,16,512]{2,1,0:T(8,128)(2,1)} %bitcast.17), calls=%async_computation.4 | async-start | bytes 262144 | tf_op jit(solution)/shard_map/all_to_all | solution.py:104
  62.4 54.4 %all-reduce.4.cloned.1.call-start = ((), (), s32[]{:S(2)}) async-start(), calls=%async_computation.6 | async-start | bytes 262144 | tf_op jit(solution)/shard_map/psum | solution.py:47
  78.8 3.9 %copy-start.2 = (bf16[2048,1024]{1,0:T(8,128)(2,1)S(1)}, bf16[2048,1024]{1,0:T(8,128)(2,1)}, u32[]{:S(2)}) copy-start(bf16[2048,1024]{1,0:T(8,128)(2,1)} %param.16) | copy-start | bytes 12582916
  84.8 46.9 %copy-start.4 = (bf16[128,512]{1,0:T(8,128)(2,1)S(1)}, bf16[128,512]{1,0:T(8,128)(2,1)}, u32[]{:S(2)}) copy-start(bf16[128,512]{1,0:T(8,128)(2,1)} %param.11) | copy-start | bytes 393220
  118.8 12.9 %all-to-all-start.2 = ((bf16[8,16,512]{2,1,0:T(8,128)(2,1)}), bf16[8,16,512]{2,1,0:T(8,128)(2,1)S(1)}, u32[]{:S(2)}, u32[]{:S(2)}) async-start(bf16[8,16,512]{2,1,0:T(8,128)(2,1)} %bitcast.13), calls=%async_computation.2 | async-start | bytes 262144 | tf_op jit(solution)/shard_map/all_to_all | solution.py:122
  132.9 10.7 %all-to-all-start.3 = ((bf16[8,16,512]{2,1,0:T(8,128)(2,1)}), bf16[8,16,512]{2,1,0:T(8,128)(2,1)S(1)}, u32[]{:S(2)}, u32[]{:S(2)}) async-start(bf16[8,16,512]{2,1,0:T(8,128)(2,1)} %bitcast.15), calls=%async_computation.3 | async-start | bytes 262144 | tf_op jit(solution)/shard_map/all_to_all | solution.py:105
  136.2 59.4 %all-reduce.6.cloned.1.call-start = ((), (), s32[]{:S(2)}) async-start(), calls=%async_computation.7 | async-start | bytes 524288 | tf_op jit(solution)/shard_map/psum | solution.py:47
  159.4 4.1 %copy-start.3 = (bf16[2048,1024]{1,0:T(8,128)(2,1)S(1)}, bf16[2048,1024]{1,0:T(8,128)(2,1)}, u32[]{:S(2)}) copy-start(bf16[2048,1024]{1,0:T(8,128)(2,1)} %param.16) | copy-start | bytes 12582916
Sparse Core Ops, SparseCore 0:
  84.9 31.8 all-reduce.3
  165.9 29.7 all-reduce.5
where the time goes:
time: 219 us; the launch traced here: 218 us
  waiting for transfers between devices  64.2 us (29%)
  blocking collectives  61.7 us (28%)
  matrix products  38 us (17%)
  starting transfers between devices  24.3 us (11%)
  between operations  14.3 us (7%)
  other arithmetic  12.5 us (6%)
  local copies, waits for them, and re-layouts  2.58 us (1%)
    psum x2, waiting for transfers between devices, block_grad(): lax.psum(norm_part.astype(jnp.bfloat16), 'tensor').astype(jnp.float32)  55.8 us
    dot_general x6, matrix products, contract_last(): lax.dot_general(left, right, (((1,), (1,)), ((), ())), preferred_element_...  19.1 us
    psum x2, blocking collectives, block_grad(): lax.psum(score_part.astype(jnp.bfloat16), 'tensor').astype(jnp.float32)  13.4 us
    unnamed x1, blocking collectives  13.1 us
    all_to_all x1, blocking collectives, spread_pass(): lax.all_to_all(back_rows, 'dp', split_axis=0, concat_axis=0, tiled=True)  12.7 us
    all_gather x2, blocking collectives, block_grad(): lax.all_gather(x_slice, 'tensor', axis=1, tiled=True)  11.3 us
    all_gather x2, blocking collectives, block_grad(): lax.all_gather(cot_slice, 'tensor', axis=1, tiled=True)  11.2 us
    all_to_all x2, starting transfers between devices, spread_pass(): lax.all_to_all(send_x, 'dp', split_axis=0, concat_axis=0, tiled=True)  9.38 us
  transfers between devices with their start and end apart: 7, of which 4 were waited for; matrix products, arithmetic and copies ran while one was open for 13% of the time, Pallas kernels for 0%

commit v1 on v0

v1 whole, which is shorter than its diff:
```python
import functools

import jax
import jax.numpy as jnp
from jax import lax
from jax.experimental import pallas as pl
from jax.experimental.pallas import tpu as pltpu
from jax.sharding import PartitionSpec as P

epsilon = 1e-06
LANES = 128
EXTRA = 16
VM = pltpu.VMEM
F32 = jnp.float32
BF16 = jnp.bfloat16


def hop(value, bit):
    size = lax.axis_size("tensor")
    return lax.ppermute(value, "tensor", [(j, j ^ bit) for j in range(size)])


def after(value, *others):
    return lax.optimization_barrier((value,) + others)[0]


def spread(own, low_bits):
    parts = {0: own}
    for bit in reversed(low_bits):
        for key in list(parts):
            parts[key ^ bit] = hop(parts[key], bit)
    return [parts[key] for key in range(len(parts))]


def scatter(blocks, low_bits):
    blocks = dict(enumerate(blocks))
    for bit in low_bits:
        kept = {}
        for r in sorted(blocks):
            if r & bit == 0:
                kept[r] = blocks[r].astype(F32) + hop(blocks[r ^ bit].astype(BF16), bit).astype(F32)
        blocks = kept
    return blocks[0]


def kernel_call(kernel, outs, *args, flops=0):
    many = isinstance(outs, (list, tuple))
    shapes = outs if many else [outs]
    moved = sum(a.size * a.dtype.itemsize for a in args)
    spec = pl.BlockSpec(memory_space=VM)
    return pl.pallas_call(
        kernel,
        out_shape=list(outs) if many else outs,
        in_specs=[spec] * len(args),
        out_specs=[spec] * len(shapes) if many else spec,
        compiler_params=pltpu.CompilerParams(vmem_limit_bytes=16 * 2**20),
        cost_estimate=pl.CostEstimate(flops=flops, bytes_accessed=moved, transcendentals=0),
    )(*args)


def place(top):
    index = lax.axis_index("tensor")
    return index // top, index % top


def span(block, feat):
    return pl.ds(pl.multiple_of(block * feat, feat), feat)


def turned(value):
    value = value.astype(F32)
    return jnp.concatenate(
        [value[:, k : k + LANES].T for k in range(0, value.shape[1], LANES)], axis=0
    )


def column(row, tokens):
    return turned(jnp.broadcast_to(row, (tokens, row.shape[1])))


def mat(left, right):
    return jnp.dot(left, right, preferred_element_type=F32)


def turn_kernel(value_ref, out_ref):
    out_ref[...] = turned(value_ref[...]).astype(out_ref.dtype)


def norm_kernel(top, which, halves, router_row, first, last, *refs):
    refs = list(refs)
    parts = [refs.pop(0) for _ in halves for _ in range(top)]
    gain_ref, router_ref, gate_w, up_w = [refs.pop(0) for _ in range(4)]
    held = [] if first else [refs.pop(0) for _ in range(3)]
    outs = refs
    side, inner = place(top)
    feat = parts[0].shape[1]
    wide = feat * top * 2
    gate = up = None
    squares = jnp.zeros((parts[0].shape[0], LANES), F32)
    logits = jnp.zeros((parts[0].shape[0], LANES), F32)
    if not first:
        gate, up = held[0][...], held[1][...]
        squares, logits = held[2][0], held[2][1]
    for number, part in enumerate(parts):
        half = halves[number // top]
        block = (side if half == 0 else 1 - side) * top + (inner ^ (number % top))
        at = span(block, feat)
        x = part[...].astype(F32)
        gained = (x * gain_ref[:, at]).astype(BF16)
        routed = x * router_ref[router_row : router_row + 1, at]
        for k in range(0, feat, LANES):
            squares += x[:, k : k + LANES] * x[:, k : k + LANES]
            logits += routed[:, k : k + LANES]
        gate_now, up_now = mat(gained, gate_w[at, :]), mat(gained, up_w[at, :])
        gate = gate_now if gate is None else gate + gate_now
        up = up_now if up is None else up + up_now
    if not last:
        outs[0][...], outs[1][...] = gate, up
        outs[2][0], outs[2][1] = squares, logits
        return
    inv_rms = lax.rsqrt(jnp.sum(squares.T, axis=0, keepdims=True) / wide + epsilon)
    score = jax.nn.sigmoid(jnp.sum(logits.T, axis=0, keepdims=True))
    rows = outs[4]
    rows[...] = jnp.concatenate(
        [inv_rms, score, jnp.zeros((6, inv_rms.shape[1]), F32)], axis=0
    )
    for k in range(0, gate.shape[1], LANES):
        g = gate[:, k : k + LANES].T * inv_rms
        u = up[:, k : k + LANES].T * inv_rms
        sigma = jax.nn.sigmoid(g)
        silu = g * sigma
        grad = u * sigma * (1.0 + g * (1.0 - sigma))
        act = silu * u
        here = slice(k, k + LANES)
        outs[0][here, :] = score * grad
        outs[1][here, :] = score * silu
        outs[2][here, :] = act
        outs[3][here, :] = score * (grad * g + act)


def back_part_kernel(top, half, *refs):
    parts, (down_w, out_ref) = refs[:top], refs[top:]
    side, inner = place(top)
    feat = parts[0].shape[0]
    start = (side if half == "mine" else 1 - side if half == "theirs" else half) * top
    total = None
    for r, part in enumerate(parts):
        now = mat(down_w[:, span(start + (inner ^ r), feat)], part[...])
        total = now if total is None else total + now
    out_ref[...] = total


def write_terms(top, half, feat, gg, gu, sums, gate_w, up_w, outs):
    side, inner = place(top)
    start = (side if half == "mine" else 1 - side if half == "theirs" else half) * top
    for r, out_ref in enumerate(outs):
        at = span(start + (inner ^ r), feat)
        term = mat(gate_w[at, :], gg) + mat(up_w[at, :], gu)
        out_ref[0:feat, :] = term.astype(out_ref.dtype)
        out_ref[feat : feat + EXTRA, :] = sums.astype(out_ref.dtype)


def back_kernel(top, half, out_half, feat, *refs):
    parts = refs[:top]
    held, grad_p, silu_p, act_p, dot_p, down_w, gate_w, up_w, gg_ref, gu_ref, sums_ref = refs[
        top : top + 11
    ]
    outs = refs[top + 11 :]
    side, inner = place(top)
    start = (side if half == "mine" else 1 - side if half == "theirs" else half) * top
    back = held[...]
    for r, part in enumerate(parts):
        back = back + mat(down_w[:, span(start + (inner ^ r), feat)], part[...])
    gg = (back * grad_p[...]).astype(BF16)
    gu = (back * silu_p[...]).astype(BF16)
    score_part = jnp.sum(back * act_p[...], axis=0, keepdims=True)
    dot_part = jnp.sum(back * dot_p[...], axis=0, keepdims=True)
    sums = jnp.concatenate(
        [score_part, dot_part, jnp.zeros((EXTRA - 2, LANES), F32)], axis=0
    )
    gg_ref[...] = gg
    gu_ref[...] = gu
    sums_ref[...] = sums
    write_terms(top, out_half, feat, gg, gu, sums, gate_w, up_w, outs)


def term_kernel(top, half, feat, gg_ref, gu_ref, sums_ref, gate_w, up_w, *outs):
    write_terms(top, half, feat, gg_ref[...], gu_ref[...], sums_ref[...], gate_w, up_w, outs)


def row_factors(sums, rows, wide):
    inv_rms, score = rows[0:1, :], rows[1:2, :]
    return inv_rms, inv_rms * inv_rms * (sums[1:2, :] / wide), sums[0:1, :] * score * (1.0 - score)


def second_kernel(top, half, chip, got, cot_own, cot_cross, x_own, x_cross, gain_ref, router_ref, depths_ref, rows_ref, out_ref):
    side, inner = place(top)
    feat = out_ref.shape[0]
    tokens = x_own.shape[0]
    total = chip[...] + got[...].astype(F32)
    inv_rms, coef, logit = row_factors(total[feat : feat + 2, :], rows_ref[...], feat * top * 2)
    active = (depths_ref[...] >= 2).astype(F32)
    at = span(half * top + inner, feat)
    mine = side == half
    x = turned(jnp.where(mine, x_own[...].astype(F32), x_cross[...].astype(F32)))
    cot = jnp.where(mine, cot_own[...].astype(F32), cot_cross[...].astype(F32))
    gain = column(gain_ref[:, at], tokens)
    router = column(router_ref[1:2, at], tokens)
    delta = (active * inv_rms) * (gain * total[0:feat, :]) - x * (active * coef) + router * (active * logit)
    out_ref[...] = (cot + delta).astype(out_ref.dtype)


def last_kernel(top, own_sum, chip_theirs, got, second_a, second_b, x_own, gain_ref, router_ref, depths_ref, rows_ref, out_ref):
    side, inner = place(top)
    tokens, feat = out_ref.shape
    cross = got[...].astype(F32)
    total = own_sum[0:feat, :] + cross[0:feat, :]
    sums = chip_theirs[feat : feat + 2, :] + cross[feat : feat + 2, :]
    inv_rms, coef, logit = row_factors(sums, rows_ref[...], feat * top * 2)
    active = (depths_ref[...] >= 1).astype(F32)
    at = span(side * top + inner, feat)
    x = turned(x_own[...])
    gain = column(gain_ref[:, at], tokens)
    router = column(router_ref[0:1, at], tokens)
    second = jnp.where(side == 0, second_a[...].astype(F32), second_b[...].astype(F32))
    delta = (active * inv_rms) * (gain * total) - x * (active * coef) + router * (active * logit)
    result = second + delta
    for k in range(0, feat, LANES):
        out_ref[:, k : k + LANES] = result[k : k + LANES, :].T.astype(out_ref.dtype)


def body(hidden_first, hidden_second, cotangent, depths, norm_gain, router, w_gate, w_up, w_down):
    size = lax.axis_size("tensor")
    bits = []
    while 2 ** len(bits) < size:
        bits.append(2 ** len(bits))
    top, low = bits[-1], bits[:-1]
    tokens, feat = hidden_first.shape
    units = w_gate.shape[1]
    depths = depths.reshape(1, tokens)
    gain = norm_gain.reshape(1, -1)
    product = 2 * tokens * feat * top * units
    wide_units = VM((units, LANES), F32)
    factor_outs = [wide_units] * 4 + [VM((8, LANES), F32)]
    partial_outs = [VM((tokens, units), F32)] * 2 + [VM((2, tokens, LANES), F32)]
    block_outs = [VM((feat + EXTRA, LANES), BF16 if r & 1 else F32) for r in range(top)]
    grad_outs = [VM((units, LANES), BF16)] * 2 + [VM((EXTRA, LANES), F32)]

    x2_cross = hop(hidden_second, top)
    x2_mine = spread(hidden_second, low)
    cot_own = kernel_call(turn_kernel, VM((feat, tokens), BF16), cotangent)
    cot_cross = hop(cot_own, top)
    cot_mine = spread(cot_own, low)
    x2_theirs = spread(x2_cross, low)
    norm_weights = (gain, router, w_gate, w_up)
    partial = kernel_call(
        functools.partial(norm_kernel, top, "a", (0,), 1, True, False),
        partial_outs, *x2_mine, *norm_weights, flops=2 * product,
    )
    back_mine = kernel_call(
        functools.partial(back_part_kernel, top, "mine"),
        wide_units, *cot_mine, w_down, flops=product,
    )
    factors2 = kernel_call(
        functools.partial(norm_kernel, top, "b", (1,), 1, False, True),
        factor_outs, *x2_theirs, *norm_weights, *partial, flops=2 * product,
    )
    cot_theirs = spread(cot_cross, low)

    gg, gu, sums, *blocks = kernel_call(
        functools.partial(back_kernel, top, "theirs", 0, feat),
        grad_outs + block_outs,
        *cot_theirs, back_mine, *factors2[:4], w_down, w_gate, w_up, flops=3 * product,
    )
    chip_a = scatter(blocks, low)
    blocks = kernel_call(
        functools.partial(term_kernel, top, 1, feat),
        block_outs, gg, gu, sums, w_gate, w_up, flops=2 * product,
    )
    got_a = hop(chip_a.astype(BF16), top)
    chip_b = scatter(blocks, low)
    got_b = hop(chip_b.astype(BF16), top)

    x1_cross = hop(after(hidden_first, cot_cross), top)
    x1_parts = spread(hidden_first, low) + spread(x1_cross, low)
    x1_parts = list(lax.optimization_barrier((tuple(x1_parts), chip_b))[0])
    factors1 = kernel_call(
        functools.partial(norm_kernel, top, "c", (0, 1), 0, True, True),
        factor_outs, *x1_parts, *norm_weights, flops=4 * product,
    )

    seconds = []
    for half, chip, got in ((0, chip_a, got_a), (1, chip_b, got_b)):
        seconds.append(
            kernel_call(
                functools.partial(second_kernel, top, half),
                VM((feat, tokens), BF16),
                chip, got, cot_own, cot_cross, hidden_second, x2_cross, gain, router, depths,
                factors2[4],
            )
        )
    second_a, second_b = (spread(value, low) for value in seconds)
    back_a = kernel_call(
        functools.partial(back_part_kernel, top, 0), wide_units, *second_a, w_down, flops=product
    )
    gg, gu, sums, *blocks = kernel_call(
        functools.partial(back_kernel, top, 1, "theirs", feat),
        grad_outs + block_outs,
        *second_b, back_a, *factors1[:4], w_down, w_gate, w_up, flops=3 * product,
    )
    chip_theirs = scatter(blocks, low)
    got = hop(chip_theirs.astype(BF16), top)
    blocks = kernel_call(
        functools.partial(term_kernel, top, "mine", feat),
        block_outs, gg, gu, sums, w_gate, w_up, flops=2 * product,
    )
    own_sum = scatter(blocks, low)
    return kernel_call(
        functools.partial(last_kernel, top),
        jax.ShapeDtypeStruct((tokens, feat), BF16),
        own_sum, chip_theirs, got, seconds[0], seconds[1], hidden_first, gain, router, depths,
        factors1[4],
    )


def solution(mesh):
    in_specs = (
        P("dp", "tensor"),
        P("dp", "tensor"),
        P("dp", "tensor"),
        P("dp"),
        P(),
        P(),
        P(None, "tensor"),
        P(None, "tensor"),
        P("tensor", None),
    )
    out_specs = P("dp", "tensor")
    return jax.shard_map(body, mesh=mesh, in_specs=in_specs, out_specs=out_specs, check_vma=False)
```

time: 219 us -> 47.5 us (0.22)
  blocking collectives: 61.7 us -> 0 us
  waiting for transfers between devices: 64.2 us -> 16.7 us
  matrix products: 38 us -> 0 us
  starting transfers between devices: 24.3 us -> 9.47 us
  between operations: 14.3 us -> 0.21 us
  Pallas kernels: 0 us -> 12.8 us
  other arithmetic: 12.5 us -> 0.16 us
  local copies, waits for them, and re-layouts: 2.58 us -> 7.87 us
    psum x2 -> x0, waiting for transfers between devices: 55.8 us -> none  [block_grad(): lax.psum(norm_part.astype(jnp.bfloat16), 'tensor').astype(jnp.float32)]
    dot_general x24 -> x0, matrix products: 38 us -> none  [the longest x6 19.1 us: contract_last(): lax.dot_general(left, right, (((1,), (1,)), ((), ())), preferred_element_...]
    all_to_all x5 -> x0, starting transfers between devices: 24.2 us -> none  [the longest x2 9.38 us: spread_pass(): lax.all_to_all(send_x, 'dp', split_axis=0, concat_axis=0, tiled=True)]
    all_gather x4 -> x0, blocking collectives: 22.5 us -> none  [the longest x2 11.3 us: block_grad(): lax.all_gather(x_slice, 'tensor', axis=1, tiled=True)]
    ppermute x0 -> x18, waiting for transfers between devices: none -> 16.7 us  [hop(): return lax.ppermute(value, 'tensor', [(j, j ^ bit) for j in range(size)])]
    psum x2 -> x0, blocking collectives: 13.4 us -> none  [block_grad(): lax.psum(score_part.astype(jnp.bfloat16), 'tensor').astype(jnp.float32)]
    unnamed x1 -> x0, blocking collectives: 13.1 us -> none
    pallas_call x0 -> x13, Pallas kernels: none -> 12.8 us  [kernel_call(): pl.pallas_call(kernel, out_shape=list(outs) if many else outs, in_specs=[...]
  transfers between devices with their start and end apart: 7 -> 18, of which waited for: 4 -> 8; matrix products, arithmetic and copies ran while one was open for 13% -> 0% of each run, Pallas kernels for 0% -> 17%
where the time goes in v1:
time: 47.5 us; the launch traced here: 47.2 us
  waiting for transfers between devices  16.7 us (35%)
  Pallas kernels  12.8 us (27%)
  starting transfers between devices  9.47 us (20%)
  local copies, waits for them, and re-layouts  7.87 us (17%)
    ppermute x18, waiting for transfers between devices, hop(): return lax.ppermute(value, 'tensor', [(j, j ^ bit) for j in range(size)])  16.7 us
    pallas_call x13, Pallas kernels, kernel_call(): pl.pallas_call(kernel, out_shape=list(outs) if many else outs, in_specs=[...  12.8 us
    ppermute x18, starting transfers between devices, hop(): return lax.ppermute(value, 'tensor', [(j, j ^ bit) for j in range(size)])  9.47 us
    unnamed x22, local copies, waits for them, and re-layouts  7.87 us
  transfers between devices with their start and end apart: 18, of which 8 were waited for; matrix products, arithmetic and copies ran while one was open for 0% of the time, Pallas kernels for 17%

profile of v1, /device:TPU:0, one launch (start us, length us, event | category | flops | bytes accessed | tf_op | source)
XLA Modules:
  0.0 47.2 jit_solution(1369502285490156161)
XLA Ops:
  0.0 3.0 %collective-permute-start.3 = (bf16[128,512]{1,0:T(8,128)(2,1)}, bf16[128,512]{1,0:T(8,128)(2,1)S(1)}, u32[]{:S(2)}, u32[]{:S(2)}) collective-permute-start(bf16[128,512]{1,0:T(8,128)(2,1)} %x_own.4), channel_id=1, source_target_pairs={{0,2},{1,3},{2,0},{3,1},{4,6},{5,7},{6,4},{7,5},{8,10},{9,11},{10,... | collective-permute-start | bytes 393224 | tf_op jit(solution)/shard_map/ppermute | solution.py:20
  3.0 0.9 %copy-done.9 = bf16[128,512]{1,0:T(8,128)(2,1)S(1)} copy-done((bf16[128,512]{1,0:T(8,128)(2,1)S(1)}, bf16[128,512]{1,0:T(8,128)(2,1)}, u32[]{:S(2)}) %copy-start.9) | copy-done | bytes 131096
  4.2 0.5 %collective-permute-start.5 = (bf16[128,512]{1,0:T(8,128)(2,1)}, bf16[128,512]{1,0:T(8,128)(2,1)S(1)}, u32[]{:S(2)}, u32[]{:S(2)}) collective-permute-start(bf16[128,512]{1,0:T(8,128)(2,1)} %x_own.4), channel_id=1, source_target_pairs={{0,1},{1,0},{2,3},{3,2},{4,5},{5,4},{6,7},{7,6},{8,9},{9,8},{10,11... | collective-permute-start | bytes 393224 | tf_op jit(solution)/shard_map/ppermute | solution.py:20
  4.7 2.5 %collective-permute-done.3.refs_0_.x_cross = bf16[128,512]{1,0:T(8,128)(2,1)S(1)} collective-permute-done((bf16[128,512]{1,0:T(8,128)(2,1)}, bf16[128,512]{1,0:T(8,128)(2,1)S(1)}, u32[]{:S(2)}, u32[]{:S(2)}) %collective-permute-start.3) | collective-permute-done | bytes 131104 | tf_op jit(solution)/shard_map/ppermute | solution.py:20
  7.2 2.3 %collective-permute-done.refs_0_.cot_cross = bf16[512,128]{1,0:T(8,128)(2,1)S(1)} collective-permute-done((bf16[512,128]{1,0:T(8,128)(2,1)S(1)}, bf16[512,128]{1,0:T(8,128)(2,1)S(1)}, u32[]{:S(2)}, u32[]{:S(2)}) %collective-permute-start) | collective-permute-done | bytes 131104 | tf_op jit(solution)/shard_map/ppermute | solution.py:20
  9.5 2.2 %copy-done.3 = bf16[1024,2048]{1,0:T(8,128)(2,1)S(1)} copy-done((bf16[1024,2048]{1,0:T(8,128)(2,1)S(1)}, bf16[1024,2048]{1,0:T(8,128)(2,1)}, u32[]{:S(2)}) %copy-start.3) | copy-done | bytes 4194328
  11.7 0.7 %shard_map.92.refs_2_ = f32[1024,128]{1,0:T(8,128)S(1)} custom-call(bf16[512,128]{1,0:T(8,128)(2,1)S(1)} %shard_map.91.refs_0_.cot_own, bf16[512,128]{1,0:T(8,128)(2,1)S(1)} %collective-permute-done.2.refs_1_, bf16[1024,2048]{1,0:T(8,128)(2,1)S(1)} %copy-done.3), custom_call_target="tpu_custom_call" | custom-call | flops 268435456 | bytes 4456448 | tf_op jit(solution)/shard_map/pallas_call | solution.py:51
  12.6 2.2 %copy-done.1 = bf16[2048,1024]{1,0:T(8,128)(2,1)S(1)} copy-done((bf16[2048,1024]{1,0:T(8,128)(2,1)S(1)}, bf16[2048,1024]{1,0:T(8,128)(2,1)}, u32[]{:S(2)}) %copy-start.1) | copy-done | bytes 4194328
  14.8 0.8 %shard_map.93 = (f32[128,1024]{1,0:T(8,128)S(1)}, f32[128,1024]{1,0:T(8,128)S(1)}, f32[2,128,128]{2,1,0:T(8,128)S(1)}) custom-call(bf16[128,512]{1,0:T(8,128)(2,1)S(1)} %copy-done.5, bf16[128,512]{1,0:T(8,128)(2,1)S(1)} %collective-permute-done.5.refs_1_, f32[1,2048]{1,0:T(1,128)S(1)} %bitcast.2, f32[2,2048]{1,0:T(2,128)S(1)} %copy-done.6, ...), custom_call_target="tpu_custom_call" | custom-call | flops 536870912 | bytes 8675328 | tf_op jit(solution)/shard_map/pallas_call | solution.py:51
  15.6 1.4 %copy-done.2 = bf16[2048,1024]{1,0:T(8,128)(2,1)S(1)} copy-done((bf16[2048,1024]{1,0:T(8,128)(2,1)S(1)}, bf16[2048,1024]{1,0:T(8,128)(2,1)}, u32[]{:S(2)}) %copy-start.2) | copy-done | bytes 4194328
  17.0 1.1 %shard_map.94 = (f32[1024,128]{1,0:T(8,128)S(1)}, f32[1024,128]{1,0:T(8,128)S(1)}, f32[1024,128]{1,0:T(8,128)S(1)}, f32[1024,128]{1,0:T(8,128)S(1)}, f32[8,128]{1,0:T(8,128)S(1)}) custom-call(bf16[128,512]{1,0:T(8,128)(2,1)S(1)} %collective-permute-done.3.refs_0_.x_cross, bf16[128,512]{1,0:T(8,128)(2,1)S(1)} %collective-permute-done.4.refs_1_, ...), custom_call_target="tpu_custom_call" | custom-call | flops 536870912 | bytes 9854976 | tf_op jit(solution)/shard_map/pallas_call | solution.py:51
  18.1 1.0 %copy-done.4 = bf16[1024,2048]{1,0:T(8,128)(2,1)S(1)} copy-done((bf16[1024,2048]{1,0:T(8,128)(2,1)S(1)}, bf16[1024,2048]{1,0:T(8,128)(2,1)}, u32[]{:S(2)}) %copy-start.4) | copy-done | bytes 4194328
  19.2 1.8 %shard_map.95 = (bf16[1024,128]{1,0:T(8,128)(2,1)S(1)}, bf16[1024,128]{1,0:T(8,128)(2,1)S(1)}, f32[16,128]{1,0:T(8,128)S(1)}, f32[528,128]{1,0:T(8,128)S(1)}, bf16[528,128]{1,0:T(8,128)(2,1)S(1)}) custom-call(bf16[512,128]{1,0:T(8,128)(2,1)S(1)} %collective-permute-done.refs_0_.cot_cross, bf16[512,128]{1,0:T(8,128)(2,1)S(1)} %collective-permute-done.1.refs_1_, ...), custom_call_target="tpu_custom_call" | custom-call | flops 805306368 | bytes 15466496 | tf_op jit(solution)/shard_map/pallas_call | solution.py:51
  21.0 0.6 %collective-permute-start.9 = (bf16[528,128]{1,0:T(8,128)(2,1)S(1)}, bf16[528,128]{1,0:T(8,128)(2,1)S(1)}, u32[]{:S(2)}, u32[]{:S(2)}) collective-permute-start(bf16[528,128]{1,0:T(8,128)(2,1)S(1)} %get-tuple-element.51), channel_id=1, source_target_pairs={{0,1},{1,0},{2,3},{3,2},{4,5},{5,4},{6,7},{7,6},{8,9},{9,8},{10,11... | collective-permute-start | bytes 405512 | tf_op jit(solution)/shard_map/ppermute | solution.py:20
  21.6 1.7 %collective-permute-start.13 = (bf16[128,512]{1,0:T(8,128)(2,1)S(1)}, bf16[128,512]{1,0:T(8,128)(2,1)S(1)}, u32[]{:S(2)}, u32[]{:S(2)}) collective-permute-start(bf16[128,512]{1,0:T(8,128)(2,1)S(1)} %copy-done.7), channel_id=1, source_target_pairs={{0,2},{1,3},{2,0},{3,1},{4,6},{5,7},{6,4},{7,5},{8,10},{9,11},{10,... | collective-permute-start | bytes 393224 | tf_op jit(solution)/shard_map/ppermute | solution.py:20
  23.3 1.2 %shard_map.96 = (f32[528,128]{1,0:T(8,128)S(1)}, bf16[528,128]{1,0:T(8,128)(2,1)S(1)}) custom-call(bf16[1024,128]{1,0:T(8,128)(2,1)S(1)} %get-tuple-element.44.gg_ref, bf16[1024,128]{1,0:T(8,128)(2,1)S(1)} %get-tuple-element.45.gu_ref, f32[16,128]{1,0:T(8,128)S(1)} %get-tuple-element.46.sums_ref, bf16[2048,1024]{1,0:T(8,128)(2,1)S(1)} %copy-done, ...), custom_call_target="tpu_custom_call" | custom-call | flops 536870912 | bytes 8921088 | tf_op jit(solution)/shard_map/pallas_call | solution.py:51
  24.7 0.3 collective-permute-start.10
  25.1 0.9 %collective-permute-done.6 = bf16[528,128]{1,0:T(8,128)(2,1)S(1)} collective-permute-done((bf16[528,128]{1,0:T(8,128)(2,1)S(1)}, bf16[528,128]{1,0:T(8,128)(2,1)S(1)}, u32[]{:S(2)}, u32[]{:S(2)}) %collective-permute-start.6) | collective-permute-done | bytes 135200 | tf_op jit(solution)/shard_map/ppermute | solution.py:20
  26.0 0.9 %collective-permute-start.7 = (bf16[528,128]{1,0:T(8,128)(2,1)S(1)}, bf16[528,128]{1,0:T(8,128)(2,1)S(1)}, u32[]{:S(2)}, u32[]{:S(2)}) collective-permute-start(bf16[528,128]{1,0:T(8,128)(2,1)S(1)} %get-tuple-element.73), channel_id=1, source_target_pairs={{0,2},{1,3},{2,0},{3,1},{4,6},{5,7},{6,4},{7,5},{8,10},{9,11},{10,... | collective-permute-start | bytes 405512 | tf_op jit(solution)/shard_map/ppermute | solution.py:20
  27.1 0.4 collective-permute-start.14
  27.4 3.7 %collective-permute-done.10.got = bf16[528,128]{1,0:T(8,128)(2,1)S(1)} collective-permute-done((bf16[528,128]{1,0:T(8,128)(2,1)S(1)}, bf16[528,128]{1,0:T(8,128)(2,1)S(1)}, u32[]{:S(2)}, u32[]{:S(2)}) %collective-permute-start.10) | collective-permute-done | bytes 135200 | tf_op jit(solution)/shard_map/ppermute | solution.py:20
  31.2 0.2 shard_map.98.refs_0_.second_a
  31.5 2.2 %collective-permute-done.7.got = bf16[528,128]{1,0:T(8,128)(2,1)S(1)} collective-permute-done((bf16[528,128]{1,0:T(8,128)(2,1)S(1)}, bf16[528,128]{1,0:T(8,128)(2,1)S(1)}, u32[]{:S(2)}, u32[]{:S(2)}) %collective-permute-start.7) | collective-permute-done | bytes 135200 | tf_op jit(solution)/shard_map/ppermute | solution.py:20
  33.7 0.2 shard_map.97.refs_0_.second_b
  34.0 1.7 %shard_map.100 = (f32[1024,128]{1,0:T(8,128)S(1)}, f32[1024,128]{1,0:T(8,128)S(1)}, f32[1024,128]{1,0:T(8,128)S(1)}, f32[1024,128]{1,0:T(8,128)S(1)}, f32[8,128]{1,0:T(8,128)S(1)}) custom-call(bf16[128,512]{1,0:T(8,128)(2,1)S(1)} %copy-done.7, bf16[128,512]{1,0:T(8,128)(2,1)S(1)} %collective-permute-done.12.refs_1_, ...), custom_call_target="tpu_custom_call" | custom-call | flops 1073741824 | bytes 8937472 | tf_op jit(solution)/shard_map/pallas_call | solution.py:51
  35.7 0.7 %shard_map.99.refs_2_ = f32[1024,128]{1,0:T(8,128)S(1)} custom-call(bf16[512,128]{1,0:T(8,128)(2,1)S(1)} %shard_map.98.refs_0_.second_a, bf16[512,128]{1,0:T(8,128)(2,1)S(1)} %collective-permute-done.11.refs_1_, bf16[1024,2048]{1,0:T(8,128)(2,1)S(1)} %copy-done.4), custom_call_target="tpu_custom_call" | custom-call | flops 268435456 | bytes 4456448 | tf_op jit(solution)/shard_map/pallas_call | solution.py:51
  36.4 1.9 %shard_map.101 = (bf16[1024,128]{1,0:T(8,128)(2,1)S(1)}, bf16[1024,128]{1,0:T(8,128)(2,1)S(1)}, f32[16,128]{1,0:T(8,128)S(1)}, f32[528,128]{1,0:T(8,128)S(1)}, bf16[528,128]{1,0:T(8,128)(2,1)S(1)}) custom-call(bf16[512,128]{1,0:T(8,128)(2,1)S(1)} %shard_map.97.refs_0_.second_b, bf16[512,128]{1,0:T(8,128)(2,1)S(1)} %collective-permute-done.8.refs_1_, ...), custom_call_target="tpu_custom_call" | custom-call | flops 805306368 | bytes 15466496 | tf_op jit(solution)/shard_map/pallas_call | solution.py:51
  38.3 0.5 %collective-permute-start.16 = (bf16[528,128]{1,0:T(8,128)(2,1)S(1)}, bf16[528,128]{1,0:T(8,128)(2,1)S(1)}, u32[]{:S(2)}, u32[]{:S(2)}) collective-permute-start(bf16[528,128]{1,0:T(8,128)(2,1)S(1)} %get-tuple-element.67), channel_id=1, source_target_pairs={{0,1},{1,0},{2,3},{3,2},{4,5},{5,4},{6,7},{7,6},{8,9},{9,8},{10,11... | collective-permute-start | bytes 405512 | tf_op jit(solution)/shard_map/ppermute | solution.py:20
  38.8 1.2 %shard_map.102 = (f32[528,128]{1,0:T(8,128)S(1)}, bf16[528,128]{1,0:T(8,128)(2,1)S(1)}) custom-call(bf16[1024,128]{1,0:T(8,128)(2,1)S(1)} %get-tuple-element.61.gg_ref, bf16[1024,128]{1,0:T(8,128)(2,1)S(1)} %get-tuple-element.62.gu_ref, f32[16,128]{1,0:T(8,128)S(1)} %get-tuple-element.63.sums_ref, bf16[2048,1024]{1,0:T(8,128)(2,1)S(1)} %copy-done, ...), custom_call_target="tpu_custom_call" | custom-call | flops 536870912 | bytes 8921088 | tf_op jit(solution)/shard_map/pallas_call | solution.py:51
  40.2 1.0 %collective-permute-start.17 = (bf16[528,128]{1,0:T(8,128)(2,1)S(1)}, bf16[528,128]{1,0:T(8,128)(2,1)S(1)}, u32[]{:S(2)}, u32[]{:S(2)}) collective-permute-start(bf16[528,128]{1,0:T(8,128)(2,1)S(1)} %get-tuple-element.69), channel_id=1, source_target_pairs={{0,2},{1,3},{2,0},{3,1},{4,6},{5,7},{6,4},{7,5},{8,10},{9,11},{10,... | collective-permute-start | bytes 405512 | tf_op jit(solution)/shard_map/ppermute | solution.py:20
  41.5 4.7 %collective-permute-done.17.got = bf16[528,128]{1,0:T(8,128)(2,1)S(1)} collective-permute-done((bf16[528,128]{1,0:T(8,128)(2,1)S(1)}, bf16[528,128]{1,0:T(8,128)(2,1)S(1)}, u32[]{:S(2)}, u32[]{:S(2)}) %collective-permute-start.17) | collective-permute-done | bytes 135200 | tf_op jit(solution)/shard_map/ppermute | solution.py:20
  46.3 1.0 %shard_map.103 = bf16[128,512]{1,0:T(8,128)(2,1)} custom-call(f32[528,128]{1,0:T(8,128)S(1)} %convert_add_fusion.1.own_sum, f32[528,128]{1,0:T(8,128)S(1)} %get-tuple-element.70.chip_theirs, bf16[528,128]{1,0:T(8,128)(2,1)S(1)} %collective-permute-done.17.got, bf16[512,128]{1,0:T(8,128)(2,1)S(1)} %shard_map.98.refs_0_.second_a, ...), custom_call_target="tpu_custom_call" | custom-call | bytes 1098240 | tf_op jit(solution)/shard_map/pallas_call | solution.py:51
  (43 shorter events, 1.4 us)
Async XLA Ops:
  0.0 12.4 %copy-start = (bf16[2048,1024]{1,0:T(8,128)(2,1)S(1)}, bf16[2048,1024]{1,0:T(8,128)(2,1)}, u32[]{:S(2)}) copy-start(bf16[2048,1024]{1,0:T(8,128)(2,1)} %gate_w.3) | copy-start | bytes 12582916
  0.0 7.2 %collective-permute-start.3 = (bf16[128,512]{1,0:T(8,128)(2,1)}, bf16[128,512]{1,0:T(8,128)(2,1)S(1)}, u32[]{:S(2)}, u32[]{:S(2)}) collective-permute-start(bf16[128,512]{1,0:T(8,128)(2,1)} %x_own.4), channel_id=1, source_target_pairs={{0,2},{1,3},{2,0},{3,1},{4,6},{5,7},{6,4},{7,5},{8,10},{9,11},{10,... | collective-permute-start | bytes 393224 | tf_op jit(solution)/shard_map/ppermute | solution.py:20
  3.0 0.9 %copy-start.9 = (bf16[128,512]{1,0:T(8,128)(2,1)S(1)}, bf16[128,512]{1,0:T(8,128)(2,1)}, u32[]{:S(2)}) copy-start(bf16[128,512]{1,0:T(8,128)(2,1)} %value_ref.1) | copy-start | bytes 393220
  4.0 5.5 %collective-permute-start = (bf16[512,128]{1,0:T(8,128)(2,1)S(1)}, bf16[512,128]{1,0:T(8,128)(2,1)S(1)}, u32[]{:S(2)}, u32[]{:S(2)}) collective-permute-start(bf16[512,128]{1,0:T(8,128)(2,1)S(1)} %shard_map.91.refs_0_.cot_own), channel_id=1, source_target_pairs={{0,2},{1,3},{2,0},{3,1},{4,6},{5,7},{6,4},{7,5},{8,10},{9,11},{10,... | collective-permute-start | bytes 393224 | tf_op jit(solution)/shard_map/ppermute | solution.py:20
  4.2 5.3 %collective-permute-start.2 = (bf16[512,128]{1,0:T(8,128)(2,1)S(1)}, bf16[512,128]{1,0:T(8,128)(2,1)S(1)}, u32[]{:S(2)}, u32[]{:S(2)}) collective-permute-start(bf16[512,128]{1,0:T(8,128)(2,1)S(1)} %shard_map.91.refs_0_.cot_own), channel_id=1, source_target_pairs={{0,1},{1,0},{2,3},{3,2},{4,5},{5,4},{6,7},{7,6},{8,9},{9,8},{10,11... | collective-permute-start | bytes 393224 | tf_op jit(solution)/shard_map/ppermute | solution.py:20
  4.2 8.2 %collective-permute-start.5 = (bf16[128,512]{1,0:T(8,128)(2,1)}, bf16[128,512]{1,0:T(8,128)(2,1)S(1)}, u32[]{:S(2)}, u32[]{:S(2)}) collective-permute-start(bf16[128,512]{1,0:T(8,128)(2,1)} %x_own.4), channel_id=1, source_target_pairs={{0,1},{1,0},{2,3},{3,2},{4,5},{5,4},{6,7},{7,6},{8,9},{9,8},{10,11... | collective-permute-start | bytes 393224 | tf_op jit(solution)/shard_map/ppermute | solution.py:20
  7.2 8.4 %collective-permute-start.4 = (bf16[128,512]{1,0:T(8,128)(2,1)S(1)}, bf16[128,512]{1,0:T(8,128)(2,1)S(1)}, u32[]{:S(2)}, u32[]{:S(2)}) collective-permute-start(bf16[128,512]{1,0:T(8,128)(2,1)S(1)} %collective-permute-done.3.refs_0_.x_cross), channel_id=1, source_target_pairs={{0,1},{1,0},{2,3},{3,2},{4,5},{5,4},{6,7},{7,6},{8,9},{9,8},{10,11... | collective-permute-start | bytes 393224 | tf_op jit(solution)/shard_map/ppermute | solution.py:20
  9.5 8.6 %collective-permute-start.1 = (bf16[512,128]{1,0:T(8,128)(2,1)S(1)}, bf16[512,128]{1,0:T(8,128)(2,1)S(1)}, u32[]{:S(2)}, u32[]{:S(2)}) collective-permute-start(bf16[512,128]{1,0:T(8,128)(2,1)S(1)} %collective-permute-done.refs_0_.cot_cross), channel_id=1, source_target_pairs={{0,1},{1,0},{2,3},{3,2},{4,5},{5,4},{6,7},{7,6},{8,9},{9,8},{10,11... | collective-permute-start | bytes 393224 | tf_op jit(solution)/shard_map/ppermute | solution.py:20
  9.5 2.2 %copy-start.3 = (bf16[1024,2048]{1,0:T(8,128)(2,1)S(1)}, bf16[1024,2048]{1,0:T(8,128)(2,1)}, u32[]{:S(2)}) copy-start(bf16[1024,2048]{1,0:T(8,128)(2,1)} %refs_7_.5) | copy-start | bytes 12582916
  11.7 0.9 %copy-start.5 = (bf16[128,512]{1,0:T(8,128)(2,1)S(1)}, bf16[128,512]{1,0:T(8,128)(2,1)}, u32[]{:S(2)}) copy-start(bf16[128,512]{1,0:T(8,128)(2,1)} %x_own.4) | copy-start | bytes 393220
  11.7 0.9 %copy-start.6 = (f32[2,2048]{1,0:T(2,128)S(1)}, f32[2,2048]{1,0:T(2,128)}, u32[]{:S(2)}) copy-start(f32[2,2048]{1,0:T(2,128)} %router_ref.5) | copy-start | bytes 49156
  11.7 0.9 %copy-start.8 = (f32[2048]{0:T(1024)S(1)}, f32[2048]{0:T(1024)}, u32[]{:S(2)}) copy-start(f32[2048]{0:T(1024)} %param.13) | copy-start | bytes 24580
  12.6 2.2 %copy-start.1 = (bf16[2048,1024]{1,0:T(8,128)(2,1)S(1)}, bf16[2048,1024]{1,0:T(8,128)(2,1)}, u32[]{:S(2)}) copy-start(bf16[2048,1024]{1,0:T(8,128)(2,1)} %up_w.3) | copy-start | bytes 12582916
  14.8 2.2 %copy-start.2 = (bf16[2048,1024]{1,0:T(8,128)(2,1)S(1)}, bf16[2048,1024]{1,0:T(8,128)(2,1)}, u32[]{:S(2)}) copy-start(bf16[2048,1024]{1,0:T(8,128)(2,1)} %up_w.3) | copy-start | bytes 12582916
  17.0 2.2 %copy-start.4 = (bf16[1024,2048]{1,0:T(8,128)(2,1)S(1)}, bf16[1024,2048]{1,0:T(8,128)(2,1)}, u32[]{:S(2)}) copy-start(bf16[1024,2048]{1,0:T(8,128)(2,1)} %refs_7_.5) | copy-start | bytes 12582916
  19.2 2.4 %copy-start.7 = (bf16[128,512]{1,0:T(8,128)(2,1)S(1)}, bf16[128,512]{1,0:T(8,128)(2,1)}, u32[]{:S(2)}) copy-start(bf16[128,512]{1,0:T(8,128)(2,1)} %x_own.5) | copy-start | bytes 393220
  21.0 3.6 %collective-permute-start.9 = (bf16[528,128]{1,0:T(8,128)(2,1)S(1)}, bf16[528,128]{1,0:T(8,128)(2,1)S(1)}, u32[]{:S(2)}, u32[]{:S(2)}) collective-permute-start(bf16[528,128]{1,0:T(8,128)(2,1)S(1)} %get-tuple-element.51), channel_id=1, source_target_pairs={{0,1},{1,0},{2,3},{3,2},{4,5},{5,4},{6,7},{7,6},{8,9},{9,8},{10,11... | collective-permute-start | bytes 405512 | tf_op jit(solution)/shard_map/ppermute | solution.py:20
  21.6 5.5 %collective-permute-start.13 = (bf16[128,512]{1,0:T(8,128)(2,1)S(1)}, bf16[128,512]{1,0:T(8,128)(2,1)S(1)}, u32[]{:S(2)}, u32[]{:S(2)}) collective-permute-start(bf16[128,512]{1,0:T(8,128)(2,1)S(1)} %copy-done.7), channel_id=1, source_target_pairs={{0,2},{1,3},{2,0},{3,1},{4,6},{5,7},{6,4},{7,5},{8,10},{9,11},{10,... | collective-permute-start | bytes 393224 | tf_op jit(solution)/shard_map/ppermute | solution.py:20
  23.3 7.8 %copy-start.10 = (s32[128]{0:T(128)S(1)}, s32[128]{0:T(128)}, u32[]{:S(2)}) copy-start(s32[128]{0:T(128)} %param.12) | copy-start | bytes 1540
  24.6 1.4 %collective-permute-start.6 = (bf16[528,128]{1,0:T(8,128)(2,1)S(1)}, bf16[528,128]{1,0:T(8,128)(2,1)S(1)}, u32[]{:S(2)}, u32[]{:S(2)}) collective-permute-start(bf16[528,128]{1,0:T(8,128)(2,1)S(1)} %get-tuple-element.48), channel_id=1, source_target_pairs={{0,1},{1,0},{2,3},{3,2},{4,5},{5,4},{6,7},{7,6},{8,9},{9,8},{10,11... | collective-permute-start | bytes 405512 | tf_op jit(solution)/shard_map/ppermute | solution.py:20
  24.7 6.4 %collective-permute-start.10 = (bf16[528,128]{1,0:T(8,128)(2,1)S(1)}, bf16[528,128]{1,0:T(8,128)(2,1)S(1)}, u32[]{:S(2)}, u32[]{:S(2)}) collective-permute-start(bf16[528,128]{1,0:T(8,128)(2,1)S(1)} %get-tuple-element.71), channel_id=1, source_target_pairs={{0,2},{1,3},{2,0},{3,1},{4,6},{5,7},{6,4},{7,5},{8,10},{9,11},{10,... | collective-permute-start | bytes 405512 | tf_op jit(solution)/shard_map/ppermute | solution.py:20
  26.0 7.6 %collective-permute-start.7 = (bf16[528,128]{1,0:T(8,128)(2,1)S(1)}, bf16[528,128]{1,0:T(8,128)(2,1)S(1)}, u32[]{:S(2)}, u32[]{:S(2)}) collective-permute-start(bf16[528,128]{1,0:T(8,128)(2,1)S(1)} %get-tuple-element.73), channel_id=1, source_target_pairs={{0,2},{1,3},{2,0},{3,1},{4,6},{5,7},{6,4},{7,5},{8,10},{9,11},{10,... | collective-permute-start | bytes 405512 | tf_op jit(solution)/shard_map/ppermute | solution.py:20
  26.9 7.1 %collective-permute-start.12 = (bf16[128,512]{1,0:T(8,128)(2,1)S(1)}, bf16[128,512]{1,0:T(8,128)(2,1)S(1)}, u32[]{:S(2)}, u32[]{:S(2)}) collective-permute-start(bf16[128,512]{1,0:T(8,128)(2,1)S(1)} %copy-done.7), channel_id=1, source_target_pairs={{0,1},{1,0},{2,3},{3,2},{4,5},{5,4},{6,7},{7,6},{8,9},{9,8},{10,11... | collective-permute-start | bytes 393224 | tf_op jit(solution)/shard_map/ppermute | solution.py:20
  27.1 6.9 %collective-permute-start.14 = (bf16[128,512]{1,0:T(8,128)(2,1)S(1)}, bf16[128,512]{1,0:T(8,128)(2,1)S(1)}, u32[]{:S(2)}, u32[]{:S(2)}) collective-permute-start(bf16[128,512]{1,0:T(8,128)(2,1)S(1)} %collective-permute-done.13.refs_2_), channel_id=1, source_target_pairs={{0,1},{1,0},{2,3},{3,2},{4,5},{5,4},{6,7},{7,6},{8,9},{9,8},{10,11... | collective-permute-start | bytes 393224 | tf_op jit(solution)/shard_map/ppermute | solution.py:20
  31.4 4.3 %collective-permute-start.11 = (bf16[512,128]{1,0:T(8,128)(2,1)S(1)}, bf16[512,128]{1,0:T(8,128)(2,1)S(1)}, u32[]{:S(2)}, u32[]{:S(2)}) collective-permute-start(bf16[512,128]{1,0:T(8,128)(2,1)S(1)} %shard_map.98.refs_0_.second_a), channel_id=1, source_target_pairs={{0,1},{1,0},{2,3},{3,2},{4,5},{5,4},{6,7},{7,6},{8,9},{9,8},{10,11... | collective-permute-start | bytes 393224 | tf_op jit(solution)/shard_map/ppermute | solution.py:20
  33.9 2.5 %collective-permute-start.8 = (bf16[512,128]{1,0:T(8,128)(2,1)S(1)}, bf16[512,128]{1,0:T(8,128)(2,1)S(1)}, u32[]{:S(2)}, u32[]{:S(2)}) collective-permute-start(bf16[512,128]{1,0:T(8,128)(2,1)S(1)} %shard_map.97.refs_0_.second_b), channel_id=1, source_target_pairs={{0,1},{1,0},{2,3},{3,2},{4,5},{5,4},{6,7},{7,6},{8,9},{9,8},{10,11... | collective-permute-start | bytes 393224 | tf_op jit(solution)/shard_map/ppermute | solution.py:20
  38.3 1.9 %collective-permute-start.16 = (bf16[528,128]{1,0:T(8,128)(2,1)S(1)}, bf16[528,128]{1,0:T(8,128)(2,1)S(1)}, u32[]{:S(2)}, u32[]{:S(2)}) collective-permute-start(bf16[528,128]{1,0:T(8,128)(2,1)S(1)} %get-tuple-element.67), channel_id=1, source_target_pairs={{0,1},{1,0},{2,3},{3,2},{4,5},{5,4},{6,7},{7,6},{8,9},{9,8},{10,11... | collective-permute-start | bytes 405512 | tf_op jit(solution)/shard_map/ppermute | solution.py:20
  40.1 1.4 %collective-permute-start.15 = (bf16[528,128]{1,0:T(8,128)(2,1)S(1)}, bf16[528,128]{1,0:T(8,128)(2,1)S(1)}, u32[]{:S(2)}, u32[]{:S(2)}) collective-permute-start(bf16[528,128]{1,0:T(8,128)(2,1)S(1)} %get-tuple-element.65), channel_id=1, source_target_pairs={{0,1},{1,0},{2,3},{3,2},{4,5},{5,4},{6,7},{7,6},{8,9},{9,8},{10,11... | collective-permute-start | bytes 405512 | tf_op jit(solution)/shard_map/ppermute | solution.py:20
  40.2 6.0 %collective-permute-start.17 = (bf16[528,128]{1,0:T(8,128)(2,1)S(1)}, bf16[528,128]{1,0:T(8,128)(2,1)S(1)}, u32[]{:S(2)}, u32[]{:S(2)}) collective-permute-start(bf16[528,128]{1,0:T(8,128)(2,1)S(1)} %get-tuple-element.69), channel_id=1, source_target_pairs={{0,2},{1,3},{2,0},{3,1},{4,6},{5,7},{6,4},{7,5},{8,10},{9,11},{10,... | collective-permute-start | bytes 405512 | tf_op jit(solution)/shard_map/ppermute | solution.py:20

commit v2 on v1

v2 whole, which is shorter than its diff:
```python
import functools

import jax
import jax.numpy as jnp
from jax import lax
from jax.experimental import pallas as pl
from jax.experimental.pallas import tpu as pltpu
from jax.sharding import PartitionSpec as P

epsilon = 1e-06
LANES = 128
EXTRA = 16
PIECE = 256
VM = pltpu.VMEM
F32 = jnp.float32
BF16 = jnp.bfloat16


def hop(value, bit):
    size = lax.axis_size("tensor")
    return lax.ppermute(value, "tensor", [(j, j ^ bit) for j in range(size)])


def after(value, *others):
    return lax.optimization_barrier((value,) + others)[0]


def spread(own, low_bits):
    parts = {0: own}
    for bit in reversed(low_bits):
        for key in list(parts):
            parts[key ^ bit] = hop(parts[key], bit)
    return [parts[key] for key in range(len(parts))]


def kernel_call(kernel, outs, *args, flops=0, far=(), scratch=()):
    many = isinstance(outs, (list, tuple))
    args = [
        pltpu.with_memory_space_constraint(a, pltpu.HBM) if n in far else a
        for n, a in enumerate(args)
    ]
    near = pl.BlockSpec(memory_space=VM)
    away = pl.BlockSpec(memory_space=pltpu.HBM)
    return pl.pallas_call(
        kernel,
        out_shape=list(outs) if many else outs,
        in_specs=[away if n in far else near for n in range(len(args))],
        out_specs=[near] * len(outs) if many else near,
        scratch_shapes=list(scratch),
        compiler_params=pltpu.CompilerParams(vmem_limit_bytes=8 * 2**20),
        cost_estimate=pl.CostEstimate(flops=flops, bytes_accessed=0, transcendentals=0),
    )(*args)


def place(top):
    index = lax.axis_index("tensor")
    return index // top, index % top


def span(block, feat):
    return pl.ds(pl.multiple_of(block * feat, feat), feat)


def inside(top, key, feat):
    return span(place(top)[1] ^ (key % top), feat)


def overall(top, key, feat):
    side, inner = place(top)
    return span((side * top + inner) ^ key, feat)


def turned(value):
    value = value.astype(F32)
    return jnp.concatenate(
        [value[:, k : k + LANES].T for k in range(0, value.shape[1], LANES)], axis=0
    )


def column(row, tokens):
    return turned(jnp.broadcast_to(row, (tokens, row.shape[1])))


def mat(left, right):
    return jnp.dot(left, right, preferred_element_type=F32)


def mat_turned(left, right):
    return lax.dot_general(
        left, right, (((1,), (1,)), ((), ())), preferred_element_type=F32
    )


def fetch(sems, pairs):
    copies = []
    for n, (source, target) in enumerate(pairs):
        copy = pltpu.make_async_copy(source, target, sems.at[n])
        copy.start()
        copies.append(copy)
    return copies


def pieces(source, target):
    rows = target.shape[0]
    step = min(PIECE, rows)
    return [
        (source.at[n : n + step, :], target.at[n : n + step, :]) for n in range(0, rows, step)
    ]


def half_rows(top, far, mine):
    half = far.shape[0] // 2
    side, _ = place(top)
    return far.at[span(side if mine else 1 - side, half), :]


def norm_block(top, key, x_ref, router_row, gain_ref, router_ref, gate_w, up_w, total):
    gate, up, squares, logits = total
    feat = x_ref.shape[1]
    at, rows = overall(top, key, feat), inside(top, key, feat)
    x = x_ref[...].astype(F32)
    gained = (x * gain_ref[:, at]).astype(BF16)
    routed = x * router_ref[router_row : router_row + 1, at]
    for k in range(0, feat, LANES):
        squares = squares + x[:, k : k + LANES] * x[:, k : k + LANES]
        logits = logits + routed[:, k : k + LANES]
    gate_now, up_now = mat(gained, gate_w[rows, :]), mat(gained, up_w[rows, :])
    if gate is None:
        return gate_now, up_now, squares, logits
    return gate + gate_now, up + up_now, squares, logits


def norm_start(tokens):
    zeros = jnp.zeros((tokens, LANES), F32)
    return None, None, zeros, zeros


def own_kernel(top, router_row, *refs):
    smalls, (gate_far, up_far, down_far), small_outs, nears, outs, sems = (
        refs[:6], refs[6:9], refs[9:15], refs[15:18], refs[18:22], refs[22]
    )
    copies = fetch(
        sems,
        [
            *zip(smalls, small_outs),
            *pieces(half_rows(top, gate_far, True), nears[0]),
            *pieces(half_rows(top, up_far, True), nears[1]),
            *pieces(down_far, nears[2]),
        ],
    )
    ready = 6 + 2 * len(pieces(nears[0], nears[0]))
    for copy in copies[:ready]:
        copy.wait()
    x, cot, _, gain_ref, router_ref, _ = small_outs
    total = norm_block(
        top, 0, x, router_row, gain_ref, router_ref, *nears[:2], norm_start(x.shape[0])
    )
    outs[0][...], outs[1][...], outs[2][0], outs[2][1] = total
    for copy in copies[ready:]:
        copy.wait()
    outs[3][...] = back_raw(top, (0,), (cot,), nears[2])


def near_kernel(top, router_row, *refs):
    n = top - 1
    xs, cots, weights, down_w, held, fars, outs, nears, sems = (
        refs[:n], refs[n : 2 * n], refs[2 * n : 2 * n + 4], refs[2 * n + 4],
        refs[2 * n + 5 : 2 * n + 9], refs[2 * n + 9 : 2 * n + 11],
        refs[2 * n + 11 : 2 * n + 15], refs[2 * n + 15 : 2 * n + 17], refs[2 * n + 17],
    )
    copies = fetch(
        sems,
        [pair for far, near in zip(fars, nears) for pair in pieces(half_rows(top, far, False), near)],
    )
    total = (held[0][...], held[1][...], held[2][0], held[2][1])
    for key, x in enumerate(xs):
        total = norm_block(top, key + 1, x, router_row, *weights, total)
    outs[0][...], outs[1][...], outs[2][0], outs[2][1] = total
    outs[3][...] = back_raw(top, range(1, top), cots, down_w, held[3][...])
    for copy in copies:
        copy.wait()


def write_factors(total, wide, outs):
    gate, up, squares, logits = total
    inv_rms = lax.rsqrt(jnp.sum(squares.T, axis=0, keepdims=True) / wide + epsilon)
    score = jax.nn.sigmoid(jnp.sum(logits.T, axis=0, keepdims=True))
    outs[4][...] = jnp.concatenate(
        [inv_rms, score, jnp.zeros((6, inv_rms.shape[1]), F32)], axis=0
    )
    for k in range(0, gate.shape[1], LANES):
        g = gate[:, k : k + LANES].T * inv_rms
        u = up[:, k : k + LANES].T * inv_rms
        sigma = jax.nn.sigmoid(g)
        silu = g * sigma
        grad = u * sigma * (1.0 + g * (1.0 - sigma))
        act = silu * u
        here = slice(k, k + LANES)
        outs[0][here, :] = score * grad
        outs[1][here, :] = score * silu
        outs[2][here, :] = act
        outs[3][here, :] = score * (grad * g + act)


def factors_second_kernel(top, router_row, *refs):
    xs, (gain_ref, router_ref, gate_w, up_w), held, outs = (
        refs[:top], refs[top : top + 4], refs[top + 4 : top + 7], refs[top + 7 :]
    )
    total = (held[0][...], held[1][...], held[2][0], held[2][1])
    for n, x in enumerate(xs):
        total = norm_block(top, top + n, x, router_row, gain_ref, router_ref, gate_w, up_w, total)
    write_factors(total, gain_ref.shape[1], outs)


def factors_first_kernel(top, router_row, *refs):
    xs, (gain_ref, router_ref), weights, outs = (
        refs[: 2 * top], refs[2 * top : 2 * top + 2], refs[2 * top + 2 : 2 * top + 6],
        refs[2 * top + 6 :],
    )
    total = norm_start(xs[0].shape[0])
    for key, x in enumerate(xs):
        gate_w, up_w = weights[:2] if key < top else weights[2:]
        total = norm_block(top, key, x, router_row, gain_ref, router_ref, gate_w, up_w, total)
    write_factors(total, gain_ref.shape[1], outs)


def back_raw(top, keys, parts, down_w, total=None):
    for key, part in zip(keys, parts):
        now = mat_turned(down_w[:, overall(top, key, part.shape[1])], part[...])
        total = now if total is None else total + now
    return total


def back_sum(top, keys, parts, down_w, total=None):
    for key, part in zip(keys, parts):
        now = mat(down_w[:, overall(top, key, part.shape[0])], part[...])
        total = now if total is None else total + now
    return total


def back_part_kernel(top, keys, *refs):
    n = len(keys)
    refs[n + 1][...] = back_sum(top, keys, refs[:n], refs[n])


def write_terms(top, keys, gg, gu, sums, weights, outs):
    for n, out_ref in enumerate(outs):
        gate_w, up_w = weights[2 * (n // len(keys)) : 2 * (n // len(keys)) + 2]
        feat = out_ref.shape[0] - EXTRA
        rows = inside(top, keys[n % len(keys)], feat)
        term = mat(gate_w[rows, :], gg) + mat(up_w[rows, :], gu)
        out_ref[0:feat, :] = term.astype(out_ref.dtype)
        out_ref[feat : feat + EXTRA, :] = sums.astype(out_ref.dtype)


def double(out_ref):
    rows = out_ref.shape[0] // 2
    return out_ref.at[0:rows, :], out_ref.at[rows : 2 * rows, :]


def back_kernel(top, keys, raw, *refs):
    n = len(keys)
    parts, down_w = refs[:n], refs[n]
    held, grad_p, silu_p, act_p, dot_p = refs[n + 1 : n + 6]
    weights, (gg_ref, gu_ref, sums_ref), outs = (
        refs[n + 6 : n + 10], refs[n + 10 : n + 13], refs[n + 13 :]
    )
    back = (back_raw if raw else back_sum)(top, keys, parts, down_w, held[...])
    gg = (back * grad_p[...]).astype(BF16)
    gu = (back * silu_p[...]).astype(BF16)
    score_part = jnp.sum(back * act_p[...], axis=0, keepdims=True)
    dot_part = jnp.sum(back * dot_p[...], axis=0, keepdims=True)
    sums = jnp.concatenate(
        [score_part, dot_part, jnp.zeros((EXTRA - 2, LANES), F32)], axis=0
    )
    gg_ref[...] = gg
    gu_ref[...] = gu
    sums_ref[...] = sums
    for key, out_ref in zip(range(1, top, 2), outs):
        write_terms(top, (key,), gg, gu, sums, weights, double(out_ref))


def kept_kernel(top, keys, gg_ref, gu_ref, sums_ref, *refs):
    weights, outs = refs[:4], refs[4:]
    write_terms(top, keys, gg_ref[...], gu_ref[...], sums_ref[...], weights, outs)


def row_factors(sums, rows, wide):
    inv_rms, score = rows[0:1, :], rows[1:2, :]
    return inv_rms * inv_rms * (sums[1:2, :] / wide), sums[0:1, :] * score * (1.0 - score)


def column_kernel(top, keys, level, *refs):
    n = len(keys)
    xs, (gain_ref, router_ref, depths_ref, rows_ref), outs = refs[:n], refs[n : n + 4], refs[n + 4 :]
    active = (depths_ref[...] >= level).astype(F32)
    for n, key in enumerate(keys):
        tokens, feat = xs[n].shape
        at = overall(top, key, feat)
        outs[3 * n][...] = turned(xs[n][...]) * active
        outs[3 * n + 1][...] = column(gain_ref[:, at], tokens) * (active * rows_ref[0:1, :])
        outs[3 * n + 2][...] = column(router_ref[level - 1 : level, at], tokens) * active


def turn_kernel(first, second, first_out, second_out):
    first_out[...] = turned(first[...])
    second_out[...] = turned(second[...])


def second_kernel(wide, chip, got, cot, x, scale, router, rows_ref, out_ref):
    feat = out_ref.shape[0]
    total = chip[...] + got[...].astype(F32)
    coef, logit = row_factors(total[feat : feat + 2, :], rows_ref[...], wide)
    delta = scale[...] * total[0:feat, :] - x[...] * coef + router[...] * logit
    out_ref[...] = (cot[...].astype(F32) + delta).astype(out_ref.dtype)


def last_kernel(wide, chip, got, second, x, scale, router, rows_ref, out_ref):
    feat = out_ref.shape[1]
    total = chip[...] + got[...].astype(F32)
    coef, logit = row_factors(total[feat : feat + 2, :], rows_ref[...], wide)
    delta = scale[...] * total[0:feat, :] - x[...] * coef + router[...] * logit
    result = second[...].astype(F32) + delta
    for k in range(0, feat, LANES):
        out_ref[:, k : k + LANES] = result[k : k + LANES, :].T.astype(out_ref.dtype)


def body(hidden_first, hidden_second, cotangent, depths, norm_gain, router, w_gate, w_up, w_down):
    size = lax.axis_size("tensor")
    bits = []
    while 2 ** len(bits) < size:
        bits.append(2 ** len(bits))
    top, low = bits[-1], bits[:-1]
    tokens, feat = hidden_first.shape
    wide, units = w_gate.shape
    half = wide // 2
    product = 2 * tokens * half * units
    wide_units = VM((units, LANES), F32)
    factor_outs = [wide_units] * 4 + [VM((8, LANES), F32)]
    partial_outs = [VM((tokens, units), F32)] * 2 + [VM((2, tokens, LANES), F32)]
    grad_outs = [VM((units, LANES), BF16)] * 2 + [VM((EXTRA, LANES), F32)]
    columns = [VM((feat, tokens), F32)] * 3
    row_half = VM((half, units), BF16)
    near, across = range(top), range(top, 2 * top)
    sent, kept = range(1, top, 2), range(0, top, 2)
    block = feat + EXTRA

    def semaphores(count):
        return [pltpu.SemaphoreType.DMA((count,))]

    def reduce(grads, blocks_sent):
        parts = kernel_call(
            functools.partial(kept_kernel, top, kept),
            [VM((block, LANES), F32)] * (2 * len(kept)), *grads, *theirs, *mine,
            flops=8 * product,
        )
        blocks = dict(zip(kept, zip(parts[: len(kept)], parts[len(kept) :])))
        whole = dict(zip(sent, blocks_sent))
        for bit in low:
            for key in sorted(blocks):
                if key & bit == 0:
                    value = whole.get(key ^ bit)
                    if value is None:
                        value = jnp.concatenate(blocks[key ^ bit]).astype(BF16)
                    value = hop(value, bit).astype(F32)
                    blocks[key] = tuple(
                        own + got for own, got in zip(blocks[key], (value[:block], value[block:]))
                    )
                    blocks.pop(key ^ bit, None)
        return blocks[0]

    def back_call(keys, raw, parts, held, factors):
        *grads, = kernel_call(
            functools.partial(back_kernel, top, keys, raw),
            grad_outs + [VM((2 * block, LANES), BF16)] * len(sent),
            *parts, down, held, *factors, *theirs, *mine, flops=2 * product,
        )
        return grads[:3], grads[3:]

    x2_cross = hop(hidden_second, top)
    cot_cross = hop(cotangent, top)
    x2_mine = spread(hidden_second, low)
    cot_mine = spread(cotangent, low)
    smalls = (
        hidden_second, cotangent, hidden_first, norm_gain.reshape(1, -1), router,
        depths.reshape(1, tokens),
    )
    own_outs = partial_outs + [wide_units]
    outs = kernel_call(
        functools.partial(own_kernel, top, 1),
        [VM(a.shape, a.dtype) for a in smalls] + [row_half] * 2 + [VM(w_down.shape, BF16)] + own_outs,
        *smalls, w_gate, w_up, w_down,
        flops=3 * product // top, far=range(9),
        scratch=semaphores(6 + 2 * -(-half // PIECE) + -(-units // PIECE)),
    )
    x2_own, cot_own, x1_own, gain, router, depths, gate_mine, up_mine, down, *partial = outs
    x2_cross, *partial = lax.optimization_barrier((x2_cross, *partial))
    x2_theirs = spread(x2_cross, low)
    x1_cross = hop(after(x1_own, x2_cross), top)
    x1_mine = spread(x1_own, low)
    *partial, back_mine, gate_theirs, up_theirs = kernel_call(
        functools.partial(near_kernel, top, 1),
        own_outs + [row_half] * 2,
        *x2_mine[1:], *cot_mine[1:], gain, router, gate_mine, up_mine, down, *partial,
        w_gate, w_up, flops=3 * product * (top - 1) // top,
        far=(2 * top + 7, 2 * top + 8), scratch=semaphores(2 * -(-half // PIECE)),
    )
    mine, theirs = (gate_mine, up_mine), (gate_theirs, up_theirs)
    cot_cross, back_mine, x1_mine = lax.optimization_barrier((cot_cross, back_mine, x1_mine))
    cot_theirs = spread(cot_cross, low)
    *factors2, rows2 = kernel_call(
        functools.partial(factors_second_kernel, top, 1),
        factor_outs, *x2_theirs, gain, router, *theirs, *partial, flops=2 * product,
    )

    grads, blocks_sent = back_call(across, True, cot_theirs, back_mine, factors2)
    x1_cross, *grads = lax.optimization_barrier((x1_cross, *grads))
    x1_theirs = spread(x1_cross, low)
    chip_theirs, chip_mine = reduce(grads, blocks_sent)
    x1_theirs, chip_theirs, chip_mine = lax.optimization_barrier(
        (x1_theirs, chip_theirs, chip_mine)
    )
    got_mine = hop(chip_theirs.astype(BF16), top)
    got_theirs = hop(chip_mine.astype(BF16), top)

    rows2, chip_mine = lax.optimization_barrier((rows2, chip_mine))
    columns2 = kernel_call(
        functools.partial(column_kernel, top, (0, top), 2),
        columns * 2, x2_own, x2_cross, gain, router, depths, rows2,
    )
    cot_columns = kernel_call(turn_kernel, columns[:2], after(cot_own, rows2), cot_cross)

    x1_parts = (*x1_mine, *x1_theirs)
    *factors1, rows1 = kernel_call(
        functools.partial(factors_first_kernel, top, 0),
        factor_outs, *x1_parts, gain, router, *mine, *theirs, flops=4 * product,
    )

    def second(chip, got, cot, columns):
        return kernel_call(
            functools.partial(second_kernel, wide),
            VM((feat, tokens), BF16), chip, got, cot, *columns, rows2,
        )

    got_mine, *factors1 = lax.optimization_barrier((got_mine, *factors1))
    own_second = second(chip_mine, got_mine, cot_columns[0], columns2[:3])
    second_mine = spread(own_second, low)
    cross_second = second(chip_theirs, got_theirs, cot_columns[1], columns2[3:])
    second_theirs = spread(cross_second, low)
    back_most = kernel_call(
        functools.partial(back_part_kernel, top, (*near, top)),
        wide_units, *second_mine, cross_second, down, flops=product,
    )
    grads, blocks_sent = back_call(across[1:], False, second_theirs[1:], back_most, factors1)
    chip_theirs, chip_mine = reduce(grads, blocks_sent)
    got = hop(chip_theirs.astype(BF16), top)
    rows1 = after(rows1, chip_mine)
    columns1 = kernel_call(
        functools.partial(column_kernel, top, (0,), 1),
        columns, x1_own, gain, router, depths, rows1,
    )
    return kernel_call(
        functools.partial(last_kernel, wide),
        jax.ShapeDtypeStruct((tokens, feat), BF16),
        chip_mine, got, own_second, *columns1, rows1,
    )


def solution(mesh):
    in_specs = (
        P("dp", "tensor"),
        P("dp", "tensor"),
        P("dp", "tensor"),
        P("dp"),
        P(),
        P(),
        P(None, "tensor"),
        P(None, "tensor"),
        P("tensor", None),
    )
    out_specs = P("dp", "tensor")
    return jax.shard_map(body, mesh=mesh, in_specs=in_specs, out_specs=out_specs, check_vma=False)
```

time: 47.5 us -> 39.2 us (0.83)
  local copies, waits for them, and re-layouts: 7.87 us -> 0 us
  waiting for transfers between devices: 16.7 us -> 9.54 us
  Pallas kernels: 12.8 us -> 18.3 us
  starting transfers between devices: 9.47 us -> 10.7 us
    unnamed x22 -> x0, local copies, waits for them, and re-layouts: 7.87 us -> none
    ppermute x18 -> x16, waiting for transfers between devices: 16.7 us -> 9.54 us  [hop(): return lax.ppermute(value, 'tensor', [(j, j ^ bit) for j in range(size)])]
    pallas_call x13 -> x15, Pallas kernels: 12.8 us -> 18.3 us  [kernel_call(): pl.pallas_call(kernel, out_shape=list(outs) if many else outs, in_specs=[...]
    ppermute x18 -> x16, starting transfers between devices: 9.47 us -> 10.7 us  [hop(): return lax.ppermute(value, 'tensor', [(j, j ^ bit) for j in range(size)])]
  transfers between devices with their start and end apart: 18 -> 16, of which waited for: 8 -> 6; matrix products, arithmetic and copies ran while one was open for 0% -> 0% of each run, Pallas kernels for 17% -> 41%
where the time goes in v2:
time: 39.2 us; the launch traced here: 39.1 us
  Pallas kernels  18.3 us (47%)
  starting transfers between devices  10.7 us (27%)
  waiting for transfers between devices  9.54 us (24%)
    pallas_call x15, Pallas kernels, kernel_call(): pl.pallas_call(kernel, out_shape=list(outs) if many else outs, in_specs=[...  18.3 us
    ppermute x16, starting transfers between devices, hop(): return lax.ppermute(value, 'tensor', [(j, j ^ bit) for j in range(size)])  10.7 us
    ppermute x16, waiting for transfers between devices, hop(): return lax.ppermute(value, 'tensor', [(j, j ^ bit) for j in range(size)])  9.54 us
  transfers between devices with their start and end apart: 16, of which 6 were waited for; matrix products, arithmetic and copies ran while one was open for 0% of the time, Pallas kernels for 41%

profile of v2, /device:TPU:0, one launch (start us, length us, event | category | flops | bytes accessed | tf_op | source)
XLA Modules:
  0.0 39.1 jit_solution(16521715292624786427)
XLA Ops:
  0.0 3.0 %collective-permute-start = (bf16[128,512]{1,0:T(8,128)(2,1)}, bf16[128,512]{1,0:T(8,128)(2,1)S(1)}, u32[]{:S(2)}, u32[]{:S(2)}) collective-permute-start(bf16[128,512]{1,0:T(8,128)(2,1)} %refs_0_.1), channel_id=1, source_target_pairs={{0,2},{1,3},{2,0},{3,1},{4,6},{5,7},{6,4},{7,5},{8,10},{9,11},{10,... | collective-permute-start | bytes 393224 | tf_op jit(solution)/shard_map/ppermute | solution.py:21
  3.0 0.5 %collective-permute-start.4 = (bf16[128,512]{1,0:T(8,128)(2,1)}, bf16[128,512]{1,0:T(8,128)(2,1)S(1)}, u32[]{:S(2)}, u32[]{:S(2)}) collective-permute-start(bf16[128,512]{1,0:T(8,128)(2,1)} %refs_1_.1), channel_id=1, source_target_pairs={{0,1},{1,0},{2,3},{3,2},{4,5},{5,4},{6,7},{7,6},{8,9},{9,8},{10,11... | collective-permute-start | bytes 393224 | tf_op jit(solution)/shard_map/ppermute | solution.py:21
  3.5 4.2 %shard_map.91 = (bf16[128,512]{1,0:T(8,128)(2,1)S(1)}, bf16[128,512]{1,0:T(8,128)(2,1)S(1)}, bf16[128,512]{1,0:T(8,128)(2,1)S(1)}, f32[1,2048]{1,0:T(1,128)S(1)}...) custom-call(bf16[128,512]{1,0:T(8,128)(2,1)} %refs_0_.1, ...), custom_call_target="tpu_custom_call" | custom-call | flops 402653184 | tf_op jit(solution)/shard_map/pallas_call | solution.py:44
  7.8 0.5 %collective-permute-start.7 = (bf16[128,512]{1,0:T(8,128)(2,1)S(1)}, bf16[128,512]{1,0:T(8,128)(2,1)S(1)}, u32[]{:S(2)}, u32[]{:S(2)}) collective-permute-start(bf16[128,512]{1,0:T(8,128)(2,1)S(1)} %collective-permute-done.refs_0_.refs_1_), channel_id=1, source_target_pairs={{0,1},{1,0},{2,3},{3,2},{4,5},{5,4},{6,7},{7,6},{8,9},{9,8},{10,11... | collective-permute-start | bytes 393224 | tf_op jit(solution)/shard_map/ppermute | solution.py:21
  8.3 2.6 %shard_map.92 = (f32[128,1024]{1,0:T(8,128)S(1)}, f32[128,1024]{1,0:T(8,128)S(1)}, f32[2,128,128]{2,1,0:T(8,128)S(1)}, f32[1024,128]{1,0:T(8,128)S(1)}, bf16[102...) custom-call(bf16[128,512]{1,0:T(8,128)(2,1)S(1)} %collective-permute-done.3.refs_0_, ...), custom_call_target="tpu_custom_call" | custom-call | flops 402653184 | tf_op jit(solution)/shard_map/pallas_call | solution.py:44
  11.0 0.1 collective-permute-start.6
  11.1 2.0 %collective-permute-start.1 = (bf16[128,512]{1,0:T(8,128)(2,1)S(1)}, bf16[128,512]{1,0:T(8,128)(2,1)S(1)}, u32[]{:S(2)}, u32[]{:S(2)}) collective-permute-start(bf16[128,512]{1,0:T(8,128)(2,1)S(1)} %get-tuple-element.135.refs_0_), channel_id=1, source_target_pairs={{0,2},{1,3},{2,0},{3,1},{4,6},{5,7},{6,4},{7,5},{8,10},{9,11},{10,... | collective-permute-start | bytes 393224 | tf_op jit(solution)/shard_map/ppermute | solution.py:21
  13.1 1.1 %shard_map.93 = (f32[1024,128]{1,0:T(8,128)S(1)}, f32[1024,128]{1,0:T(8,128)S(1)}, f32[1024,128]{1,0:T(8,128)S(1)}, f32[1024,128]{1,0:T(8,128)S(1)}, f32[8,128]{1,0:T(8,128)S(1)}) custom-call(bf16[128,512]{1,0:T(8,128)(2,1)S(1)} %collective-permute-done.refs_0_.refs_1_, bf16[128,512]{1,0:T(8,128)(2,1)S(1)} %collective-permute-done.7.refs_1_, ...), custom_call_target="tpu_custom_call" | custom-call | flops 536870912 | tf_op jit(solution)/shard_map/pallas_call | solution.py:44
  14.3 1.8 %shard_map.94 = (bf16[1024,128]{1,0:T(8,128)(2,1)S(1)}, bf16[1024,128]{1,0:T(8,128)(2,1)S(1)}, f32[16,128]{1,0:T(8,128)S(1)}, bf16[1056,128]{1,0:T(8,128)(2,1)S(1)}) custom-call(bf16[128,512]{1,0:T(8,128)(2,1)S(1)} %collective-permute-done.2.refs_0_.second, bf16[128,512]{1,0:T(8,128)(2,1)S(1)} %collective-permute-done.6.refs_1_, ...), custom_call_target="tpu_custom_call" | custom-call | flops 536870912 | tf_op jit(solution)/shard_map/pallas_call | solution.py:44
  16.1 0.2 collective-permute-start.9
  16.3 0.9 %collective-permute-done.1.refs_2_ = bf16[128,512]{1,0:T(8,128)(2,1)S(1)} collective-permute-done((bf16[128,512]{1,0:T(8,128)(2,1)S(1)}, bf16[128,512]{1,0:T(8,128)(2,1)S(1)}, u32[]{:S(2)}, u32[]{:S(2)}) %collective-permute-start.1) | collective-permute-done | bytes 131104 | tf_op jit(solution)/shard_map/ppermute | solution.py:21
  17.2 1.2 %shard_map.95 = (f32[528,128]{1,0:T(8,128)S(1)}, f32[528,128]{1,0:T(8,128)S(1)}) custom-call(bf16[1024,128]{1,0:T(8,128)(2,1)S(1)} %get-tuple-element.116.gg_ref, bf16[1024,128]{1,0:T(8,128)(2,1)S(1)} %get-tuple-element.117.gu_ref, f32[16,128]{1,0:T(8,128)S(1)} %get-tuple-element.118.sums_ref, ...), custom_call_target="tpu_custom_call" | custom-call | flops 2147483648 | tf_op jit(solution)/shard_map/pallas_call | solution.py:44
  18.5 0.1 slice_add_fusion.2
  18.7 1.8 %collective-permute-start.12 = (bf16[528,128]{1,0:T(8,128)(2,1)S(1)}, bf16[528,128]{1,0:T(8,128)(2,1)S(1)}, u32[]{:S(2)}, u32[]{:S(2)}) collective-permute-start(bf16[528,128]{1,0:T(8,128)(2,1)S(1)} %convert_element_type.17), channel_id=1, source_target_pairs={{0,2},{1,3},{2,0},{3,1},{4,6},{5,7},{6,4},{7,5},{8,10},{9,11},{10,... | collective-permute-start | bytes 405512 | tf_op jit(solution)/shard_map/ppermute | solution.py:21
  20.5 0.3 collective-permute-start.10
  20.8 0.1 shard_map.96
  21.0 0.4 %shard_map.97 = (f32[512,128]{1,0:T(8,128)S(1)}, f32[512,128]{1,0:T(8,128)S(1)}, f32[512,128]{1,0:T(8,128)S(1)}, f32[512,128]{1,0:T(8,128)S(1)}, f32[512,128]{1,0:T(8,128)S(1)}, /*index=5*/f32[512,128]{1,0:T(8,128)S(1)}) custom-call(bf16[128,512]{1,0:T(8,128)(2,1)S(1)} %get-tuple-element.129.refs_0_, ...), custom_call_target="tpu_custom_call" | custom-call | tf_op jit(solution)/shard_map/pallas_call | solution.py:44
  21.4 1.7 %shard_map.99 = (f32[1024,128]{1,0:T(8,128)S(1)}, f32[1024,128]{1,0:T(8,128)S(1)}, f32[1024,128]{1,0:T(8,128)S(1)}, f32[1024,128]{1,0:T(8,128)S(1)}, f32[8,128]{1,0:T(8,128)S(1)}) custom-call(bf16[128,512]{1,0:T(8,128)(2,1)S(1)} %get-tuple-element.135.refs_0_, bf16[128,512]{1,0:T(8,128)(2,1)S(1)} %collective-permute-done.5.refs_1_, ...), custom_call_target="tpu_custom_call" | custom-call | flops 1073741824 | tf_op jit(solution)/shard_map/pallas_call | solution.py:44
  23.1 2.0 %collective-permute-done.12.got = bf16[528,128]{1,0:T(8,128)(2,1)S(1)} collective-permute-done((bf16[528,128]{1,0:T(8,128)(2,1)S(1)}, bf16[528,128]{1,0:T(8,128)(2,1)S(1)}, u32[]{:S(2)}, u32[]{:S(2)}) %collective-permute-start.12) | collective-permute-done | bytes 135200 | tf_op jit(solution)/shard_map/ppermute | solution.py:21
  25.1 0.1 shard_map.100.refs_0_.second
  25.3 2.4 %collective-permute-done.10.got = bf16[528,128]{1,0:T(8,128)(2,1)S(1)} collective-permute-done((bf16[528,128]{1,0:T(8,128)(2,1)S(1)}, bf16[528,128]{1,0:T(8,128)(2,1)S(1)}, u32[]{:S(2)}, u32[]{:S(2)}) %collective-permute-start.10) | collective-permute-done | bytes 135200 | tf_op jit(solution)/shard_map/ppermute | solution.py:21
  27.6 0.1 shard_map.98.refs_2_
  27.8 1.0 %shard_map.101.refs_2_ = f32[1024,128]{1,0:T(8,128)S(1)} custom-call(bf16[512,128]{1,0:T(8,128)(2,1)S(1)} %shard_map.100.refs_0_.second, bf16[512,128]{1,0:T(8,128)(2,1)S(1)} %collective-permute-done.13.refs_1_, bf16[512,128]{1,0:T(8,128)(2,1)S(1)} %shard_map.98.refs_2_, bf16[1024,2048]{1,0:T(8,128)(2,1)S(1)} %get-tuple-element.95.refs_6_.refs_2_.refs_3_.refs_1_), custom_call_target="tpu_custom_call" | custom-call | flops 268435456 | tf_op jit(solution)/shard_map/pallas_call | solution.py:44
  28.8 0.3 collective-permute-done.11.refs_0_
  29.2 1.6 %shard_map.102 = (bf16[1024,128]{1,0:T(8,128)(2,1)S(1)}, bf16[1024,128]{1,0:T(8,128)(2,1)S(1)}, f32[16,128]{1,0:T(8,128)S(1)}, bf16[1056,128]{1,0:T(8,128)(2,1)S(1)}) custom-call(bf16[512,128]{1,0:T(8,128)(2,1)S(1)} %collective-permute-done.11.refs_0_, bf16[1024,2048]{1,0:T(8,128)(2,1)S(1)} %get-tuple-element.95.refs_6_.refs_2_.refs_3_.refs_1_, ...), custom_call_target="tpu_custom_call" | custom-call | flops 536870912 | tf_op jit(solution)/shard_map/pallas_call | solution.py:44
  30.7 0.2 collective-permute-start.14
  30.9 1.2 %shard_map.103 = (f32[528,128]{1,0:T(8,128)S(1)}, f32[528,128]{1,0:T(8,128)S(1)}) custom-call(bf16[1024,128]{1,0:T(8,128)(2,1)S(1)} %get-tuple-element.152.gg_ref, bf16[1024,128]{1,0:T(8,128)(2,1)S(1)} %get-tuple-element.153.gu_ref, f32[16,128]{1,0:T(8,128)S(1)} %get-tuple-element.154.sums_ref, ...), custom_call_target="tpu_custom_call" | custom-call | flops 2147483648 | tf_op jit(solution)/shard_map/pallas_call | solution.py:44
  32.2 0.2 collective-permute-done.14
  32.5 1.8 %collective-permute-start.15 = (bf16[528,128]{1,0:T(8,128)(2,1)S(1)}, bf16[528,128]{1,0:T(8,128)(2,1)S(1)}, u32[]{:S(2)}, u32[]{:S(2)}) collective-permute-start(bf16[528,128]{1,0:T(8,128)(2,1)S(1)} %get-tuple-element.163), channel_id=1, source_target_pairs={{0,2},{1,3},{2,0},{3,1},{4,6},{5,7},{6,4},{7,5},{8,10},{9,11},{10,... | collective-permute-start | bytes 405512 | tf_op jit(solution)/shard_map/ppermute | solution.py:21
  34.3 0.2 shard_map.104
  34.5 3.7 %collective-permute-done.15.got = bf16[528,128]{1,0:T(8,128)(2,1)S(1)} collective-permute-done((bf16[528,128]{1,0:T(8,128)(2,1)S(1)}, bf16[528,128]{1,0:T(8,128)(2,1)S(1)}, u32[]{:S(2)}, u32[]{:S(2)}) %collective-permute-start.15) | collective-permute-done | bytes 135200 | tf_op jit(solution)/shard_map/ppermute | solution.py:21
  38.2 0.8 %shard_map.105 = bf16[128,512]{1,0:T(8,128)(2,1)} custom-call(f32[528,128]{1,0:T(8,128)S(1)} %get-tuple-element.164.chip, bf16[528,128]{1,0:T(8,128)(2,1)S(1)} %collective-permute-done.15.got, bf16[512,128]{1,0:T(8,128)(2,1)S(1)} %shard_map.100.refs_0_.second, f32[512,128]{1,0:T(8,128)S(1)} %get-tuple-element.160.x, ...), custom_call_target="tpu_custom_call" | custom-call | tf_op jit(solution)/shard_map/pallas_call | solution.py:44
  (21 shorter events, 0.4 us)
Async XLA Ops:
  0.0 7.8 %collective-permute-start = (bf16[128,512]{1,0:T(8,128)(2,1)}, bf16[128,512]{1,0:T(8,128)(2,1)S(1)}, u32[]{:S(2)}, u32[]{:S(2)}) collective-permute-start(bf16[128,512]{1,0:T(8,128)(2,1)} %refs_0_.1), channel_id=1, source_target_pairs={{0,2},{1,3},{2,0},{3,1},{4,6},{5,7},{6,4},{7,5},{8,10},{9,11},{10,... | collective-permute-start | bytes 393224 | tf_op jit(solution)/shard_map/ppermute | solution.py:21
  3.0 5.3 %collective-permute-start.3 = (bf16[128,512]{1,0:T(8,128)(2,1)}, bf16[128,512]{1,0:T(8,128)(2,1)S(1)}, u32[]{:S(2)}, u32[]{:S(2)}) collective-permute-start(bf16[128,512]{1,0:T(8,128)(2,1)} %refs_0_.1), channel_id=1, source_target_pairs={{0,1},{1,0},{2,3},{3,2},{4,5},{5,4},{6,7},{7,6},{8,9},{9,8},{10,11... | collective-permute-start | bytes 393224 | tf_op jit(solution)/shard_map/ppermute | solution.py:21
  3.0 5.3 %collective-permute-start.4 = (bf16[128,512]{1,0:T(8,128)(2,1)}, bf16[128,512]{1,0:T(8,128)(2,1)S(1)}, u32[]{:S(2)}, u32[]{:S(2)}) collective-permute-start(bf16[128,512]{1,0:T(8,128)(2,1)} %refs_1_.1), channel_id=1, source_target_pairs={{0,1},{1,0},{2,3},{3,2},{4,5},{5,4},{6,7},{7,6},{8,9},{9,8},{10,11... | collective-permute-start | bytes 393224 | tf_op jit(solution)/shard_map/ppermute | solution.py:21
  3.5 7.5 %collective-permute-start.2 = (bf16[128,512]{1,0:T(8,128)(2,1)}, bf16[128,512]{1,0:T(8,128)(2,1)S(1)}, u32[]{:S(2)}, u32[]{:S(2)}) collective-permute-start(bf16[128,512]{1,0:T(8,128)(2,1)} %refs_1_.1), channel_id=1, source_target_pairs={{0,2},{1,3},{2,0},{3,1},{4,6},{5,7},{6,4},{7,5},{8,10},{9,11},{10,... | collective-permute-start | bytes 393224 | tf_op jit(solution)/shard_map/ppermute | solution.py:21
  7.7 3.2 %collective-permute-start.5 = (bf16[128,512]{1,0:T(8,128)(2,1)S(1)}, bf16[128,512]{1,0:T(8,128)(2,1)S(1)}, u32[]{:S(2)}, u32[]{:S(2)}) collective-permute-start(bf16[128,512]{1,0:T(8,128)(2,1)S(1)} %get-tuple-element.135.refs_0_), channel_id=1, source_target_pairs={{0,1},{1,0},{2,3},{3,2},{4,5},{5,4},{6,7},{7,6},{8,9},{9,8},{10,11... | collective-permute-start | bytes 393224 | tf_op jit(solution)/shard_map/ppermute | solution.py:21
  7.8 5.3 %collective-permute-start.7 = (bf16[128,512]{1,0:T(8,128)(2,1)S(1)}, bf16[128,512]{1,0:T(8,128)(2,1)S(1)}, u32[]{:S(2)}, u32[]{:S(2)}) collective-permute-start(bf16[128,512]{1,0:T(8,128)(2,1)S(1)} %collective-permute-done.refs_0_.refs_1_), channel_id=1, source_target_pairs={{0,1},{1,0},{2,3},{3,2},{4,5},{5,4},{6,7},{7,6},{8,9},{9,8},{10,11... | collective-permute-start | bytes 393224 | tf_op jit(solution)/shard_map/ppermute | solution.py:21
  11.0 3.3 %collective-permute-start.6 = (bf16[128,512]{1,0:T(8,128)(2,1)S(1)}, bf16[128,512]{1,0:T(8,128)(2,1)S(1)}, u32[]{:S(2)}, u32[]{:S(2)}) collective-permute-start(bf16[128,512]{1,0:T(8,128)(2,1)S(1)} %collective-permute-done.2.refs_0_.second), channel_id=1, source_target_pairs={{0,1},{1,0},{2,3},{3,2},{4,5},{5,4},{6,7},{7,6},{8,9},{9,8},{10,11... | collective-permute-start | bytes 393224 | tf_op jit(solution)/shard_map/ppermute | solution.py:21
  11.1 6.1 %collective-permute-start.1 = (bf16[128,512]{1,0:T(8,128)(2,1)S(1)}, bf16[128,512]{1,0:T(8,128)(2,1)S(1)}, u32[]{:S(2)}, u32[]{:S(2)}) collective-permute-start(bf16[128,512]{1,0:T(8,128)(2,1)S(1)} %get-tuple-element.135.refs_0_), channel_id=1, source_target_pairs={{0,2},{1,3},{2,0},{3,1},{4,6},{5,7},{6,4},{7,5},{8,10},{9,11},{10,... | collective-permute-start | bytes 393224 | tf_op jit(solution)/shard_map/ppermute | solution.py:21
  16.1 2.4 %collective-permute-start.9 = (bf16[1056,128]{1,0:T(8,128)(2,1)S(1)}, bf16[1056,128]{1,0:T(8,128)(2,1)S(1)}, u32[]{:S(2)}, u32[]{:S(2)}) collective-permute-start(bf16[1056,128]{1,0:T(8,128)(2,1)S(1)} %get-tuple-element.120), channel_id=1, source_target_pairs={{0,1},{1,0},{2,3},{3,2},{4,5},{5,4},{6,7},{7,6},{8,9},{9,8},{10,11... | collective-permute-start | bytes 811016 | tf_op jit(solution)/shard_map/ppermute | solution.py:21
  17.2 1.4 %collective-permute-start.8 = (bf16[128,512]{1,0:T(8,128)(2,1)S(1)}, bf16[128,512]{1,0:T(8,128)(2,1)S(1)}, u32[]{:S(2)}, u32[]{:S(2)}) collective-permute-start(bf16[128,512]{1,0:T(8,128)(2,1)S(1)} %collective-permute-done.1.refs_2_), channel_id=1, source_target_pairs={{0,1},{1,0},{2,3},{3,2},{4,5},{5,4},{6,7},{7,6},{8,9},{9,8},{10,11... | collective-permute-start | bytes 393224 | tf_op jit(solution)/shard_map/ppermute | solution.py:21
  18.7 6.4 %collective-permute-start.12 = (bf16[528,128]{1,0:T(8,128)(2,1)S(1)}, bf16[528,128]{1,0:T(8,128)(2,1)S(1)}, u32[]{:S(2)}, u32[]{:S(2)}) collective-permute-start(bf16[528,128]{1,0:T(8,128)(2,1)S(1)} %convert_element_type.17), channel_id=1, source_target_pairs={{0,2},{1,3},{2,0},{3,1},{4,6},{5,7},{6,4},{7,5},{8,10},{9,11},{10,... | collective-permute-start | bytes 405512 | tf_op jit(solution)/shard_map/ppermute | solution.py:21
  20.5 7.1 %collective-permute-start.10 = (bf16[528,128]{1,0:T(8,128)(2,1)S(1)}, bf16[528,128]{1,0:T(8,128)(2,1)S(1)}, u32[]{:S(2)}, u32[]{:S(2)}) collective-permute-start(bf16[528,128]{1,0:T(8,128)(2,1)S(1)} %convert_element_type.16), channel_id=1, source_target_pairs={{0,2},{1,3},{2,0},{3,1},{4,6},{5,7},{6,4},{7,5},{8,10},{9,11},{10,... | collective-permute-start | bytes 405512 | tf_op jit(solution)/shard_map/ppermute | solution.py:21
  25.2 2.6 %collective-permute-start.13 = (bf16[512,128]{1,0:T(8,128)(2,1)S(1)}, bf16[512,128]{1,0:T(8,128)(2,1)S(1)}, u32[]{:S(2)}, u32[]{:S(2)}) collective-permute-start(bf16[512,128]{1,0:T(8,128)(2,1)S(1)} %shard_map.100.refs_0_.second), channel_id=1, source_target_pairs={{0,1},{1,0},{2,3},{3,2},{4,5},{5,4},{6,7},{7,6},{8,9},{9,8},{10,11... | collective-permute-start | bytes 393224 | tf_op jit(solution)/shard_map/ppermute | solution.py:21
  27.8 1.4 %collective-permute-start.11 = (bf16[512,128]{1,0:T(8,128)(2,1)S(1)}, bf16[512,128]{1,0:T(8,128)(2,1)S(1)}, u32[]{:S(2)}, u32[]{:S(2)}) collective-permute-start(bf16[512,128]{1,0:T(8,128)(2,1)S(1)} %shard_map.98.refs_2_), channel_id=1, source_target_pairs={{0,1},{1,0},{2,3},{3,2},{4,5},{5,4},{6,7},{7,6},{8,9},{9,8},{10,11... | collective-permute-start | bytes 393224 | tf_op jit(solution)/shard_map/ppermute | solution.py:21
  30.7 1.6 %collective-permute-start.14 = (bf16[1056,128]{1,0:T(8,128)(2,1)S(1)}, bf16[1056,128]{1,0:T(8,128)(2,1)S(1)}, u32[]{:S(2)}, u32[]{:S(2)}) collective-permute-start(bf16[1056,128]{1,0:T(8,128)(2,1)S(1)} %get-tuple-element.156), channel_id=1, source_target_pairs={{0,1},{1,0},{2,3},{3,2},{4,5},{5,4},{6,7},{7,6},{8,9},{9,8},{10,11... | collective-permute-start | bytes 811016 | tf_op jit(solution)/shard_map/ppermute | solution.py:21
  32.5 5.8 %collective-permute-start.15 = (bf16[528,128]{1,0:T(8,128)(2,1)S(1)}, bf16[528,128]{1,0:T(8,128)(2,1)S(1)}, u32[]{:S(2)}, u32[]{:S(2)}) collective-permute-start(bf16[528,128]{1,0:T(8,128)(2,1)S(1)} %get-tuple-element.163), channel_id=1, source_target_pairs={{0,2},{1,3},{2,0},{3,1},{4,6},{5,7},{6,4},{7,5},{8,10},{9,11},{10,... | collective-permute-start | bytes 405512 | tf_op jit(solution)/shard_map/ppermute | solution.py:21

commit v3 on v2

--- a/solution.py
+++ b/solution.py
@@ -48,7 +48,7 @@
         out_specs=[near] * len(outs) if many else near,
         scratch_shapes=list(scratch),
         compiler_params=pltpu.CompilerParams(vmem_limit_bytes=8 * 2**20),
-        cost_estimate=pl.CostEstimate(flops=flops, bytes_accessed=0, transcendentals=0),
+        cost_estimate=pl.CostEstimate(flops=6 * flops, bytes_accessed=0, transcendentals=0),
     )(*args)
 
 
@@ -137,7 +137,7 @@
 
 def own_kernel(top, router_row, *refs):
     smalls, (gate_far, up_far, down_far), small_outs, nears, outs, sems = (
-        refs[:6], refs[6:9], refs[9:15], refs[15:18], refs[18:22], refs[22]
+        refs[:6], refs[6:9], refs[9:15], refs[15:20], refs[20:24], refs[24]
     )
     copies = fetch(
         sems,
@@ -146,6 +146,8 @@
             *pieces(half_rows(top, gate_far, True), nears[0]),
             *pieces(half_rows(top, up_far, True), nears[1]),
             *pieces(down_far, nears[2]),
+            *pieces(half_rows(top, gate_far, False), nears[3]),
+            *pieces(half_rows(top, up_far, False), nears[4]),
         ],
     )
     ready = 6 + 2 * len(pieces(nears[0], nears[0]))
@@ -156,29 +158,25 @@
         top, 0, x, router_row, gain_ref, router_ref, *nears[:2], norm_start(x.shape[0])
     )
     outs[0][...], outs[1][...], outs[2][0], outs[2][1] = total
-    for copy in copies[ready:]:
+    rest = ready + len(pieces(nears[2], nears[2]))
+    for copy in copies[ready:rest]:
         copy.wait()
     outs[3][...] = back_raw(top, (0,), (cot,), nears[2])
+    for copy in copies[rest:]:
+        copy.wait()
 
 
 def near_kernel(top, router_row, *refs):
     n = top - 1
-    xs, cots, weights, down_w, held, fars, outs, nears, sems = (
+    xs, cots, weights, down_w, held, outs = (
         refs[:n], refs[n : 2 * n], refs[2 * n : 2 * n + 4], refs[2 * n + 4],
-        refs[2 * n + 5 : 2 * n + 9], refs[2 * n + 9 : 2 * n + 11],
-        refs[2 * n + 11 : 2 * n + 15], refs[2 * n + 15 : 2 * n + 17], refs[2 * n + 17],
-    )
-    copies = fetch(
-        sems,
-        [pair for far, near in zip(fars, nears) for pair in pieces(half_rows(top, far, False), near)],
+        refs[2 * n + 5 : 2 * n + 9], refs[2 * n + 9 :],
     )
     total = (held[0][...], held[1][...], held[2][0], held[2][1])
     for key, x in enumerate(xs):
         total = norm_block(top, key + 1, x, router_row, *weights, total)
     outs[0][...], outs[1][...], outs[2][0], outs[2][1] = total
     outs[3][...] = back_raw(top, range(1, top), cots, down_w, held[3][...])
-    for copy in copies:
-        copy.wait()
 
 
 def write_factors(total, wide, outs):
@@ -388,22 +386,23 @@
     own_outs = partial_outs + [wide_units]
     outs = kernel_call(
         functools.partial(own_kernel, top, 1),
-        [VM(a.shape, a.dtype) for a in smalls] + [row_half] * 2 + [VM(w_down.shape, BF16)] + own_outs,
+        [VM(a.shape, a.dtype) for a in smalls]
+        + [row_half] * 2 + [VM(w_down.shape, BF16)] + [row_half] * 2 + own_outs,
         *smalls, w_gate, w_up, w_down,
         flops=3 * product // top, far=range(9),
-        scratch=semaphores(6 + 2 * -(-half // PIECE) + -(-units // PIECE)),
-    )
-    x2_own, cot_own, x1_own, gain, router, depths, gate_mine, up_mine, down, *partial = outs
+        scratch=semaphores(6 + 4 * -(-half // PIECE) + -(-units // PIECE)),
+    )
+    x2_own, cot_own, x1_own, gain, router, depths, gate_mine, up_mine, down = outs[:9]
+    gate_theirs, up_theirs, *partial = outs[9:]
     x2_cross, *partial = lax.optimization_barrier((x2_cross, *partial))
     x2_theirs = spread(x2_cross, low)
-    x1_cross = hop(after(x1_own, x2_cross), top)
+    x1_cross = hop(hidden_first, top)
     x1_mine = spread(x1_own, low)
-    *partial, back_mine, gate_theirs, up_theirs = kernel_call(
+    *partial, back_mine = kernel_call(
         functools.partial(near_kernel, top, 1),
-        own_outs + [row_half] * 2,
+        own_outs,
         *x2_mine[1:], *cot_mine[1:], gain, router, gate_mine, up_mine, down, *partial,
-        w_gate, w_up, flops=3 * product * (top - 1) // top,
-        far=(2 * top + 7, 2 * top + 8), scratch=semaphores(2 * -(-half // PIECE)),
+        flops=3 * product * (top - 1) // top,
     )
     mine, theirs = (gate_mine, up_mine), (gate_theirs, up_theirs)
     cot_cross, back_mine, x1_mine = lax.optimization_barrier((cot_cross, back_mine, x1_mine))
@@ -421,7 +420,6 @@
         (x1_theirs, chip_theirs, chip_mine)
     )
     got_mine = hop(chip_theirs.astype(BF16), top)
-    got_theirs = hop(chip_mine.astype(BF16), top)
 
     rows2, chip_mine = lax.optimization_barrier((rows2, chip_mine))
     columns2 = kernel_call(
@@ -430,6 +428,8 @@
     )
     cot_columns = kernel_call(turn_kernel, columns[:2], after(cot_own, rows2), cot_cross)
 
+    columns2, chip_mine = lax.optimization_barrier((columns2, chip_mine))
+    got_theirs = hop(chip_mine.astype(BF16), top)
     x1_parts = (*x1_mine, *x1_theirs)
     *factors1, rows1 = kernel_call(
         functools.partial(factors_first_kernel, top, 0),

time: 39.2 us -> 36.9 us (0.941)
  Pallas kernels: 18.3 us -> 17.1 us
  starting transfers between devices: 10.7 us -> 9.8 us
    pallas_call x15, Pallas kernels: 18.3 us -> 17.1 us  [kernel_call(): pl.pallas_call(kernel, out_shape=list(outs) if many else outs, in_specs=[...]
    ppermute x16, starting transfers between devices: 10.7 us -> 9.8 us  [hop(): return lax.ppermute(value, 'tensor', [(j, j ^ bit) for j in range(size)])]
  transfers between devices with their start and end apart: 16 -> 16, of which waited for: 6 -> 7; matrix products, arithmetic and copies ran while one was open for 0% -> 0% of each run, Pallas kernels for 41% -> 40%
where the time goes in v3:
time: 36.9 us; the launch traced here: 36.8 us
  Pallas kernels  17.1 us (46%)
  starting transfers between devices  9.8 us (27%)
  waiting for transfers between devices  9.44 us (26%)
    pallas_call x15, Pallas kernels, kernel_call(): pl.pallas_call(kernel, out_shape=list(outs) if many else outs, in_specs=[...  17.1 us
    ppermute x16, starting transfers between devices, hop(): return lax.ppermute(value, 'tensor', [(j, j ^ bit) for j in range(size)])  9.8 us
    ppermute x16, waiting for transfers between devices, hop(): return lax.ppermute(value, 'tensor', [(j, j ^ bit) for j in range(size)])  9.44 us
  transfers between devices with their start and end apart: 16, of which 7 were waited for; matrix products, arithmetic and copies ran while one was open for 0% of the time, Pallas kernels for 40%

profile of v3, /device:TPU:0, one launch (start us, length us, event | category | flops | bytes accessed | tf_op | source)
XLA Modules:
  0.0 36.8 jit_solution(11654332208397621087)
XLA Ops:
  0.0 0.5 %collective-permute-start.2 = (bf16[128,512]{1,0:T(8,128)(2,1)}, bf16[128,512]{1,0:T(8,128)(2,1)S(1)}, u32[]{:S(2)}, u32[]{:S(2)}) collective-permute-start(bf16[128,512]{1,0:T(8,128)(2,1)} %refs_0_.1), channel_id=1, source_target_pairs={{0,1},{1,0},{2,3},{3,2},{4,5},{5,4},{6,7},{7,6},{8,9},{9,8},{10,11... | collective-permute-start | bytes 393224 | tf_op jit(solution)/shard_map/ppermute | solution.py:21
  0.5 2.5 %collective-permute-start.4 = (bf16[128,512]{1,0:T(8,128)(2,1)}, bf16[128,512]{1,0:T(8,128)(2,1)S(1)}, u32[]{:S(2)}, u32[]{:S(2)}) collective-permute-start(bf16[128,512]{1,0:T(8,128)(2,1)} %refs_0_.1), channel_id=1, source_target_pairs={{0,2},{1,3},{2,0},{3,1},{4,6},{5,7},{6,4},{7,5},{8,10},{9,11},{10,... | collective-permute-start | bytes 393224 | tf_op jit(solution)/shard_map/ppermute | solution.py:21
  3.0 0.2 collective-permute-start.3
  3.2 1.8 %collective-permute-start = (bf16[128,512]{1,0:T(8,128)(2,1)}, bf16[128,512]{1,0:T(8,128)(2,1)S(1)}, u32[]{:S(2)}, u32[]{:S(2)}) collective-permute-start(bf16[128,512]{1,0:T(8,128)(2,1)} %refs_2_.1), channel_id=1, source_target_pairs={{0,2},{1,3},{2,0},{3,1},{4,6},{5,7},{6,4},{7,5},{8,10},{9,11},{10,... | collective-permute-start | bytes 393224 | tf_op jit(solution)/shard_map/ppermute | solution.py:21
  5.0 5.0 %shard_map.91 = (bf16[128,512]{1,0:T(8,128)(2,1)S(1)}, bf16[128,512]{1,0:T(8,128)(2,1)S(1)}, bf16[128,512]{1,0:T(8,128)(2,1)S(1)}, f32[1,2048]{1,0:T(1,128)S(1)}...) custom-call(bf16[128,512]{1,0:T(8,128)(2,1)} %refs_0_.1, ...), custom_call_target="tpu_custom_call" | custom-call | flops 2415919104 | tf_op jit(solution)/shard_map/pallas_call | solution.py:44
  10.0 0.3 collective-permute-start.5
  10.3 0.3 collective-permute-start.7
  10.6 0.8 %shard_map.92 = (f32[128,1024]{1,0:T(8,128)S(1)}, f32[128,1024]{1,0:T(8,128)S(1)}, f32[2,128,128]{2,1,0:T(8,128)S(1)}, f32[1024,128]{1,0:T(8,128)S(1)}) custom-call(bf16[128,512]{1,0:T(8,128)(2,1)S(1)} %collective-permute-done.2.refs_0_, bf16[128,512]{1,0:T(8,128)(2,1)S(1)} %collective-permute-done.3.refs_1_, ...), custom_call_target="tpu_custom_call" | custom-call | flops 2415919104 | tf_op jit(solution)/shard_map/pallas_call | solution.py:44
  11.5 0.2 collective-permute-start.6
  11.7 1.1 %shard_map.93 = (f32[1024,128]{1,0:T(8,128)S(1)}, f32[1024,128]{1,0:T(8,128)S(1)}, f32[1024,128]{1,0:T(8,128)S(1)}, f32[1024,128]{1,0:T(8,128)S(1)}, f32[8,128]{1,0:T(8,128)S(1)}) custom-call(bf16[128,512]{1,0:T(8,128)(2,1)S(1)} %collective-permute-done.4.refs_0_.refs_1_, bf16[128,512]{1,0:T(8,128)(2,1)S(1)} %collective-permute-done.7.refs_1_, ...), custom_call_target="tpu_custom_call" | custom-call | flops 3221225472 | tf_op jit(solution)/shard_map/pallas_call | solution.py:44
  12.8 1.8 %shard_map.94 = (bf16[1024,128]{1,0:T(8,128)(2,1)S(1)}, bf16[1024,128]{1,0:T(8,128)(2,1)S(1)}, f32[16,128]{1,0:T(8,128)S(1)}, bf16[1056,128]{1,0:T(8,128)(2,1)S(1)}) custom-call(bf16[128,512]{1,0:T(8,128)(2,1)S(1)} %collective-permute-done.1.refs_0_.second, bf16[128,512]{1,0:T(8,128)(2,1)S(1)} %collective-permute-done.6.refs_1_, ...), custom_call_target="tpu_custom_call" | custom-call | flops 3221225472 | tf_op jit(solution)/shard_map/pallas_call | solution.py:44
  14.7 0.3 collective-permute-start.8
  15.0 0.2 collective-permute-start.9
  15.2 1.2 %shard_map.95 = (f32[528,128]{1,0:T(8,128)S(1)}, f32[528,128]{1,0:T(8,128)S(1)}) custom-call(bf16[1024,128]{1,0:T(8,128)(2,1)S(1)} %get-tuple-element.121.gg_ref, bf16[1024,128]{1,0:T(8,128)(2,1)S(1)} %get-tuple-element.122.gu_ref, f32[16,128]{1,0:T(8,128)S(1)} %get-tuple-element.123.sums_ref, ...), custom_call_target="tpu_custom_call" | custom-call | flops 12884901888 | tf_op jit(solution)/shard_map/pallas_call | solution.py:44
  16.7 0.9 %collective-permute-start.12 = (bf16[528,128]{1,0:T(8,128)(2,1)S(1)}, bf16[528,128]{1,0:T(8,128)(2,1)S(1)}, u32[]{:S(2)}, u32[]{:S(2)}) collective-permute-start(bf16[528,128]{1,0:T(8,128)(2,1)S(1)} %convert_element_type.17), channel_id=1, source_target_pairs={{0,2},{1,3},{2,0},{3,1},{4,6},{5,7},{6,4},{7,5},{8,10},{9,11},{10,... | collective-permute-start | bytes 405512 | tf_op jit(solution)/shard_map/ppermute | solution.py:21
  17.6 0.4 %shard_map.96 = (f32[512,128]{1,0:T(8,128)S(1)}, f32[512,128]{1,0:T(8,128)S(1)}, f32[512,128]{1,0:T(8,128)S(1)}, f32[512,128]{1,0:T(8,128)S(1)}, f32[512,128]{1,0:T(8,128)S(1)}, /*index=5*/f32[512,128]{1,0:T(8,128)S(1)}) custom-call(bf16[128,512]{1,0:T(8,128)(2,1)S(1)} %get-tuple-element.128.refs_0_, ...), custom_call_target="tpu_custom_call" | custom-call | tf_op jit(solution)/shard_map/pallas_call | solution.py:44
  18.0 1.3 %collective-permute-start.10 = (bf16[528,128]{1,0:T(8,128)(2,1)S(1)}, bf16[528,128]{1,0:T(8,128)(2,1)S(1)}, u32[]{:S(2)}, u32[]{:S(2)}) collective-permute-start(bf16[528,128]{1,0:T(8,128)(2,1)S(1)} %convert_element_type.16), channel_id=1, source_target_pairs={{0,2},{1,3},{2,0},{3,1},{4,6},{5,7},{6,4},{7,5},{8,10},{9,11},{10,... | collective-permute-start | bytes 405512 | tf_op jit(solution)/shard_map/ppermute | solution.py:21
  19.3 1.6 %shard_map.99 = (f32[1024,128]{1,0:T(8,128)S(1)}, f32[1024,128]{1,0:T(8,128)S(1)}, f32[1024,128]{1,0:T(8,128)S(1)}, f32[1024,128]{1,0:T(8,128)S(1)}, f32[8,128]{1,0:T(8,128)S(1)}) custom-call(bf16[128,512]{1,0:T(8,128)(2,1)S(1)} %get-tuple-element.147.refs_0_, bf16[128,512]{1,0:T(8,128)(2,1)S(1)} %collective-permute-done.5.refs_1_, ...), custom_call_target="tpu_custom_call" | custom-call | flops 6442450944 | tf_op jit(solution)/shard_map/pallas_call | solution.py:44
  21.0 0.1 shard_map.97
  21.1 2.1 %collective-permute-done.12.got = bf16[528,128]{1,0:T(8,128)(2,1)S(1)} collective-permute-done((bf16[528,128]{1,0:T(8,128)(2,1)S(1)}, bf16[528,128]{1,0:T(8,128)(2,1)S(1)}, u32[]{:S(2)}, u32[]{:S(2)}) %collective-permute-start.12) | collective-permute-done | bytes 135200 | tf_op jit(solution)/shard_map/ppermute | solution.py:21
  23.2 0.1 shard_map.100.refs_0_.second
  23.4 2.0 %collective-permute-done.10.got = bf16[528,128]{1,0:T(8,128)(2,1)S(1)} collective-permute-done((bf16[528,128]{1,0:T(8,128)(2,1)S(1)}, bf16[528,128]{1,0:T(8,128)(2,1)S(1)}, u32[]{:S(2)}, u32[]{:S(2)}) %collective-permute-start.10) | collective-permute-done | bytes 135200 | tf_op jit(solution)/shard_map/ppermute | solution.py:21
  25.6 1.0 %shard_map.101.refs_2_ = f32[1024,128]{1,0:T(8,128)S(1)} custom-call(bf16[512,128]{1,0:T(8,128)(2,1)S(1)} %shard_map.100.refs_0_.second, bf16[512,128]{1,0:T(8,128)(2,1)S(1)} %collective-permute-done.13.refs_1_, bf16[512,128]{1,0:T(8,128)(2,1)S(1)} %shard_map.98.refs_2_, bf16[1024,2048]{1,0:T(8,128)(2,1)S(1)} %get-tuple-element.94.refs_6_.refs_2_.refs_3_.refs_1_), custom_call_target="tpu_custom_call" | custom-call | flops 1610612736 | tf_op jit(solution)/shard_map/pallas_call | solution.py:44
  26.6 0.3 collective-permute-done.11.refs_0_
  26.9 1.5 %shard_map.102 = (bf16[1024,128]{1,0:T(8,128)(2,1)S(1)}, bf16[1024,128]{1,0:T(8,128)(2,1)S(1)}, f32[16,128]{1,0:T(8,128)S(1)}, bf16[1056,128]{1,0:T(8,128)(2,1)S(1)}) custom-call(bf16[512,128]{1,0:T(8,128)(2,1)S(1)} %collective-permute-done.11.refs_0_, bf16[1024,2048]{1,0:T(8,128)(2,1)S(1)} %get-tuple-element.94.refs_6_.refs_2_.refs_3_.refs_1_, ...), custom_call_target="tpu_custom_call" | custom-call | flops 3221225472 | tf_op jit(solution)/shard_map/pallas_call | solution.py:44
  28.5 0.2 collective-permute-start.14
  28.7 1.2 %shard_map.103 = (f32[528,128]{1,0:T(8,128)S(1)}, f32[528,128]{1,0:T(8,128)S(1)}) custom-call(bf16[1024,128]{1,0:T(8,128)(2,1)S(1)} %get-tuple-element.164.gg_ref, bf16[1024,128]{1,0:T(8,128)(2,1)S(1)} %get-tuple-element.165.gu_ref, f32[16,128]{1,0:T(8,128)S(1)} %get-tuple-element.166.sums_ref, ...), custom_call_target="tpu_custom_call" | custom-call | flops 12884901888 | tf_op jit(solution)/shard_map/pallas_call | solution.py:44
  29.9 0.1 collective-permute-done.14
  30.2 0.9 %collective-permute-start.15 = (bf16[528,128]{1,0:T(8,128)(2,1)S(1)}, bf16[528,128]{1,0:T(8,128)(2,1)S(1)}, u32[]{:S(2)}, u32[]{:S(2)}) collective-permute-start(bf16[528,128]{1,0:T(8,128)(2,1)S(1)} %get-tuple-element.175), channel_id=1, source_target_pairs={{0,2},{1,3},{2,0},{3,1},{4,6},{5,7},{6,4},{7,5},{8,10},{9,11},{10,... | collective-permute-start | bytes 405512 | tf_op jit(solution)/shard_map/ppermute | solution.py:21
  31.1 0.2 shard_map.104
  31.3 4.7 %collective-permute-done.15.got = bf16[528,128]{1,0:T(8,128)(2,1)S(1)} collective-permute-done((bf16[528,128]{1,0:T(8,128)(2,1)S(1)}, bf16[528,128]{1,0:T(8,128)(2,1)S(1)}, u32[]{:S(2)}, u32[]{:S(2)}) %collective-permute-start.15) | collective-permute-done | bytes 135200 | tf_op jit(solution)/shard_map/ppermute | solution.py:21
  36.0 0.8 %shard_map.105 = bf16[128,512]{1,0:T(8,128)(2,1)} custom-call(f32[528,128]{1,0:T(8,128)S(1)} %get-tuple-element.176.chip, bf16[528,128]{1,0:T(8,128)(2,1)S(1)} %collective-permute-done.15.got, bf16[512,128]{1,0:T(8,128)(2,1)S(1)} %shard_map.100.refs_0_.second, f32[512,128]{1,0:T(8,128)S(1)} %get-tuple-element.172.x, ...), custom_call_target="tpu_custom_call" | custom-call | tf_op jit(solution)/shard_map/pallas_call | solution.py:44
  (21 shorter events, 0.7 us)
Async XLA Ops:
  0.0 10.3 %collective-permute-start.2 = (bf16[128,512]{1,0:T(8,128)(2,1)}, bf16[128,512]{1,0:T(8,128)(2,1)S(1)}, u32[]{:S(2)}, u32[]{:S(2)}) collective-permute-start(bf16[128,512]{1,0:T(8,128)(2,1)} %refs_0_.1), channel_id=1, source_target_pairs={{0,1},{1,0},{2,3},{3,2},{4,5},{5,4},{6,7},{7,6},{8,9},{9,8},{10,11... | collective-permute-start | bytes 393224 | tf_op jit(solution)/shard_map/ppermute | solution.py:21
  0.5 9.6 %collective-permute-start.4 = (bf16[128,512]{1,0:T(8,128)(2,1)}, bf16[128,512]{1,0:T(8,128)(2,1)S(1)}, u32[]{:S(2)}, u32[]{:S(2)}) collective-permute-start(bf16[128,512]{1,0:T(8,128)(2,1)} %refs_0_.1), channel_id=1, source_target_pairs={{0,2},{1,3},{2,0},{3,1},{4,6},{5,7},{6,4},{7,5},{8,10},{9,11},{10,... | collective-permute-start | bytes 393224 | tf_op jit(solution)/shard_map/ppermute | solution.py:21
  3.0 8.4 %collective-permute-start.1 = (bf16[128,512]{1,0:T(8,128)(2,1)}, bf16[128,512]{1,0:T(8,128)(2,1)S(1)}, u32[]{:S(2)}, u32[]{:S(2)}) collective-permute-start(bf16[128,512]{1,0:T(8,128)(2,1)} %refs_1_.1), channel_id=1, source_target_pairs={{0,2},{1,3},{2,0},{3,1},{4,6},{5,7},{6,4},{7,5},{8,10},{9,11},{10,... | collective-permute-start | bytes 393224 | tf_op jit(solution)/shard_map/ppermute | solution.py:21
  3.0 7.6 %collective-permute-start.3 = (bf16[128,512]{1,0:T(8,128)(2,1)}, bf16[128,512]{1,0:T(8,128)(2,1)S(1)}, u32[]{:S(2)}, u32[]{:S(2)}) collective-permute-start(bf16[128,512]{1,0:T(8,128)(2,1)} %refs_1_.1), channel_id=1, source_target_pairs={{0,1},{1,0},{2,3},{3,2},{4,5},{5,4},{6,7},{7,6},{8,9},{9,8},{10,11... | collective-permute-start | bytes 393224 | tf_op jit(solution)/shard_map/ppermute | solution.py:21
  3.2 11.4 %collective-permute-start = (bf16[128,512]{1,0:T(8,128)(2,1)}, bf16[128,512]{1,0:T(8,128)(2,1)S(1)}, u32[]{:S(2)}, u32[]{:S(2)}) collective-permute-start(bf16[128,512]{1,0:T(8,128)(2,1)} %refs_2_.1), channel_id=1, source_target_pairs={{0,2},{1,3},{2,0},{3,1},{4,6},{5,7},{6,4},{7,5},{8,10},{9,11},{10,... | collective-permute-start | bytes 393224 | tf_op jit(solution)/shard_map/ppermute | solution.py:21
  10.0 1.4 %collective-permute-start.5 = (bf16[128,512]{1,0:T(8,128)(2,1)S(1)}, bf16[128,512]{1,0:T(8,128)(2,1)S(1)}, u32[]{:S(2)}, u32[]{:S(2)}) collective-permute-start(bf16[128,512]{1,0:T(8,128)(2,1)S(1)} %get-tuple-element.147.refs_0_), channel_id=1, source_target_pairs={{0,1},{1,0},{2,3},{3,2},{4,5},{5,4},{6,7},{7,6},{8,9},{9,8},{10,11... | collective-permute-start | bytes 393224 | tf_op jit(solution)/shard_map/ppermute | solution.py:21
  10.3 1.4 %collective-permute-start.7 = (bf16[128,512]{1,0:T(8,128)(2,1)S(1)}, bf16[128,512]{1,0:T(8,128)(2,1)S(1)}, u32[]{:S(2)}, u32[]{:S(2)}) collective-permute-start(bf16[128,512]{1,0:T(8,128)(2,1)S(1)} %collective-permute-done.4.refs_0_.refs_1_), channel_id=1, source_target_pairs={{0,1},{1,0},{2,3},{3,2},{4,5},{5,4},{6,7},{7,6},{8,9},{9,8},{10,11... | collective-permute-start | bytes 393224 | tf_op jit(solution)/shard_map/ppermute | solution.py:21
  11.5 1.4 %collective-permute-start.6 = (bf16[128,512]{1,0:T(8,128)(2,1)S(1)}, bf16[128,512]{1,0:T(8,128)(2,1)S(1)}, u32[]{:S(2)}, u32[]{:S(2)}) collective-permute-start(bf16[128,512]{1,0:T(8,128)(2,1)S(1)} %collective-permute-done.1.refs_0_.second), channel_id=1, source_target_pairs={{0,1},{1,0},{2,3},{3,2},{4,5},{5,4},{6,7},{7,6},{8,9},{9,8},{10,11... | collective-permute-start | bytes 393224 | tf_op jit(solution)/shard_map/ppermute | solution.py:21
  14.7 2.0 %collective-permute-start.8 = (bf16[128,512]{1,0:T(8,128)(2,1)S(1)}, bf16[128,512]{1,0:T(8,128)(2,1)S(1)}, u32[]{:S(2)}, u32[]{:S(2)}) collective-permute-start(bf16[128,512]{1,0:T(8,128)(2,1)S(1)} %collective-permute-done.refs_2_), channel_id=1, source_target_pairs={{0,1},{1,0},{2,3},{3,2},{4,5},{5,4},{6,7},{7,6},{8,9},{9,8},{10,11... | collective-permute-start | bytes 393224 | tf_op jit(solution)/shard_map/ppermute | solution.py:21
  15.0 1.5 %collective-permute-start.9 = (bf16[1056,128]{1,0:T(8,128)(2,1)S(1)}, bf16[1056,128]{1,0:T(8,128)(2,1)S(1)}, u32[]{:S(2)}, u32[]{:S(2)}) collective-permute-start(bf16[1056,128]{1,0:T(8,128)(2,1)S(1)} %get-tuple-element.125), channel_id=1, source_target_pairs={{0,1},{1,0},{2,3},{3,2},{4,5},{5,4},{6,7},{7,6},{8,9},{9,8},{10,11... | collective-permute-start | bytes 811016 | tf_op jit(solution)/shard_map/ppermute | solution.py:21
  16.7 6.5 %collective-permute-start.12 = (bf16[528,128]{1,0:T(8,128)(2,1)S(1)}, bf16[528,128]{1,0:T(8,128)(2,1)S(1)}, u32[]{:S(2)}, u32[]{:S(2)}) collective-permute-start(bf16[528,128]{1,0:T(8,128)(2,1)S(1)} %convert_element_type.17), channel_id=1, source_target_pairs={{0,2},{1,3},{2,0},{3,1},{4,6},{5,7},{6,4},{7,5},{8,10},{9,11},{10,... | collective-permute-start | bytes 405512 | tf_op jit(solution)/shard_map/ppermute | solution.py:21
  18.0 7.4 %collective-permute-start.10 = (bf16[528,128]{1,0:T(8,128)(2,1)S(1)}, bf16[528,128]{1,0:T(8,128)(2,1)S(1)}, u32[]{:S(2)}, u32[]{:S(2)}) collective-permute-start(bf16[528,128]{1,0:T(8,128)(2,1)S(1)} %convert_element_type.16), channel_id=1, source_target_pairs={{0,2},{1,3},{2,0},{3,1},{4,6},{5,7},{6,4},{7,5},{8,10},{9,11},{10,... | collective-permute-start | bytes 405512 | tf_op jit(solution)/shard_map/ppermute | solution.py:21
  23.3 2.3 %collective-permute-start.13 = (bf16[512,128]{1,0:T(8,128)(2,1)S(1)}, bf16[512,128]{1,0:T(8,128)(2,1)S(1)}, u32[]{:S(2)}, u32[]{:S(2)}) collective-permute-start(bf16[512,128]{1,0:T(8,128)(2,1)S(1)} %shard_map.100.refs_0_.second), channel_id=1, source_target_pairs={{0,1},{1,0},{2,3},{3,2},{4,5},{5,4},{6,7},{7,6},{8,9},{9,8},{10,11... | collective-permute-start | bytes 393224 | tf_op jit(solution)/shard_map/ppermute | solution.py:21
  25.5 1.4 %collective-permute-start.11 = (bf16[512,128]{1,0:T(8,128)(2,1)S(1)}, bf16[512,128]{1,0:T(8,128)(2,1)S(1)}, u32[]{:S(2)}, u32[]{:S(2)}) collective-permute-start(bf16[512,128]{1,0:T(8,128)(2,1)S(1)} %shard_map.98.refs_2_), channel_id=1, source_target_pairs={{0,1},{1,0},{2,3},{3,2},{4,5},{5,4},{6,7},{7,6},{8,9},{9,8},{10,11... | collective-permute-start | bytes 393224 | tf_op jit(solution)/shard_map/ppermute | solution.py:21
  28.5 1.6 %collective-permute-start.14 = (bf16[1056,128]{1,0:T(8,128)(2,1)S(1)}, bf16[1056,128]{1,0:T(8,128)(2,1)S(1)}, u32[]{:S(2)}, u32[]{:S(2)}) collective-permute-start(bf16[1056,128]{1,0:T(8,128)(2,1)S(1)} %get-tuple-element.168), channel_id=1, source_target_pairs={{0,1},{1,0},{2,3},{3,2},{4,5},{5,4},{6,7},{7,6},{8,9},{9,8},{10,11... | collective-permute-start | bytes 811016 | tf_op jit(solution)/shard_map/ppermute | solution.py:21
  30.2 5.8 %collective-permute-start.15 = (bf16[528,128]{1,0:T(8,128)(2,1)S(1)}, bf16[528,128]{1,0:T(8,128)(2,1)S(1)}, u32[]{:S(2)}, u32[]{:S(2)}) collective-permute-start(bf16[528,128]{1,0:T(8,128)(2,1)S(1)} %get-tuple-element.175), channel_id=1, source_target_pairs={{0,2},{1,3},{2,0},{3,1},{4,6},{5,7},{6,4},{7,5},{8,10},{9,11},{10,... | collective-permute-start | bytes 405512 | tf_op jit(solution)/shard_map/ppermute | solution.py:21

commit v4 on v3

--- a/solution.py
+++ b/solution.py
@@ -100,31 +100,22 @@
     return copies
 
 
-def pieces(source, target):
-    rows = target.shape[0]
-    step = min(PIECE, rows)
-    return [
-        (source.at[n : n + step, :], target.at[n : n + step, :]) for n in range(0, rows, step)
-    ]
-
-
-def half_rows(top, far, mine):
-    half = far.shape[0] // 2
-    side, _ = place(top)
-    return far.at[span(side if mine else 1 - side, half), :]
+def pieces(source, target, start, rows):
+    places = [pl.ds(pl.multiple_of(start + n, PIECE), PIECE) for n in range(0, rows, PIECE)]
+    return [(source.at[at, :], target.at[at, :]) for at in places]
 
 
 def norm_block(top, key, x_ref, router_row, gain_ref, router_ref, gate_w, up_w, total):
     gate, up, squares, logits = total
     feat = x_ref.shape[1]
-    at, rows = overall(top, key, feat), inside(top, key, feat)
+    at = overall(top, key, feat)
     x = x_ref[...].astype(F32)
     gained = (x * gain_ref[:, at]).astype(BF16)
     routed = x * router_ref[router_row : router_row + 1, at]
     for k in range(0, feat, LANES):
         squares = squares + x[:, k : k + LANES] * x[:, k : k + LANES]
         logits = logits + routed[:, k : k + LANES]
-    gate_now, up_now = mat(gained, gate_w[rows, :]), mat(gained, up_w[rows, :])
+    gate_now, up_now = mat(gained, gate_w[at, :]), mat(gained, up_w[at, :])
     if gate is None:
         return gate_now, up_now, squares, logits
     return gate + gate_now, up + up_now, squares, logits
@@ -136,47 +127,38 @@
 
 
 def own_kernel(top, router_row, *refs):
-    smalls, (gate_far, up_far, down_far), small_outs, nears, outs, sems = (
-        refs[:6], refs[6:9], refs[9:15], refs[15:20], refs[20:24], refs[24]
-    )
+    n = top - 1
+    xs, cots, refs = refs[:n], refs[n : 2 * n], refs[2 * n :]
+    smalls, weights, small_outs, nears, outs, sems = (
+        refs[:6], refs[6:9], refs[9:15], refs[15:18], refs[18:22], refs[22]
+    )
+    side, _ = place(top)
+    half = weights[0].shape[0] // 2
     copies = fetch(
         sems,
         [
             *zip(smalls, small_outs),
-            *pieces(half_rows(top, gate_far, True), nears[0]),
-            *pieces(half_rows(top, up_far, True), nears[1]),
-            *pieces(down_far, nears[2]),
-            *pieces(half_rows(top, gate_far, False), nears[3]),
-            *pieces(half_rows(top, up_far, False), nears[4]),
+            *pieces(weights[0], nears[0], side * half, half),
+            *pieces(weights[1], nears[1], side * half, half),
+            *pieces(weights[2], nears[2], 0, weights[2].shape[0]),
+            *pieces(weights[0], nears[0], (1 - side) * half, half),
+            *pieces(weights[1], nears[1], (1 - side) * half, half),
         ],
     )
-    ready = 6 + 2 * len(pieces(nears[0], nears[0]))
+    ready = 6 + 2 * (half // PIECE)
+    rest = ready + weights[2].shape[0] // PIECE
     for copy in copies[:ready]:
         copy.wait()
     x, cot, _, gain_ref, router_ref, _ = small_outs
-    total = norm_block(
-        top, 0, x, router_row, gain_ref, router_ref, *nears[:2], norm_start(x.shape[0])
-    )
+    total = norm_start(x.shape[0])
+    for key, part in enumerate((x, *xs)):
+        total = norm_block(top, key, part, router_row, gain_ref, router_ref, *nears[:2], total)
     outs[0][...], outs[1][...], outs[2][0], outs[2][1] = total
-    rest = ready + len(pieces(nears[2], nears[2]))
     for copy in copies[ready:rest]:
         copy.wait()
-    outs[3][...] = back_raw(top, (0,), (cot,), nears[2])
+    outs[3][...] = back_raw(top, range(top), (cot, *cots), nears[2])
     for copy in copies[rest:]:
         copy.wait()
-
-
-def near_kernel(top, router_row, *refs):
-    n = top - 1
-    xs, cots, weights, down_w, held, outs = (
-        refs[:n], refs[n : 2 * n], refs[2 * n : 2 * n + 4], refs[2 * n + 4],
-        refs[2 * n + 5 : 2 * n + 9], refs[2 * n + 9 :],
-    )
-    total = (held[0][...], held[1][...], held[2][0], held[2][1])
-    for key, x in enumerate(xs):
-        total = norm_block(top, key + 1, x, router_row, *weights, total)
-    outs[0][...], outs[1][...], outs[2][0], outs[2][1] = total
-    outs[3][...] = back_raw(top, range(1, top), cots, down_w, held[3][...])
 
 
 def write_factors(total, wide, outs):
@@ -211,15 +193,11 @@
 
 
 def factors_first_kernel(top, router_row, *refs):
-    xs, (gain_ref, router_ref), weights, outs = (
-        refs[: 2 * top], refs[2 * top : 2 * top + 2], refs[2 * top + 2 : 2 * top + 6],
-        refs[2 * top + 6 :],
-    )
+    xs, weights, outs = refs[: 2 * top], refs[2 * top : 2 * top + 4], refs[2 * top + 4 :]
     total = norm_start(xs[0].shape[0])
     for key, x in enumerate(xs):
-        gate_w, up_w = weights[:2] if key < top else weights[2:]
-        total = norm_block(top, key, x, router_row, gain_ref, router_ref, gate_w, up_w, total)
-    write_factors(total, gain_ref.shape[1], outs)
+        total = norm_block(top, key, x, router_row, *weights, total)
+    write_factors(total, weights[0].shape[1], outs)
 
 
 def back_raw(top, keys, parts, down_w, total=None):
@@ -241,11 +219,10 @@
     refs[n + 1][...] = back_sum(top, keys, refs[:n], refs[n])
 
 
-def write_terms(top, keys, gg, gu, sums, weights, outs):
-    for n, out_ref in enumerate(outs):
-        gate_w, up_w = weights[2 * (n // len(keys)) : 2 * (n // len(keys)) + 2]
+def write_terms(top, keys, gg, gu, sums, gate_w, up_w, outs):
+    for key, out_ref in zip(keys, outs):
         feat = out_ref.shape[0] - EXTRA
-        rows = inside(top, keys[n % len(keys)], feat)
+        rows = overall(top, key, feat)
         term = mat(gate_w[rows, :], gg) + mat(up_w[rows, :], gu)
         out_ref[0:feat, :] = term.astype(out_ref.dtype)
         out_ref[feat : feat + EXTRA, :] = sums.astype(out_ref.dtype)
@@ -260,8 +237,8 @@
     n = len(keys)
     parts, down_w = refs[:n], refs[n]
     held, grad_p, silu_p, act_p, dot_p = refs[n + 1 : n + 6]
-    weights, (gg_ref, gu_ref, sums_ref), outs = (
-        refs[n + 6 : n + 10], refs[n + 10 : n + 13], refs[n + 13 :]
+    (gate_w, up_w), (gg_ref, gu_ref, sums_ref), outs = (
+        refs[n + 6 : n + 8], refs[n + 8 : n + 11], refs[n + 11 :]
     )
     back = (back_raw if raw else back_sum)(top, keys, parts, down_w, held[...])
     gg = (back * grad_p[...]).astype(BF16)
@@ -275,12 +252,12 @@
     gu_ref[...] = gu
     sums_ref[...] = sums
     for key, out_ref in zip(range(1, top, 2), outs):
-        write_terms(top, (key,), gg, gu, sums, weights, double(out_ref))
-
-
-def kept_kernel(top, keys, gg_ref, gu_ref, sums_ref, *refs):
-    weights, outs = refs[:4], refs[4:]
-    write_terms(top, keys, gg_ref[...], gu_ref[...], sums_ref[...], weights, outs)
+        write_terms(top, (top + key, key), gg, gu, sums, gate_w, up_w, double(out_ref))
+
+
+def kept_kernel(top, keys, gg_ref, gu_ref, sums_ref, gate_w, up_w, *outs):
+    keys = [top + key for key in keys] + list(keys)
+    write_terms(top, keys, gg_ref[...], gu_ref[...], sums_ref[...], gate_w, up_w, outs)
 
 
 def row_factors(sums, rows, wide):
@@ -349,7 +326,7 @@
     def reduce(grads, blocks_sent):
         parts = kernel_call(
             functools.partial(kept_kernel, top, kept),
-            [VM((block, LANES), F32)] * (2 * len(kept)), *grads, *theirs, *mine,
+            [VM((block, LANES), F32)] * (2 * len(kept)), *grads, *gate_up,
             flops=8 * product,
         )
         blocks = dict(zip(kept, zip(parts[: len(kept)], parts[len(kept) :])))
@@ -371,53 +348,43 @@
         *grads, = kernel_call(
             functools.partial(back_kernel, top, keys, raw),
             grad_outs + [VM((2 * block, LANES), BF16)] * len(sent),
-            *parts, down, held, *factors, *theirs, *mine, flops=2 * product,
+            *parts, down, held, *factors, *gate_up, flops=2 * product,
         )
         return grads[:3], grads[3:]
 
     x2_cross = hop(hidden_second, top)
     cot_cross = hop(cotangent, top)
+    x1_cross = hop(hidden_first, top)
     x2_mine = spread(hidden_second, low)
     cot_mine = spread(cotangent, low)
     smalls = (
         hidden_second, cotangent, hidden_first, norm_gain.reshape(1, -1), router,
         depths.reshape(1, tokens),
     )
-    own_outs = partial_outs + [wide_units]
     outs = kernel_call(
         functools.partial(own_kernel, top, 1),
-        [VM(a.shape, a.dtype) for a in smalls]
-        + [row_half] * 2 + [VM(w_down.shape, BF16)] + [row_half] * 2 + own_outs,
-        *smalls, w_gate, w_up, w_down,
-        flops=3 * product // top, far=range(9),
-        scratch=semaphores(6 + 4 * -(-half // PIECE) + -(-units // PIECE)),
-    )
-    x2_own, cot_own, x1_own, gain, router, depths, gate_mine, up_mine, down = outs[:9]
-    gate_theirs, up_theirs, *partial = outs[9:]
-    x2_cross, *partial = lax.optimization_barrier((x2_cross, *partial))
+        [VM(a.shape, a.dtype) for a in (*smalls, w_gate, w_up, w_down)]
+        + partial_outs + [wide_units],
+        *x2_mine[1:], *cot_mine[1:], *smalls, w_gate, w_up, w_down,
+        flops=3 * product, far=range(2 * top - 2, 2 * top + 7),
+        scratch=semaphores(6 + 2 * (wide // PIECE) + units // PIECE),
+    )
+    x2_own, cot_own, x1_own, gain, router, depths, *gate_up, down = outs[:9]
+    *partial, back_mine = outs[9:]
+    x2_cross, cot_cross, back_mine = lax.optimization_barrier((x2_cross, cot_cross, back_mine))
     x2_theirs = spread(x2_cross, low)
-    x1_cross = hop(hidden_first, top)
-    x1_mine = spread(x1_own, low)
-    *partial, back_mine = kernel_call(
-        functools.partial(near_kernel, top, 1),
-        own_outs,
-        *x2_mine[1:], *cot_mine[1:], gain, router, gate_mine, up_mine, down, *partial,
-        flops=3 * product * (top - 1) // top,
-    )
-    mine, theirs = (gate_mine, up_mine), (gate_theirs, up_theirs)
-    cot_cross, back_mine, x1_mine = lax.optimization_barrier((cot_cross, back_mine, x1_mine))
     cot_theirs = spread(cot_cross, low)
     *factors2, rows2 = kernel_call(
         functools.partial(factors_second_kernel, top, 1),
-        factor_outs, *x2_theirs, gain, router, *theirs, *partial, flops=2 * product,
+        factor_outs, *x2_theirs, gain, router, *gate_up, *partial, flops=2 * product,
     )
 
     grads, blocks_sent = back_call(across, True, cot_theirs, back_mine, factors2)
     x1_cross, *grads = lax.optimization_barrier((x1_cross, *grads))
-    x1_theirs = spread(x1_cross, low)
+    x1_mine, x1_theirs = spread(x1_own, low), spread(x1_cross, low)
     chip_theirs, chip_mine = reduce(grads, blocks_sent)
-    x1_theirs, chip_theirs, chip_mine = lax.optimization_barrier(
-        (x1_theirs, chip_theirs, chip_mine)
+    x1_mine, x1_theirs, chip_theirs, chip_mine = lax.optimization_barrier(
+        (x1_mine, x1_theirs, chip_theirs, chip_mine)
     )
     got_mine = hop(chip_theirs.astype(BF16), top)
 
@@ -433,7 +400,7 @@
     x1_parts = (*x1_mine, *x1_theirs)
     *factors1, rows1 = kernel_call(
         functools.partial(factors_first_kernel, top, 0),
-        factor_outs, *x1_parts, gain, router, *mine, *theirs, flops=4 * product,
+        factor_outs, *x1_parts, gain, router, *gate_up, flops=4 * product,
     )
 
     def second(chip, got, cot, columns):

time: 36.9 us -> 38.3 us (1.038)
  waiting for transfers between devices: 9.44 us -> 10.6 us
  starting transfers between devices: 9.8 us -> 10.6 us
  Pallas kernels: 17.1 us -> 16.4 us
    ppermute x16, waiting for transfers between devices: 9.44 us -> 10.6 us  [hop(): return lax.ppermute(value, 'tensor', [(j, j ^ bit) for j in range(size)])]
    ppermute x16, starting transfers between devices: 9.8 us -> 10.6 us  [hop(): return lax.ppermute(value, 'tensor', [(j, j ^ bit) for j in range(size)])]
    pallas_call x15 -> x14, Pallas kernels: 17.1 us -> 16.4 us  [kernel_call(): pl.pallas_call(kernel, out_shape=list(outs) if many else outs, in_specs=[...]
  transfers between devices with their start and end apart: 16 -> 16, of which waited for: 7 -> 7; matrix products, arithmetic and copies ran while one was open for 0% -> 0% of each run, Pallas kernels for 40% -> 37%
where the time goes in v4:
time: 38.3 us; the launch traced here: 38.2 us
  Pallas kernels  16.4 us (43%)
  starting transfers between devices  10.6 us (28%)
  waiting for transfers between devices  10.6 us (28%)
    pallas_call x14, Pallas kernels, kernel_call(): pl.pallas_call(kernel, out_shape=list(outs) if many else outs, in_specs=[...  16.4 us
    ppermute x16, waiting for transfers between devices, hop(): return lax.ppermute(value, 'tensor', [(j, j ^ bit) for j in range(size)])  10.6 us
    ppermute x16, starting transfers between devices, hop(): return lax.ppermute(value, 'tensor', [(j, j ^ bit) for j in range(size)])  10.6 us
  transfers between devices with their start and end apart: 16, of which 7 were waited for; matrix products, arithmetic and copies ran while one was open for 0% of the time, Pallas kernels for 37%

profile of v4, /device:TPU:0, one launch (start us, length us, event | category | flops | bytes accessed | tf_op | source)
XLA Modules:
  0.0 38.2 jit_solution(16810484239611499269)
XLA Ops:
  0.0 0.5 %collective-permute-start = (bf16[128,512]{1,0:T(8,128)(2,1)}, bf16[128,512]{1,0:T(8,128)(2,1)S(1)}, u32[]{:S(2)}, u32[]{:S(2)}) collective-permute-start(bf16[128,512]{1,0:T(8,128)(2,1)} %refs_2_.1), channel_id=1, source_target_pairs={{0,1},{1,0},{2,3},{3,2},{4,5},{5,4},{6,7},{7,6},{8,9},{9,8},{10,11... | collective-permute-start | bytes 393224 | tf_op jit(solution)/shard_map/ppermute | solution.py:21
  0.5 3.0 %collective-permute-start.4 = (bf16[128,512]{1,0:T(8,128)(2,1)}, bf16[128,512]{1,0:T(8,128)(2,1)S(1)}, u32[]{:S(2)}, u32[]{:S(2)}) collective-permute-start(bf16[128,512]{1,0:T(8,128)(2,1)} %refs_2_.1), channel_id=1, source_target_pairs={{0,2},{1,3},{2,0},{3,1},{4,6},{5,7},{6,4},{7,5},{8,10},{9,11},{10,... | collective-permute-start | bytes 393224 | tf_op jit(solution)/shard_map/ppermute | solution.py:21
  3.5 5.1 %shard_map.91 = (bf16[128,512]{1,0:T(8,128)(2,1)S(1)}, bf16[128,512]{1,0:T(8,128)(2,1)S(1)}, bf16[128,512]{1,0:T(8,128)(2,1)S(1)}, f32[1,2048]{1,0:T(1,128)S(1)}...) custom-call(bf16[128,512]{1,0:T(8,128)(2,1)S(1)} %collective-permute, ...), custom_call_target="tpu_custom_call" | custom-call | flops 4831838208 | tf_op jit(solution)/shard_map/pallas_call | solution.py:44
  8.6 1.5 %collective-permute-done.5.refs_0_.second = bf16[128,512]{1,0:T(8,128)(2,1)S(1)} collective-permute-done((bf16[128,512]{1,0:T(8,128)(2,1)}, bf16[128,512]{1,0:T(8,128)(2,1)S(1)}, u32[]{:S(2)}, u32[]{:S(2)}) %collective-permute-start.5) | collective-permute-done | bytes 131104 | tf_op jit(solution)/shard_map/ppermute | solution.py:21
  10.2 1.7 %collective-permute-start.3 = (bf16[128,512]{1,0:T(8,128)(2,1)S(1)}, bf16[128,512]{1,0:T(8,128)(2,1)S(1)}, u32[]{:S(2)}, u32[]{:S(2)}) collective-permute-start(bf16[128,512]{1,0:T(8,128)(2,1)S(1)} %copy-done), channel_id=1, source_target_pairs={{0,2},{1,3},{2,0},{3,1},{4,6},{5,7},{6,4},{7,5},{8,10},{9,11},{10,... | collective-permute-start | bytes 393224 | tf_op jit(solution)/shard_map/ppermute | solution.py:21
  11.9 0.2 collective-permute-start.6
  12.1 0.3 collective-permute-start.2
  12.4 1.1 %shard_map.92 = (f32[1024,128]{1,0:T(8,128)S(1)}, f32[1024,128]{1,0:T(8,128)S(1)}, f32[1024,128]{1,0:T(8,128)S(1)}, f32[1024,128]{1,0:T(8,128)S(1)}, f32[8,128]{1,0:T(8,128)S(1)}) custom-call(bf16[128,512]{1,0:T(8,128)(2,1)S(1)} %collective-permute-done.4.refs_0_.refs_1_, bf16[128,512]{1,0:T(8,128)(2,1)S(1)} %collective-permute-done.7.refs_1_, ...), custom_call_target="tpu_custom_call" | custom-call | flops 3221225472 | tf_op jit(solution)/shard_map/pallas_call | solution.py:44
  13.6 1.8 %shard_map.93 = (bf16[1024,128]{1,0:T(8,128)(2,1)S(1)}, bf16[1024,128]{1,0:T(8,128)(2,1)S(1)}, f32[16,128]{1,0:T(8,128)S(1)}, bf16[1056,128]{1,0:T(8,128)(2,1)S(1)}) custom-call(bf16[128,512]{1,0:T(8,128)(2,1)S(1)} %collective-permute-done.5.refs_0_.second, bf16[128,512]{1,0:T(8,128)(2,1)S(1)} %collective-permute-done.6.refs_1_, ...), custom_call_target="tpu_custom_call" | custom-call | flops 3221225472 | tf_op jit(solution)/shard_map/pallas_call | solution.py:44
  15.4 0.7 %collective-permute-done.3.refs_2_ = bf16[128,512]{1,0:T(8,128)(2,1)S(1)} collective-permute-done((bf16[128,512]{1,0:T(8,128)(2,1)S(1)}, bf16[128,512]{1,0:T(8,128)(2,1)S(1)}, u32[]{:S(2)}, u32[]{:S(2)}) %collective-permute-start.3) | collective-permute-done | bytes 131104 | tf_op jit(solution)/shard_map/ppermute | solution.py:21
  16.1 0.5 %collective-permute-start.9 = (bf16[1056,128]{1,0:T(8,128)(2,1)S(1)}, bf16[1056,128]{1,0:T(8,128)(2,1)S(1)}, u32[]{:S(2)}, u32[]{:S(2)}) collective-permute-start(bf16[1056,128]{1,0:T(8,128)(2,1)S(1)} %get-tuple-element.105), channel_id=1, source_target_pairs={{0,1},{1,0},{2,3},{3,2},{4,5},{5,4},{6,7},{7,6},{8,9},{9,8},{10,11... | collective-permute-start | bytes 811016 | tf_op jit(solution)/shard_map/ppermute | solution.py:21
  16.6 1.2 %shard_map.94 = (f32[528,128]{1,0:T(8,128)S(1)}, f32[528,128]{1,0:T(8,128)S(1)}) custom-call(bf16[1024,128]{1,0:T(8,128)(2,1)S(1)} %get-tuple-element.101.gg_ref, bf16[1024,128]{1,0:T(8,128)(2,1)S(1)} %get-tuple-element.102.gu_ref, f32[16,128]{1,0:T(8,128)S(1)} %get-tuple-element.103.sums_ref, ...), custom_call_target="tpu_custom_call" | custom-call | flops 12884901888 | tf_op jit(solution)/shard_map/pallas_call | solution.py:44
  18.0 1.8 %collective-permute-start.12 = (bf16[528,128]{1,0:T(8,128)(2,1)S(1)}, bf16[528,128]{1,0:T(8,128)(2,1)S(1)}, u32[]{:S(2)}, u32[]{:S(2)}) collective-permute-start(bf16[528,128]{1,0:T(8,128)(2,1)S(1)} %convert_element_type.17), channel_id=1, source_target_pairs={{0,2},{1,3},{2,0},{3,1},{4,6},{5,7},{6,4},{7,5},{8,10},{9,11},{10,... | collective-permute-start | bytes 405512 | tf_op jit(solution)/shard_map/ppermute | solution.py:21
  19.8 0.4 %shard_map.95 = (f32[512,128]{1,0:T(8,128)S(1)}, f32[512,128]{1,0:T(8,128)S(1)}, f32[512,128]{1,0:T(8,128)S(1)}, f32[512,128]{1,0:T(8,128)S(1)}, f32[512,128]{1,0:T(8,128)S(1)}, /*index=5*/f32[512,128]{1,0:T(8,128)S(1)}) custom-call(bf16[128,512]{1,0:T(8,128)(2,1)S(1)} %get-tuple-element.108.refs_0_, ...), custom_call_target="tpu_custom_call" | custom-call | tf_op jit(solution)/shard_map/pallas_call | solution.py:44
  20.3 0.3 collective-permute-start.10
  20.6 1.6 %shard_map.98 = (f32[1024,128]{1,0:T(8,128)S(1)}, f32[1024,128]{1,0:T(8,128)S(1)}, f32[1024,128]{1,0:T(8,128)S(1)}, f32[1024,128]{1,0:T(8,128)S(1)}, f32[8,128]{1,0:T(8,128)S(1)}) custom-call(bf16[128,512]{1,0:T(8,128)(2,1)S(1)} %get-tuple-element.127.refs_0_, bf16[128,512]{1,0:T(8,128)(2,1)S(1)} %collective-permute-done.2.refs_1_, ...), custom_call_target="tpu_custom_call" | custom-call | flops 6442450944 | tf_op jit(solution)/shard_map/pallas_call | solution.py:44
  22.3 0.1 shard_map.96
  22.4 2.1 %collective-permute-done.12.got = bf16[528,128]{1,0:T(8,128)(2,1)S(1)} collective-permute-done((bf16[528,128]{1,0:T(8,128)(2,1)S(1)}, bf16[528,128]{1,0:T(8,128)(2,1)S(1)}, u32[]{:S(2)}, u32[]{:S(2)}) %collective-permute-start.12) | collective-permute-done | bytes 135200 | tf_op jit(solution)/shard_map/ppermute | solution.py:21
  24.5 0.1 shard_map.99.refs_0_.second
  24.7 2.1 %collective-permute-done.10.got = bf16[528,128]{1,0:T(8,128)(2,1)S(1)} collective-permute-done((bf16[528,128]{1,0:T(8,128)(2,1)S(1)}, bf16[528,128]{1,0:T(8,128)(2,1)S(1)}, u32[]{:S(2)}, u32[]{:S(2)}) %collective-permute-start.10) | collective-permute-done | bytes 135200 | tf_op jit(solution)/shard_map/ppermute | solution.py:21
  26.8 0.1 shard_map.97.refs_2_
  27.0 1.0 %shard_map.100.refs_2_ = f32[1024,128]{1,0:T(8,128)S(1)} custom-call(bf16[512,128]{1,0:T(8,128)(2,1)S(1)} %shard_map.99.refs_0_.second, bf16[512,128]{1,0:T(8,128)(2,1)S(1)} %collective-permute-done.13.refs_1_, bf16[512,128]{1,0:T(8,128)(2,1)S(1)} %shard_map.97.refs_2_, bf16[1024,2048]{1,0:T(8,128)(2,1)S(1)} %get-tuple-element.83.refs_2_.refs_3_.refs_1_), custom_call_target="tpu_custom_call" | custom-call | flops 1610612736 | tf_op jit(solution)/shard_map/pallas_call | solution.py:44
  27.9 0.3 collective-permute-done.11.refs_0_
  28.3 1.5 %shard_map.101 = (bf16[1024,128]{1,0:T(8,128)(2,1)S(1)}, bf16[1024,128]{1,0:T(8,128)(2,1)S(1)}, f32[16,128]{1,0:T(8,128)S(1)}, bf16[1056,128]{1,0:T(8,128)(2,1)S(1)}) custom-call(bf16[512,128]{1,0:T(8,128)(2,1)S(1)} %collective-permute-done.11.refs_0_, bf16[1024,2048]{1,0:T(8,128)(2,1)S(1)} %get-tuple-element.83.refs_2_.refs_3_.refs_1_, ...), custom_call_target="tpu_custom_call" | custom-call | flops 3221225472 | tf_op jit(solution)/shard_map/pallas_call | solution.py:44
  29.8 0.2 collective-permute-start.14
  30.1 1.2 %shard_map.102 = (f32[528,128]{1,0:T(8,128)S(1)}, f32[528,128]{1,0:T(8,128)S(1)}) custom-call(bf16[1024,128]{1,0:T(8,128)(2,1)S(1)} %get-tuple-element.144.gg_ref, bf16[1024,128]{1,0:T(8,128)(2,1)S(1)} %get-tuple-element.145.gu_ref, f32[16,128]{1,0:T(8,128)S(1)} %get-tuple-element.146.sums_ref, ...), custom_call_target="tpu_custom_call" | custom-call | flops 12884901888 | tf_op jit(solution)/shard_map/pallas_call | solution.py:44
  31.3 0.1 collective-permute-done.14
  31.5 0.1 fusion
  31.6 1.8 %collective-permute-start.15 = (bf16[528,128]{1,0:T(8,128)(2,1)S(1)}, bf16[528,128]{1,0:T(8,128)(2,1)S(1)}, u32[]{:S(2)}, u32[]{:S(2)}) collective-permute-start(bf16[528,128]{1,0:T(8,128)(2,1)S(1)} %get-tuple-element.155), channel_id=1, source_target_pairs={{0,2},{1,3},{2,0},{3,1},{4,6},{5,7},{6,4},{7,5},{8,10},{9,11},{10,... | collective-permute-start | bytes 405512 | tf_op jit(solution)/shard_map/ppermute | solution.py:21
  33.4 0.2 shard_map.103
  33.6 3.7 %collective-permute-done.15.got = bf16[528,128]{1,0:T(8,128)(2,1)S(1)} collective-permute-done((bf16[528,128]{1,0:T(8,128)(2,1)S(1)}, bf16[528,128]{1,0:T(8,128)(2,1)S(1)}, u32[]{:S(2)}, u32[]{:S(2)}) %collective-permute-start.15) | collective-permute-done | bytes 135200 | tf_op jit(solution)/shard_map/ppermute | solution.py:21
  37.3 0.8 %shard_map.104 = bf16[128,512]{1,0:T(8,128)(2,1)} custom-call(f32[528,128]{1,0:T(8,128)S(1)} %get-tuple-element.156.chip, bf16[528,128]{1,0:T(8,128)(2,1)S(1)} %collective-permute-done.15.got, bf16[512,128]{1,0:T(8,128)(2,1)S(1)} %shard_map.99.refs_0_.second, f32[512,128]{1,0:T(8,128)S(1)} %get-tuple-element.152.x, f32[512,128]{1,0:T(8,128)S(1)} %get-tuple-element.153.scale, ...), custom_call_target="tpu_custom_call" | custom-call | tf_op jit(solution)/shard_map/pallas_call | solution.py:44
  (22 shorter events, 0.5 us)
Async XLA Ops:
  0.0 3.5 %collective-permute-start = (bf16[128,512]{1,0:T(8,128)(2,1)}, bf16[128,512]{1,0:T(8,128)(2,1)S(1)}, u32[]{:S(2)}, u32[]{:S(2)}) collective-permute-start(bf16[128,512]{1,0:T(8,128)(2,1)} %refs_2_.1), channel_id=1, source_target_pairs={{0,1},{1,0},{2,3},{3,2},{4,5},{5,4},{6,7},{7,6},{8,9},{9,8},{10,11... | collective-permute-start | bytes 393224 | tf_op jit(solution)/shard_map/ppermute | solution.py:21
  0.5 3.1 %collective-permute-start.1 = (bf16[128,512]{1,0:T(8,128)(2,1)}, bf16[128,512]{1,0:T(8,128)(2,1)S(1)}, u32[]{:S(2)}, u32[]{:S(2)}) collective-permute-start(bf16[128,512]{1,0:T(8,128)(2,1)} %refs_3_.1), channel_id=1, source_target_pairs={{0,1},{1,0},{2,3},{3,2},{4,5},{5,4},{6,7},{7,6},{8,9},{9,8},{10,11... | collective-permute-start | bytes 393224 | tf_op jit(solution)/shard_map/ppermute | solution.py:21
  0.5 8.1 %collective-permute-start.4 = (bf16[128,512]{1,0:T(8,128)(2,1)}, bf16[128,512]{1,0:T(8,128)(2,1)S(1)}, u32[]{:S(2)}, u32[]{:S(2)}) collective-permute-start(bf16[128,512]{1,0:T(8,128)(2,1)} %refs_2_.1), channel_id=1, source_target_pairs={{0,2},{1,3},{2,0},{3,1},{4,6},{5,7},{6,4},{7,5},{8,10},{9,11},{10,... | collective-permute-start | bytes 393224 | tf_op jit(solution)/shard_map/ppermute | solution.py:21
  3.5 6.7 %collective-permute-start.5 = (bf16[128,512]{1,0:T(8,128)(2,1)}, bf16[128,512]{1,0:T(8,128)(2,1)S(1)}, u32[]{:S(2)}, u32[]{:S(2)}) collective-permute-start(bf16[128,512]{1,0:T(8,128)(2,1)} %refs_3_.1), channel_id=1, source_target_pairs={{0,2},{1,3},{2,0},{3,1},{4,6},{5,7},{6,4},{7,5},{8,10},{9,11},{10,... | collective-permute-start | bytes 393224 | tf_op jit(solution)/shard_map/ppermute | solution.py:21
  3.5 6.6 %copy-start = (bf16[128,512]{1,0:T(8,128)(2,1)S(1)}, bf16[128,512]{1,0:T(8,128)(2,1)}, u32[]{:S(2)}) copy-start(bf16[128,512]{1,0:T(8,128)(2,1)} %refs_4_.1) | copy-start | bytes 393220
  10.2 2.3 %collective-permute-start.7 = (bf16[128,512]{1,0:T(8,128)(2,1)S(1)}, bf16[128,512]{1,0:T(8,128)(2,1)S(1)}, u32[]{:S(2)}, u32[]{:S(2)}) collective-permute-start(bf16[128,512]{1,0:T(8,128)(2,1)S(1)} %collective-permute-done.4.refs_0_.refs_1_), channel_id=1, source_target_pairs={{0,1},{1,0},{2,3},{3,2},{4,5},{5,4},{6,7},{7,6},{8,9},{9,8},{10,11... | collective-permute-start | bytes 393224 | tf_op jit(solution)/shard_map/ppermute | solution.py:21
  10.2 5.9 %collective-permute-start.3 = (bf16[128,512]{1,0:T(8,128)(2,1)S(1)}, bf16[128,512]{1,0:T(8,128)(2,1)S(1)}, u32[]{:S(2)}, u32[]{:S(2)}) collective-permute-start(bf16[128,512]{1,0:T(8,128)(2,1)S(1)} %copy-done), channel_id=1, source_target_pairs={{0,2},{1,3},{2,0},{3,1},{4,6},{5,7},{6,4},{7,5},{8,10},{9,11},{10,... | collective-permute-start | bytes 393224 | tf_op jit(solution)/shard_map/ppermute | solution.py:21
  11.9 1.6 %collective-permute-start.6 = (bf16[128,512]{1,0:T(8,128)(2,1)S(1)}, bf16[128,512]{1,0:T(8,128)(2,1)S(1)}, u32[]{:S(2)}, u32[]{:S(2)}) collective-permute-start(bf16[128,512]{1,0:T(8,128)(2,1)S(1)} %collective-permute-done.5.refs_0_.second), channel_id=1, source_target_pairs={{0,1},{1,0},{2,3},{3,2},{4,5},{5,4},{6,7},{7,6},{8,9},{9,8},{10,11... | collective-permute-start | bytes 393224 | tf_op jit(solution)/shard_map/ppermute | solution.py:21
  12.1 5.8 %collective-permute-start.2 = (bf16[128,512]{1,0:T(8,128)(2,1)S(1)}, bf16[128,512]{1,0:T(8,128)(2,1)S(1)}, u32[]{:S(2)}, u32[]{:S(2)}) collective-permute-start(bf16[128,512]{1,0:T(8,128)(2,1)S(1)} %get-tuple-element.127.refs_0_), channel_id=1, source_target_pairs={{0,1},{1,0},{2,3},{3,2},{4,5},{5,4},{6,7},{7,6},{8,9},{9,8},{10,11... | collective-permute-start | bytes 393224 | tf_op jit(solution)/shard_map/ppermute | solution.py:21
  16.1 1.9 %collective-permute-start.8 = (bf16[128,512]{1,0:T(8,128)(2,1)S(1)}, bf16[128,512]{1,0:T(8,128)(2,1)S(1)}, u32[]{:S(2)}, u32[]{:S(2)}) collective-permute-start(bf16[128,512]{1,0:T(8,128)(2,1)S(1)} %collective-permute-done.3.refs_2_), channel_id=1, source_target_pairs={{0,1},{1,0},{2,3},{3,2},{4,5},{5,4},{6,7},{7,6},{8,9},{9,8},{10,11... | collective-permute-start | bytes 393224 | tf_op jit(solution)/shard_map/ppermute | solution.py:21
  16.1 1.8 %collective-permute-start.9 = (bf16[1056,128]{1,0:T(8,128)(2,1)S(1)}, bf16[1056,128]{1,0:T(8,128)(2,1)S(1)}, u32[]{:S(2)}, u32[]{:S(2)}) collective-permute-start(bf16[1056,128]{1,0:T(8,128)(2,1)S(1)} %get-tuple-element.105), channel_id=1, source_target_pairs={{0,1},{1,0},{2,3},{3,2},{4,5},{5,4},{6,7},{7,6},{8,9},{9,8},{10,11... | collective-permute-start | bytes 811016 | tf_op jit(solution)/shard_map/ppermute | solution.py:21
  18.0 6.5 %collective-permute-start.12 = (bf16[528,128]{1,0:T(8,128)(2,1)S(1)}, bf16[528,128]{1,0:T(8,128)(2,1)S(1)}, u32[]{:S(2)}, u32[]{:S(2)}) collective-permute-start(bf16[528,128]{1,0:T(8,128)(2,1)S(1)} %convert_element_type.17), channel_id=1, source_target_pairs={{0,2},{1,3},{2,0},{3,1},{4,6},{5,7},{6,4},{7,5},{8,10},{9,11},{10,... | collective-permute-start | bytes 405512 | tf_op jit(solution)/shard_map/ppermute | solution.py:21
  20.3 6.5 %collective-permute-start.10 = (bf16[528,128]{1,0:T(8,128)(2,1)S(1)}, bf16[528,128]{1,0:T(8,128)(2,1)S(1)}, u32[]{:S(2)}, u32[]{:S(2)}) collective-permute-start(bf16[528,128]{1,0:T(8,128)(2,1)S(1)} %convert_element_type.16), channel_id=1, source_target_pairs={{0,2},{1,3},{2,0},{3,1},{4,6},{5,7},{6,4},{7,5},{8,10},{9,11},{10,... | collective-permute-start | bytes 405512 | tf_op jit(solution)/shard_map/ppermute | solution.py:21
  24.6 2.4 %collective-permute-start.13 = (bf16[512,128]{1,0:T(8,128)(2,1)S(1)}, bf16[512,128]{1,0:T(8,128)(2,1)S(1)}, u32[]{:S(2)}, u32[]{:S(2)}) collective-permute-start(bf16[512,128]{1,0:T(8,128)(2,1)S(1)} %shard_map.99.refs_0_.second), channel_id=1, source_target_pairs={{0,1},{1,0},{2,3},{3,2},{4,5},{5,4},{6,7},{7,6},{8,9},{9,8},{10,11... | collective-permute-start | bytes 393224 | tf_op jit(solution)/shard_map/ppermute | solution.py:21
  26.9 1.4 %collective-permute-start.11 = (bf16[512,128]{1,0:T(8,128)(2,1)S(1)}, bf16[512,128]{1,0:T(8,128)(2,1)S(1)}, u32[]{:S(2)}, u32[]{:S(2)}) collective-permute-start(bf16[512,128]{1,0:T(8,128)(2,1)S(1)} %shard_map.97.refs_2_), channel_id=1, source_target_pairs={{0,1},{1,0},{2,3},{3,2},{4,5},{5,4},{6,7},{7,6},{8,9},{9,8},{10,11... | collective-permute-start | bytes 393224 | tf_op jit(solution)/shard_map/ppermute | solution.py:21
  29.8 1.6 %collective-permute-start.14 = (bf16[1056,128]{1,0:T(8,128)(2,1)S(1)}, bf16[1056,128]{1,0:T(8,128)(2,1)S(1)}, u32[]{:S(2)}, u32[]{:S(2)}) collective-permute-start(bf16[1056,128]{1,0:T(8,128)(2,1)S(1)} %get-tuple-element.148), channel_id=1, source_target_pairs={{0,1},{1,0},{2,3},{3,2},{4,5},{5,4},{6,7},{7,6},{8,9},{9,8},{10,11... | collective-permute-start | bytes 811016 | tf_op jit(solution)/shard_map/ppermute | solution.py:21
  31.6 5.8 %collective-permute-start.15 = (bf16[528,128]{1,0:T(8,128)(2,1)S(1)}, bf16[528,128]{1,0:T(8,128)(2,1)S(1)}, u32[]{:S(2)}, u32[]{:S(2)}) collective-permute-start(bf16[528,128]{1,0:T(8,128)(2,1)S(1)} %get-tuple-element.155), channel_id=1, source_target_pairs={{0,2},{1,3},{2,0},{3,1},{4,6},{5,7},{6,4},{7,5},{8,10},{9,11},{10,... | collective-permute-start | bytes 405512 | tf_op jit(solution)/shard_map/ppermute | solution.py:21

commit v5 on v4

--- a/solution.py
+++ b/solution.py
@@ -354,7 +354,6 @@
 
     x2_cross = hop(hidden_second, top)
     cot_cross = hop(cotangent, top)
-    x1_cross = hop(hidden_first, top)
     x2_mine = spread(hidden_second, low)
     cot_mine = spread(cotangent, low)
     smalls = (
@@ -371,9 +370,10 @@
     )
     x2_own, cot_own, x1_own, gain, router, depths, *gate_up, down = outs[:9]
     *partial, back_mine = outs[9:]
-    x2_cross, cot_cross, back_mine = lax.optimization_barrier((x2_cross, cot_cross, back_mine))
+    x2_cross, back_mine = lax.optimization_barrier((x2_cross, back_mine))
     x2_theirs = spread(x2_cross, low)
-    cot_theirs = spread(cot_cross, low)
+    x1_cross = hop(x1_own, top)
+    cot_theirs = spread(after(cot_cross, back_mine), low)
     *factors2, rows2 = kernel_call(
         functools.partial(factors_second_kernel, top, 1),
         factor_outs, *x2_theirs, gain, router, *gate_up, *partial, flops=2 * product,

time: 38.3 us -> 37 us (0.966)
  waiting for transfers between devices: 10.6 us -> 9.04 us
  starting transfers between devices: 10.6 us -> 11 us
    ppermute x16, waiting for transfers between devices: 10.6 us -> 9.04 us  [hop(): return lax.ppermute(value, 'tensor', [(j, j ^ bit) for j in range(size)])]
    ppermute x16, starting transfers between devices: 10.6 us -> 11 us  [hop(): return lax.ppermute(value, 'tensor', [(j, j ^ bit) for j in range(size)])]
  transfers between devices with their start and end apart: 16 -> 16, of which waited for: 7 -> 6; matrix products, arithmetic and copies ran while one was open for 0% -> 0% of each run, Pallas kernels for 37% -> 38%
where the time goes in v5:
time: 37 us; the launch traced here: 36.9 us
  Pallas kernels  16.4 us (44%)
  starting transfers between devices  11 us (30%)
  waiting for transfers between devices  9.04 us (24%)
    pallas_call x14, Pallas kernels, kernel_call(): pl.pallas_call(kernel, out_shape=list(outs) if many else outs, in_specs=[...  16.4 us
    ppermute x16, starting transfers between devices, hop(): return lax.ppermute(value, 'tensor', [(j, j ^ bit) for j in range(size)])  11 us
    ppermute x16, waiting for transfers between devices, hop(): return lax.ppermute(value, 'tensor', [(j, j ^ bit) for j in range(size)])  9.04 us
  transfers between devices with their start and end apart: 16, of which 6 were waited for; matrix products, arithmetic and copies ran while one was open for 0% of the time, Pallas kernels for 38%

profile of v5, /device:TPU:0, one launch (start us, length us, event | category | flops | bytes accessed | tf_op | source)
XLA Modules:
  0.0 36.9 jit_solution(14672068282158098473)
XLA Ops:
  0.0 0.5 %collective-permute-start = (bf16[128,512]{1,0:T(8,128)(2,1)}, bf16[128,512]{1,0:T(8,128)(2,1)S(1)}, u32[]{:S(2)}, u32[]{:S(2)}) collective-permute-start(bf16[128,512]{1,0:T(8,128)(2,1)} %refs_2_.1), channel_id=1, source_target_pairs={{0,1},{1,0},{2,3},{3,2},{4,5},{5,4},{6,7},{7,6},{8,9},{9,8},{10,11... | collective-permute-start | bytes 393224 | tf_op jit(solution)/shard_map/ppermute | solution.py:21
  0.5 3.0 %collective-permute-start.5 = (bf16[128,512]{1,0:T(8,128)(2,1)}, bf16[128,512]{1,0:T(8,128)(2,1)S(1)}, u32[]{:S(2)}, u32[]{:S(2)}) collective-permute-start(bf16[128,512]{1,0:T(8,128)(2,1)} %refs_2_.1), channel_id=1, source_target_pairs={{0,2},{1,3},{2,0},{3,1},{4,6},{5,7},{6,4},{7,5},{8,10},{9,11},{10,... | collective-permute-start | bytes 393224 | tf_op jit(solution)/shard_map/ppermute | solution.py:21
  3.5 5.0 %shard_map.91 = (bf16[128,512]{1,0:T(8,128)(2,1)S(1)}, bf16[128,512]{1,0:T(8,128)(2,1)S(1)}, bf16[128,512]{1,0:T(8,128)(2,1)S(1)}, f32[1,2048]{1,0:T(1,128)S(1)}...) custom-call(bf16[128,512]{1,0:T(8,128)(2,1)S(1)} %collective-permute, ...), custom_call_target="tpu_custom_call" | custom-call | flops 4831838208 | tf_op jit(solution)/shard_map/pallas_call | solution.py:44
  8.7 2.1 %collective-permute-start.3 = (bf16[128,512]{1,0:T(8,128)(2,1)S(1)}, bf16[128,512]{1,0:T(8,128)(2,1)S(1)}, u32[]{:S(2)}, u32[]{:S(2)}) collective-permute-start(bf16[128,512]{1,0:T(8,128)(2,1)S(1)} %get-tuple-element.127.refs_0_), channel_id=1, source_target_pairs={{0,2},{1,3},{2,0},{3,1},{4,6},{5,7},{6,4},{7,5},{8,10},{9,11},{10,... | collective-permute-start | bytes 393224 | tf_op jit(solution)/shard_map/ppermute | solution.py:21
  10.7 0.2 collective-permute-start.2
  10.9 0.3 collective-permute-start.6
  11.2 1.1 %shard_map.92 = (f32[1024,128]{1,0:T(8,128)S(1)}, f32[1024,128]{1,0:T(8,128)S(1)}, f32[1024,128]{1,0:T(8,128)S(1)}, f32[1024,128]{1,0:T(8,128)S(1)}, f32[8,128]{1,0:T(8,128)S(1)}) custom-call(bf16[128,512]{1,0:T(8,128)(2,1)S(1)} %collective-permute-done.5.refs_0_.refs_1_, bf16[128,512]{1,0:T(8,128)(2,1)S(1)} %collective-permute-done.7.refs_1_, ...), custom_call_target="tpu_custom_call" | custom-call | flops 3221225472 | tf_op jit(solution)/shard_map/pallas_call | solution.py:44
  12.4 1.8 %shard_map.93 = (bf16[1024,128]{1,0:T(8,128)(2,1)S(1)}, bf16[1024,128]{1,0:T(8,128)(2,1)S(1)}, f32[16,128]{1,0:T(8,128)S(1)}, bf16[1056,128]{1,0:T(8,128)(2,1)S(1)}) custom-call(bf16[128,512]{1,0:T(8,128)(2,1)S(1)} %collective-permute-done.4.refs_0_.second, bf16[128,512]{1,0:T(8,128)(2,1)S(1)} %collective-permute-done.6.refs_1_, ...), custom_call_target="tpu_custom_call" | custom-call | flops 3221225472 | tf_op jit(solution)/shard_map/pallas_call | solution.py:44
  14.2 0.6 %collective-permute-done.3.refs_2_ = bf16[128,512]{1,0:T(8,128)(2,1)S(1)} collective-permute-done((bf16[128,512]{1,0:T(8,128)(2,1)S(1)}, bf16[128,512]{1,0:T(8,128)(2,1)S(1)}, u32[]{:S(2)}, u32[]{:S(2)}) %collective-permute-start.3) | collective-permute-done | bytes 131104 | tf_op jit(solution)/shard_map/ppermute | solution.py:21
  14.8 0.5 %collective-permute-start.9 = (bf16[1056,128]{1,0:T(8,128)(2,1)S(1)}, bf16[1056,128]{1,0:T(8,128)(2,1)S(1)}, u32[]{:S(2)}, u32[]{:S(2)}) collective-permute-start(bf16[1056,128]{1,0:T(8,128)(2,1)S(1)} %get-tuple-element.105), channel_id=1, source_target_pairs={{0,1},{1,0},{2,3},{3,2},{4,5},{5,4},{6,7},{7,6},{8,9},{9,8},{10,11... | collective-permute-start | bytes 811016 | tf_op jit(solution)/shard_map/ppermute | solution.py:21
  15.3 1.2 %shard_map.94 = (f32[528,128]{1,0:T(8,128)S(1)}, f32[528,128]{1,0:T(8,128)S(1)}) custom-call(bf16[1024,128]{1,0:T(8,128)(2,1)S(1)} %get-tuple-element.101.gg_ref, bf16[1024,128]{1,0:T(8,128)(2,1)S(1)} %get-tuple-element.102.gu_ref, f32[16,128]{1,0:T(8,128)S(1)} %get-tuple-element.103.sums_ref, ...), custom_call_target="tpu_custom_call" | custom-call | flops 12884901888 | tf_op jit(solution)/shard_map/pallas_call | solution.py:44
  16.6 0.1 slice_add_fusion.2
  16.7 1.8 %collective-permute-start.12 = (bf16[528,128]{1,0:T(8,128)(2,1)S(1)}, bf16[528,128]{1,0:T(8,128)(2,1)S(1)}, u32[]{:S(2)}, u32[]{:S(2)}) collective-permute-start(bf16[528,128]{1,0:T(8,128)(2,1)S(1)} %convert_element_type.17), channel_id=1, source_target_pairs={{0,2},{1,3},{2,0},{3,1},{4,6},{5,7},{6,4},{7,5},{8,10},{9,11},{10,... | collective-permute-start | bytes 405512 | tf_op jit(solution)/shard_map/ppermute | solution.py:21
  18.6 0.4 %shard_map.95 = (f32[512,128]{1,0:T(8,128)S(1)}, f32[512,128]{1,0:T(8,128)S(1)}, f32[512,128]{1,0:T(8,128)S(1)}, f32[512,128]{1,0:T(8,128)S(1)}, f32[512,128]{1,0:T(8,128)S(1)}, /*index=5*/f32[512,128]{1,0:T(8,128)S(1)}) custom-call(bf16[128,512]{1,0:T(8,128)(2,1)S(1)} %get-tuple-element.108.refs_0_, ...), custom_call_target="tpu_custom_call" | custom-call | tf_op jit(solution)/shard_map/pallas_call | solution.py:44
  19.0 0.3 collective-permute-start.10
  19.3 1.6 %shard_map.98 = (f32[1024,128]{1,0:T(8,128)S(1)}, f32[1024,128]{1,0:T(8,128)S(1)}, f32[1024,128]{1,0:T(8,128)S(1)}, f32[1024,128]{1,0:T(8,128)S(1)}, f32[8,128]{1,0:T(8,128)S(1)}) custom-call(bf16[128,512]{1,0:T(8,128)(2,1)S(1)} %get-tuple-element.127.refs_0_, bf16[128,512]{1,0:T(8,128)(2,1)S(1)} %collective-permute-done.2.refs_1_, ...), custom_call_target="tpu_custom_call" | custom-call | flops 6442450944 | tf_op jit(solution)/shard_map/pallas_call | solution.py:44
  21.0 0.1 shard_map.96
  21.1 2.1 %collective-permute-done.12.got = bf16[528,128]{1,0:T(8,128)(2,1)S(1)} collective-permute-done((bf16[528,128]{1,0:T(8,128)(2,1)S(1)}, bf16[528,128]{1,0:T(8,128)(2,1)S(1)}, u32[]{:S(2)}, u32[]{:S(2)}) %collective-permute-start.12) | collective-permute-done | bytes 135200 | tf_op jit(solution)/shard_map/ppermute | solution.py:21
  23.2 0.1 shard_map.99.refs_0_.second
  23.4 2.1 %collective-permute-done.10.got = bf16[528,128]{1,0:T(8,128)(2,1)S(1)} collective-permute-done((bf16[528,128]{1,0:T(8,128)(2,1)S(1)}, bf16[528,128]{1,0:T(8,128)(2,1)S(1)}, u32[]{:S(2)}, u32[]{:S(2)}) %collective-permute-start.10) | collective-permute-done | bytes 135200 | tf_op jit(solution)/shard_map/ppermute | solution.py:21
  25.5 0.1 shard_map.97.refs_2_
  25.7 1.0 %shard_map.100.refs_2_ = f32[1024,128]{1,0:T(8,128)S(1)} custom-call(bf16[512,128]{1,0:T(8,128)(2,1)S(1)} %shard_map.99.refs_0_.second, bf16[512,128]{1,0:T(8,128)(2,1)S(1)} %collective-permute-done.13.refs_1_, bf16[512,128]{1,0:T(8,128)(2,1)S(1)} %shard_map.97.refs_2_, bf16[1024,2048]{1,0:T(8,128)(2,1)S(1)} %get-tuple-element.84.refs_2_.refs_3_.refs_1_), custom_call_target="tpu_custom_call" | custom-call | flops 1610612736 | tf_op jit(solution)/shard_map/pallas_call | solution.py:44
  26.7 0.3 collective-permute-done.11.refs_0_
  27.0 1.5 %shard_map.101 = (bf16[1024,128]{1,0:T(8,128)(2,1)S(1)}, bf16[1024,128]{1,0:T(8,128)(2,1)S(1)}, f32[16,128]{1,0:T(8,128)S(1)}, bf16[1056,128]{1,0:T(8,128)(2,1)S(1)}) custom-call(bf16[512,128]{1,0:T(8,128)(2,1)S(1)} %collective-permute-done.11.refs_0_, bf16[1024,2048]{1,0:T(8,128)(2,1)S(1)} %get-tuple-element.84.refs_2_.refs_3_.refs_1_, ...), custom_call_target="tpu_custom_call" | custom-call | flops 3221225472 | tf_op jit(solution)/shard_map/pallas_call | solution.py:44
  28.6 0.2 collective-permute-start.14
  28.8 1.2 %shard_map.102 = (f32[528,128]{1,0:T(8,128)S(1)}, f32[528,128]{1,0:T(8,128)S(1)}) custom-call(bf16[1024,128]{1,0:T(8,128)(2,1)S(1)} %get-tuple-element.144.gg_ref, bf16[1024,128]{1,0:T(8,128)(2,1)S(1)} %get-tuple-element.145.gu_ref, f32[16,128]{1,0:T(8,128)S(1)} %get-tuple-element.146.sums_ref, ...), custom_call_target="tpu_custom_call" | custom-call | flops 12884901888 | tf_op jit(solution)/shard_map/pallas_call | solution.py:44
  30.0 0.1 collective-permute-done.14
  30.2 0.1 fusion
  30.3 1.8 %collective-permute-start.15 = (bf16[528,128]{1,0:T(8,128)(2,1)S(1)}, bf16[528,128]{1,0:T(8,128)(2,1)S(1)}, u32[]{:S(2)}, u32[]{:S(2)}) collective-permute-start(bf16[528,128]{1,0:T(8,128)(2,1)S(1)} %get-tuple-element.155), channel_id=1, source_target_pairs={{0,2},{1,3},{2,0},{3,1},{4,6},{5,7},{6,4},{7,5},{8,10},{9,11},{10,... | collective-permute-start | bytes 405512 | tf_op jit(solution)/shard_map/ppermute | solution.py:21
  32.1 0.2 shard_map.103
  32.3 3.7 %collective-permute-done.15.got = bf16[528,128]{1,0:T(8,128)(2,1)S(1)} collective-permute-done((bf16[528,128]{1,0:T(8,128)(2,1)S(1)}, bf16[528,128]{1,0:T(8,128)(2,1)S(1)}, u32[]{:S(2)}, u32[]{:S(2)}) %collective-permute-start.15) | collective-permute-done | bytes 135200 | tf_op jit(solution)/shard_map/ppermute | solution.py:21
  36.1 0.8 %shard_map.104 = bf16[128,512]{1,0:T(8,128)(2,1)} custom-call(f32[528,128]{1,0:T(8,128)S(1)} %get-tuple-element.156.chip, bf16[528,128]{1,0:T(8,128)(2,1)S(1)} %collective-permute-done.15.got, bf16[512,128]{1,0:T(8,128)(2,1)S(1)} %shard_map.99.refs_0_.second, f32[512,128]{1,0:T(8,128)S(1)} %get-tuple-element.152.x, f32[512,128]{1,0:T(8,128)S(1)} %get-tuple-element.153.scale, ...), custom_call_target="tpu_custom_call" | custom-call | tf_op jit(solution)/shard_map/pallas_call | solution.py:44
  (20 shorter events, 0.4 us)
Async XLA Ops:
  0.0 3.5 %collective-permute-start = (bf16[128,512]{1,0:T(8,128)(2,1)}, bf16[128,512]{1,0:T(8,128)(2,1)S(1)}, u32[]{:S(2)}, u32[]{:S(2)}) collective-permute-start(bf16[128,512]{1,0:T(8,128)(2,1)} %refs_2_.1), channel_id=1, source_target_pairs={{0,1},{1,0},{2,3},{3,2},{4,5},{5,4},{6,7},{7,6},{8,9},{9,8},{10,11... | collective-permute-start | bytes 393224 | tf_op jit(solution)/shard_map/ppermute | solution.py:21
  0.5 3.1 %collective-permute-start.1 = (bf16[128,512]{1,0:T(8,128)(2,1)}, bf16[128,512]{1,0:T(8,128)(2,1)S(1)}, u32[]{:S(2)}, u32[]{:S(2)}) collective-permute-start(bf16[128,512]{1,0:T(8,128)(2,1)} %refs_3_.1), channel_id=1, source_target_pairs={{0,1},{1,0},{2,3},{3,2},{4,5},{5,4},{6,7},{7,6},{8,9},{9,8},{10,11... | collective-permute-start | bytes 393224 | tf_op jit(solution)/shard_map/ppermute | solution.py:21
  0.5 8.1 %collective-permute-start.5 = (bf16[128,512]{1,0:T(8,128)(2,1)}, bf16[128,512]{1,0:T(8,128)(2,1)S(1)}, u32[]{:S(2)}, u32[]{:S(2)}) collective-permute-start(bf16[128,512]{1,0:T(8,128)(2,1)} %refs_2_.1), channel_id=1, source_target_pairs={{0,2},{1,3},{2,0},{3,1},{4,6},{5,7},{6,4},{7,5},{8,10},{9,11},{10,... | collective-permute-start | bytes 393224 | tf_op jit(solution)/shard_map/ppermute | solution.py:21
  3.5 7.4 %collective-permute-start.4 = (bf16[128,512]{1,0:T(8,128)(2,1)}, bf16[128,512]{1,0:T(8,128)(2,1)S(1)}, u32[]{:S(2)}, u32[]{:S(2)}) collective-permute-start(bf16[128,512]{1,0:T(8,128)(2,1)} %refs_3_.1), channel_id=1, source_target_pairs={{0,2},{1,3},{2,0},{3,1},{4,6},{5,7},{6,4},{7,5},{8,10},{9,11},{10,... | collective-permute-start | bytes 393224 | tf_op jit(solution)/shard_map/ppermute | solution.py:21
  8.6 2.7 %collective-permute-start.7 = (bf16[128,512]{1,0:T(8,128)(2,1)S(1)}, bf16[128,512]{1,0:T(8,128)(2,1)S(1)}, u32[]{:S(2)}, u32[]{:S(2)}) collective-permute-start(bf16[128,512]{1,0:T(8,128)(2,1)S(1)} %collective-permute-done.5.refs_0_.refs_1_), channel_id=1, source_target_pairs={{0,1},{1,0},{2,3},{3,2},{4,5},{5,4},{6,7},{7,6},{8,9},{9,8},{10,11... | collective-permute-start | bytes 393224 | tf_op jit(solution)/shard_map/ppermute | solution.py:21
  8.7 6.1 %collective-permute-start.3 = (bf16[128,512]{1,0:T(8,128)(2,1)S(1)}, bf16[128,512]{1,0:T(8,128)(2,1)S(1)}, u32[]{:S(2)}, u32[]{:S(2)}) collective-permute-start(bf16[128,512]{1,0:T(8,128)(2,1)S(1)} %get-tuple-element.127.refs_0_), channel_id=1, source_target_pairs={{0,2},{1,3},{2,0},{3,1},{4,6},{5,7},{6,4},{7,5},{8,10},{9,11},{10,... | collective-permute-start | bytes 393224 | tf_op jit(solution)/shard_map/ppermute | solution.py:21
  10.7 6.0 %collective-permute-start.2 = (bf16[128,512]{1,0:T(8,128)(2,1)S(1)}, bf16[128,512]{1,0:T(8,128)(2,1)S(1)}, u32[]{:S(2)}, u32[]{:S(2)}) collective-permute-start(bf16[128,512]{1,0:T(8,128)(2,1)S(1)} %get-tuple-element.127.refs_0_), channel_id=1, source_target_pairs={{0,1},{1,0},{2,3},{3,2},{4,5},{5,4},{6,7},{7,6},{8,9},{9,8},{10,11... | collective-permute-start | bytes 393224 | tf_op jit(solution)/shard_map/ppermute | solution.py:21
  10.9 1.5 %collective-permute-start.6 = (bf16[128,512]{1,0:T(8,128)(2,1)S(1)}, bf16[128,512]{1,0:T(8,128)(2,1)S(1)}, u32[]{:S(2)}, u32[]{:S(2)}) collective-permute-start(bf16[128,512]{1,0:T(8,128)(2,1)S(1)} %collective-permute-done.4.refs_0_.second), channel_id=1, source_target_pairs={{0,1},{1,0},{2,3},{3,2},{4,5},{5,4},{6,7},{7,6},{8,9},{9,8},{10,11... | collective-permute-start | bytes 393224 | tf_op jit(solution)/shard_map/ppermute | solution.py:21
  14.8 1.9 %collective-permute-start.8 = (bf16[128,512]{1,0:T(8,128)(2,1)S(1)}, bf16[128,512]{1,0:T(8,128)(2,1)S(1)}, u32[]{:S(2)}, u32[]{:S(2)}) collective-permute-start(bf16[128,512]{1,0:T(8,128)(2,1)S(1)} %collective-permute-done.3.refs_2_), channel_id=1, source_target_pairs={{0,1},{1,0},{2,3},{3,2},{4,5},{5,4},{6,7},{7,6},{8,9},{9,8},{10,11... | collective-permute-start | bytes 393224 | tf_op jit(solution)/shard_map/ppermute | solution.py:21
  14.8 1.8 %collective-permute-start.9 = (bf16[1056,128]{1,0:T(8,128)(2,1)S(1)}, bf16[1056,128]{1,0:T(8,128)(2,1)S(1)}, u32[]{:S(2)}, u32[]{:S(2)}) collective-permute-start(bf16[1056,128]{1,0:T(8,128)(2,1)S(1)} %get-tuple-element.105), channel_id=1, source_target_pairs={{0,1},{1,0},{2,3},{3,2},{4,5},{5,4},{6,7},{7,6},{8,9},{9,8},{10,11... | collective-permute-start | bytes 811016 | tf_op jit(solution)/shard_map/ppermute | solution.py:21
  16.7 6.5 %collective-permute-start.12 = (bf16[528,128]{1,0:T(8,128)(2,1)S(1)}, bf16[528,128]{1,0:T(8,128)(2,1)S(1)}, u32[]{:S(2)}, u32[]{:S(2)}) collective-permute-start(bf16[528,128]{1,0:T(8,128)(2,1)S(1)} %convert_element_type.17), channel_id=1, source_target_pairs={{0,2},{1,3},{2,0},{3,1},{4,6},{5,7},{6,4},{7,5},{8,10},{9,11},{10,... | collective-permute-start | bytes 405512 | tf_op jit(solution)/shard_map/ppermute | solution.py:21
  19.0 6.5 %collective-permute-start.10 = (bf16[528,128]{1,0:T(8,128)(2,1)S(1)}, bf16[528,128]{1,0:T(8,128)(2,1)S(1)}, u32[]{:S(2)}, u32[]{:S(2)}) collective-permute-start(bf16[528,128]{1,0:T(8,128)(2,1)S(1)} %convert_element_type.16), channel_id=1, source_target_pairs={{0,2},{1,3},{2,0},{3,1},{4,6},{5,7},{6,4},{7,5},{8,10},{9,11},{10,... | collective-permute-start | bytes 405512 | tf_op jit(solution)/shard_map/ppermute | solution.py:21
  23.3 2.4 %collective-permute-start.13 = (bf16[512,128]{1,0:T(8,128)(2,1)S(1)}, bf16[512,128]{1,0:T(8,128)(2,1)S(1)}, u32[]{:S(2)}, u32[]{:S(2)}) collective-permute-start(bf16[512,128]{1,0:T(8,128)(2,1)S(1)} %shard_map.99.refs_0_.second), channel_id=1, source_target_pairs={{0,1},{1,0},{2,3},{3,2},{4,5},{5,4},{6,7},{7,6},{8,9},{9,8},{10,11... | collective-permute-start | bytes 393224 | tf_op jit(solution)/shard_map/ppermute | solution.py:21
  25.6 1.4 %collective-permute-start.11 = (bf16[512,128]{1,0:T(8,128)(2,1)S(1)}, bf16[512,128]{1,0:T(8,128)(2,1)S(1)}, u32[]{:S(2)}, u32[]{:S(2)}) collective-permute-start(bf16[512,128]{1,0:T(8,128)(2,1)S(1)} %shard_map.97.refs_2_), channel_id=1, source_target_pairs={{0,1},{1,0},{2,3},{3,2},{4,5},{5,4},{6,7},{7,6},{8,9},{9,8},{10,11... | collective-permute-start | bytes 393224 | tf_op jit(solution)/shard_map/ppermute | solution.py:21
  28.6 1.6 %collective-permute-start.14 = (bf16[1056,128]{1,0:T(8,128)(2,1)S(1)}, bf16[1056,128]{1,0:T(8,128)(2,1)S(1)}, u32[]{:S(2)}, u32[]{:S(2)}) collective-permute-start(bf16[1056,128]{1,0:T(8,128)(2,1)S(1)} %get-tuple-element.148), channel_id=1, source_target_pairs={{0,1},{1,0},{2,3},{3,2},{4,5},{5,4},{6,7},{7,6},{8,9},{9,8},{10,11... | collective-permute-start | bytes 811016 | tf_op jit(solution)/shard_map/ppermute | solution.py:21
  30.3 5.8 %collective-permute-start.15 = (bf16[528,128]{1,0:T(8,128)(2,1)S(1)}, bf16[528,128]{1,0:T(8,128)(2,1)S(1)}, u32[]{:S(2)}, u32[]{:S(2)}) collective-permute-start(bf16[528,128]{1,0:T(8,128)(2,1)S(1)} %get-tuple-element.155), channel_id=1, source_target_pairs={{0,2},{1,3},{2,0},{3,1},{4,6},{5,7},{6,4},{7,5},{8,10},{9,11},{10,... | collective-permute-start | bytes 405512 | tf_op jit(solution)/shard_map/ppermute | solution.py:21

commit v6 on v5

--- a/solution.py
+++ b/solution.py
@@ -228,11 +228,6 @@
         out_ref[feat : feat + EXTRA, :] = sums.astype(out_ref.dtype)
 
 
-def double(out_ref):
-    rows = out_ref.shape[0] // 2
-    return out_ref.at[0:rows, :], out_ref.at[rows : 2 * rows, :]
-
-
 def back_kernel(top, keys, raw, *refs):
     n = len(keys)
     parts, down_w = refs[:n], refs[n]
@@ -251,12 +246,11 @@
     gg_ref[...] = gg
     gu_ref[...] = gu
     sums_ref[...] = sums
-    for key, out_ref in zip(range(1, top, 2), outs):
-        write_terms(top, (top + key, key), gg, gu, sums, gate_w, up_w, double(out_ref))
+    sent = range(1, top, 2)
+    write_terms(top, (*(top + key for key in sent), *sent), gg, gu, sums, gate_w, up_w, outs)
 
 
 def kept_kernel(top, keys, gg_ref, gu_ref, sums_ref, gate_w, up_w, *outs):
-    keys = [top + key for key in keys] + list(keys)
     write_terms(top, keys, gg_ref[...], gu_ref[...], sums_ref[...], gate_w, up_w, outs)
 
 
@@ -323,34 +317,27 @@
     def semaphores(count):
         return [pltpu.SemaphoreType.DMA((count,))]
 
-    def reduce(grads, blocks_sent):
+    def reduce(start, grads, blocks_sent):
         parts = kernel_call(
-            functools.partial(kept_kernel, top, kept),
-            [VM((block, LANES), F32)] * (2 * len(kept)), *grads, *gate_up,
-            flops=8 * product,
+            functools.partial(kept_kernel, top, [start + key for key in kept]),
+            [VM((block, LANES), F32)] * len(kept), *grads, *gate_up,
+            flops=2 * product * len(kept) // top,
         )
-        blocks = dict(zip(kept, zip(parts[: len(kept)], parts[len(kept) :])))
-        whole = dict(zip(sent, blocks_sent))
+        blocks = dict(zip(kept, parts)) | dict(zip(sent, blocks_sent))
         for bit in low:
             for key in sorted(blocks):
                 if key & bit == 0:
-                    value = whole.get(key ^ bit)
-                    if value is None:
-                        value = jnp.concatenate(blocks[key ^ bit]).astype(BF16)
-                    value = hop(value, bit).astype(F32)
-                    blocks[key] = tuple(
-                        own + got for own, got in zip(blocks[key], (value[:block], value[block:]))
-                    )
-                    blocks.pop(key ^ bit, None)
-        return blocks[0]
+                    got = hop(blocks.pop(key ^ bit).astype(BF16), bit)
+                    blocks[key] = blocks[key].astype(F32) + got.astype(F32)
+        return blocks[0], parts[0]
 
     def back_call(keys, raw, parts, held, factors):
         *grads, = kernel_call(
             functools.partial(back_kernel, top, keys, raw),
-            grad_outs + [VM((2 * block, LANES), BF16)] * len(sent),
+            grad_outs + [VM((block, LANES), BF16)] * (2 * len(sent)),
             *parts, down, held, *factors, *gate_up, flops=2 * product,
         )
-        return grads[:3], grads[3:]
+        return grads[:3], grads[3 : 3 + len(sent)], grads[3 + len(sent) :]
 
     x2_cross = hop(hidden_second, top)
     cot_cross = hop(cotangent, top)
@@ -379,14 +366,14 @@
         factor_outs, *x2_theirs, gain, router, *gate_up, *partial, flops=2 * product,
     )
 
-    grads, blocks_sent = back_call(across, True, cot_theirs, back_mine, factors2)
-    x1_cross, *grads = lax.optimization_barrier((x1_cross, *grads))
+    grads, to_theirs, to_mine = back_call(across, True, cot_theirs, back_mine, factors2)
+    chip_theirs, part = reduce(top, grads, to_theirs)
+    x1_cross, part = lax.optimization_barrier((x1_cross, part))
     x1_mine, x1_theirs = spread(x1_own, low), spread(x1_cross, low)
-    chip_theirs, chip_mine = reduce(grads, blocks_sent)
-    x1_mine, x1_theirs, chip_theirs, chip_mine = lax.optimization_barrier(
-        (x1_mine, x1_theirs, chip_theirs, chip_mine)
-    )
     got_mine = hop(chip_theirs.astype(BF16), top)
+    *grads, chip_theirs = lax.optimization_barrier((*grads, chip_theirs))
+    chip_mine, _ = reduce(0, grads, to_mine)
+    x1_mine, x1_theirs, chip_mine = lax.optimization_barrier((x1_mine, x1_theirs, chip_mine))
 
     rows2, chip_mine = lax.optimization_barrier((rows2, chip_mine))
     columns2 = kernel_call(
@@ -395,12 +382,11 @@
     )
     cot_columns = kernel_call(turn_kernel, columns[:2], after(cot_own, rows2), cot_cross)
 
-    columns2, chip_mine = lax.optimization_barrier((columns2, chip_mine))
     got_theirs = hop(chip_mine.astype(BF16), top)
     x1_parts = (*x1_mine, *x1_theirs)
     *factors1, rows1 = kernel_call(
         functools.partial(factors_first_kernel, top, 0),
-        factor_outs, *x1_parts, gain, router, *gate_up, flops=4 * product,
+        factor_outs, *x1_parts, gain, router, *gate_up,
     )
 
     def second(chip, got, cot, columns):
@@ -418,9 +404,13 @@
         functools.partial(back_part_kernel, top, (*near, top)),
         wide_units, *second_mine, cross_second, down, flops=product,
     )
-    grads, blocks_sent = back_call(across[1:], False, second_theirs[1:], back_most, factors1)
-    chip_theirs, chip_mine = reduce(grads, blocks_sent)
+    grads, to_theirs, to_mine = back_call(
+        across[1:], False, second_theirs[1:], back_most, factors1
+    )
+    chip_theirs, _ = reduce(top, grads, to_theirs)
     got = hop(chip_theirs.astype(BF16), top)
+    *grads, chip_theirs = lax.optimization_barrier((*grads, chip_theirs))
+    chip_mine, _ = reduce(0, grads, to_mine)
     rows1 = after(rows1, chip_mine)
     columns1 = kernel_call(
         functools.partial(column_kernel, top, (0,), 1),

time: 37 us -> 37.2 us (level)
  starting transfers between devices: 11 us -> 10.5 us
  Pallas kernels: 16.4 us -> 16.8 us
    ppermute x16 -> x18, starting transfers between devices: 11 us -> 10.5 us  [hop(): return lax.ppermute(value, 'tensor', [(j, j ^ bit) for j in range(size)])]
    pallas_call x14 -> x16, Pallas kernels: 16.4 us -> 16.8 us  [kernel_call(): pl.pallas_call(kernel, out_shape=list(outs) if many else outs, in_specs=[...]
    ppermute x16 -> x18, waiting for transfers between devices: 9.04 us -> 9.4 us  [hop(): return lax.ppermute(value, 'tensor', [(j, j ^ bit) for j in range(size)])]
  transfers between devices with their start and end apart: 16 -> 18, of which waited for: 6 -> 7; matrix products, arithmetic and copies ran while one was open for 0% -> 0% of each run, Pallas kernels for 38% -> 39%
where the time goes in v6:
time: 37.2 us; the launch traced here: 37 us
  Pallas kernels  16.8 us (45%)
  starting transfers between devices  10.5 us (28%)
  waiting for transfers between devices  9.4 us (25%)
    pallas_call x16, Pallas kernels, kernel_call(): pl.pallas_call(kernel, out_shape=list(outs) if many else outs, in_specs=[...  16.8 us
    ppermute x18, starting transfers between devices, hop(): return lax.ppermute(value, 'tensor', [(j, j ^ bit) for j in range(size)])  10.5 us
    ppermute x18, waiting for transfers between devices, hop(): return lax.ppermute(value, 'tensor', [(j, j ^ bit) for j in range(size)])  9.4 us
  transfers between devices with their start and end apart: 18, of which 7 were waited for; matrix products, arithmetic and copies ran while one was open for 0% of the time, Pallas kernels for 39%

profile of v6, /device:TPU:0, one launch (start us, length us, event | category | flops | bytes accessed | tf_op | source)
XLA Modules:
  0.0 37.0 jit_solution(675823310392110209)
XLA Ops:
  0.0 0.5 %collective-permute-start.2 = (bf16[128,512]{1,0:T(8,128)(2,1)}, bf16[128,512]{1,0:T(8,128)(2,1)S(1)}, u32[]{:S(2)}, u32[]{:S(2)}) collective-permute-start(bf16[128,512]{1,0:T(8,128)(2,1)} %refs_2_.1), channel_id=1, source_target_pairs={{0,1},{1,0},{2,3},{3,2},{4,5},{5,4},{6,7},{7,6},{8,9},{9,8},{10,11... | collective-permute-start | bytes 393224 | tf_op jit(solution)/shard_map/ppermute | solution.py:21
  0.5 3.0 %collective-permute-start = (bf16[128,512]{1,0:T(8,128)(2,1)}, bf16[128,512]{1,0:T(8,128)(2,1)S(1)}, u32[]{:S(2)}, u32[]{:S(2)}) collective-permute-start(bf16[128,512]{1,0:T(8,128)(2,1)} %refs_3_.1), channel_id=1, source_target_pairs={{0,2},{1,3},{2,0},{3,1},{4,6},{5,7},{6,4},{7,5},{8,10},{9,11},{10,... | collective-permute-start | bytes 393224 | tf_op jit(solution)/shard_map/ppermute | solution.py:21
  3.5 5.0 %shard_map.91 = (bf16[128,512]{1,0:T(8,128)(2,1)S(1)}, bf16[128,512]{1,0:T(8,128)(2,1)S(1)}, bf16[128,512]{1,0:T(8,128)(2,1)S(1)}, f32[1,2048]{1,0:T(1,128)S(1)}...) custom-call(bf16[128,512]{1,0:T(8,128)(2,1)S(1)} %collective-permute, ...), custom_call_target="tpu_custom_call" | custom-call | flops 4831838208 | tf_op jit(solution)/shard_map/pallas_call | solution.py:44
  8.6 1.6 %collective-permute-done.1.refs_0_.refs_1_ = bf16[128,512]{1,0:T(8,128)(2,1)S(1)} collective-permute-done((bf16[128,512]{1,0:T(8,128)(2,1)}, bf16[128,512]{1,0:T(8,128)(2,1)S(1)}, u32[]{:S(2)}, u32[]{:S(2)}) %collective-permute-start.1) | collective-permute-done | bytes 131104 | tf_op jit(solution)/shard_map/ppermute | solution.py:21
  10.2 0.5 %collective-permute-start.7 = (bf16[128,512]{1,0:T(8,128)(2,1)S(1)}, bf16[128,512]{1,0:T(8,128)(2,1)S(1)}, u32[]{:S(2)}, u32[]{:S(2)}) collective-permute-start(bf16[128,512]{1,0:T(8,128)(2,1)S(1)} %get-tuple-element.113.refs_0_), channel_id=1, source_target_pairs={{0,1},{1,0},{2,3},{3,2},{4,5},{5,4},{6,7},{7,6},{8,9},{9,8},{10,11... | collective-permute-start | bytes 393224 | tf_op jit(solution)/shard_map/ppermute | solution.py:21
  10.7 1.7 %collective-permute-start.8 = (bf16[128,512]{1,0:T(8,128)(2,1)S(1)}, bf16[128,512]{1,0:T(8,128)(2,1)S(1)}, u32[]{:S(2)}, u32[]{:S(2)}) collective-permute-start(bf16[128,512]{1,0:T(8,128)(2,1)S(1)} %get-tuple-element.113.refs_0_), channel_id=1, source_target_pairs={{0,2},{1,3},{2,0},{3,1},{4,6},{5,7},{6,4},{7,5},{8,10},{9,11},{10,... | collective-permute-start | bytes 393224 | tf_op jit(solution)/shard_map/ppermute | solution.py:21
  12.4 1.1 %shard_map.92 = (f32[1024,128]{1,0:T(8,128)S(1)}, f32[1024,128]{1,0:T(8,128)S(1)}, f32[1024,128]{1,0:T(8,128)S(1)}, f32[1024,128]{1,0:T(8,128)S(1)}, f32[8,128]{1,0:T(8,128)S(1)}) custom-call(bf16[128,512]{1,0:T(8,128)(2,1)S(1)} %collective-permute-done.1.refs_0_.refs_1_, bf16[128,512]{1,0:T(8,128)(2,1)S(1)} %collective-permute-done.5.refs_1_, ...), custom_call_target="tpu_custom_call" | custom-call | flops 3221225472 | tf_op jit(solution)/shard_map/pallas_call | solution.py:44
  13.6 0.2 collective-permute-done.4.refs_1_
  13.8 1.8 %shard_map.93 = (bf16[1024,128]{1,0:T(8,128)(2,1)S(1)}, bf16[1024,128]{1,0:T(8,128)(2,1)S(1)}, f32[16,128]{1,0:T(8,128)S(1)}, bf16[528,128]{1,0:T(8,128)(2,1)S(1)}, bf16[528,128]{1,0:T(8,128)(2,1)S(1)}) custom-call(bf16[128,512]{1,0:T(8,128)(2,1)S(1)} %collective-permute-done.refs_0_.second, bf16[128,512]{1,0:T(8,128)(2,1)S(1)} %collective-permute-done.4.refs_1_, ...), custom_call_target="tpu_custom_call" | custom-call | flops 3221225472 | tf_op jit(solution)/shard_map/pallas_call | solution.py:44
  15.6 0.4 collective-permute-start.6
  16.0 0.7 %shard_map.94 = f32[528,128]{1,0:T(8,128)S(1)} custom-call(bf16[1024,128]{1,0:T(8,128)(2,1)S(1)} %get-tuple-element.98.gg_ref, bf16[1024,128]{1,0:T(8,128)(2,1)S(1)} %get-tuple-element.99.gu_ref, f32[16,128]{1,0:T(8,128)S(1)} %get-tuple-element.100.sums_ref, bf16[2048,1024]{1,0:T(8,128)(2,1)S(1)} %get-tuple-element.81.refs_4_.refs_8_.gate_w.refs_6_.refs_7_, ...), custom_call_target="tpu_custom_call" | custom-call | flops 1610612736 | tf_op jit(solution)/shard_map/pallas_call | solution.py:44
  16.7 0.3 collective-permute-start.9
  17.0 0.3 collective-permute-start.10
  17.3 1.1 %collective-permute-start.13 = (bf16[528,128]{1,0:T(8,128)(2,1)S(1)}, bf16[528,128]{1,0:T(8,128)(2,1)S(1)}, u32[]{:S(2)}, u32[]{:S(2)}) collective-permute-start(bf16[528,128]{1,0:T(8,128)(2,1)S(1)} %get-tuple-element.143), channel_id=1, source_target_pairs={{0,2},{1,3},{2,0},{3,1},{4,6},{5,7},{6,4},{7,5},{8,10},{9,11},{10,... | collective-permute-start | bytes 405512 | tf_op jit(solution)/shard_map/ppermute | solution.py:21
  18.4 0.7 %shard_map.95 = f32[528,128]{1,0:T(8,128)S(1)} custom-call(bf16[1024,128]{1,0:T(8,128)(2,1)S(1)} %get-tuple-element.98.gg_ref, bf16[1024,128]{1,0:T(8,128)(2,1)S(1)} %get-tuple-element.99.gu_ref, f32[16,128]{1,0:T(8,128)S(1)} %get-tuple-element.100.sums_ref, bf16[2048,1024]{1,0:T(8,128)(2,1)S(1)} %get-tuple-element.81.refs_4_.refs_8_.gate_w.refs_6_.refs_7_, ...), custom_call_target="tpu_custom_call" | custom-call | flops 1610612736 | tf_op jit(solution)/shard_map/pallas_call | solution.py:44
  19.2 1.0 %collective-permute-start.11 = (bf16[528,128]{1,0:T(8,128)(2,1)S(1)}, bf16[528,128]{1,0:T(8,128)(2,1)S(1)}, u32[]{:S(2)}, u32[]{:S(2)}) collective-permute-start(bf16[528,128]{1,0:T(8,128)(2,1)S(1)} %convert_element_type.23), channel_id=1, source_target_pairs={{0,2},{1,3},{2,0},{3,1},{4,6},{5,7},{6,4},{7,5},{8,10},{9,11},{10,... | collective-permute-start | bytes 405512 | tf_op jit(solution)/shard_map/ppermute | solution.py:21
  20.3 0.4 %shard_map.97 = (f32[512,128]{1,0:T(8,128)S(1)}, f32[512,128]{1,0:T(8,128)S(1)}, f32[512,128]{1,0:T(8,128)S(1)}, f32[512,128]{1,0:T(8,128)S(1)}, f32[512,128]{1,0:T(8,128)S(1)}, /*index=5*/f32[512,128]{1,0:T(8,128)S(1)}) custom-call(bf16[128,512]{1,0:T(8,128)(2,1)S(1)} %get-tuple-element.108.refs_0_, ...), custom_call_target="tpu_custom_call" | custom-call | tf_op jit(solution)/shard_map/pallas_call | solution.py:44
  20.7 1.7 %shard_map.99 = (f32[1024,128]{1,0:T(8,128)S(1)}, f32[1024,128]{1,0:T(8,128)S(1)}, f32[1024,128]{1,0:T(8,128)S(1)}, f32[1024,128]{1,0:T(8,128)S(1)}, f32[8,128]{1,0:T(8,128)S(1)}) custom-call(bf16[128,512]{1,0:T(8,128)(2,1)S(1)} %get-tuple-element.113.refs_0_, bf16[128,512]{1,0:T(8,128)(2,1)S(1)} %collective-permute-done.7.refs_1_, ...), custom_call_target="tpu_custom_call" | custom-call | tf_op jit(solution)/shard_map/pallas_call | solution.py:44
  22.3 0.1 shard_map.96
  22.5 1.3 %collective-permute-done.13.got = bf16[528,128]{1,0:T(8,128)(2,1)S(1)} collective-permute-done((bf16[528,128]{1,0:T(8,128)(2,1)S(1)}, bf16[528,128]{1,0:T(8,128)(2,1)S(1)}, u32[]{:S(2)}, u32[]{:S(2)}) %collective-permute-start.13) | collective-permute-done | bytes 135200 | tf_op jit(solution)/shard_map/ppermute | solution.py:21
  24.0 2.0 %collective-permute-done.11.got = bf16[528,128]{1,0:T(8,128)(2,1)S(1)} collective-permute-done((bf16[528,128]{1,0:T(8,128)(2,1)S(1)}, bf16[528,128]{1,0:T(8,128)(2,1)S(1)}, u32[]{:S(2)}, u32[]{:S(2)}) %collective-permute-start.11) | collective-permute-done | bytes 135200 | tf_op jit(solution)/shard_map/ppermute | solution.py:21
  26.2 1.0 %shard_map.101.refs_2_ = f32[1024,128]{1,0:T(8,128)S(1)} custom-call(bf16[512,128]{1,0:T(8,128)(2,1)S(1)} %shard_map.100.refs_0_.second, bf16[512,128]{1,0:T(8,128)(2,1)S(1)} %collective-permute-done.14.refs_1_, bf16[512,128]{1,0:T(8,128)(2,1)S(1)} %shard_map.98.refs_2_, bf16[1024,2048]{1,0:T(8,128)(2,1)S(1)} %get-tuple-element.77.refs_2_.refs_3_.refs_1_), custom_call_target="tpu_custom_call" | custom-call | flops 1610612736 | tf_op jit(solution)/shard_map/pallas_call | solution.py:44
  27.1 0.3 collective-permute-done.12.refs_0_
  27.5 1.5 %shard_map.102 = (bf16[1024,128]{1,0:T(8,128)(2,1)S(1)}, bf16[1024,128]{1,0:T(8,128)(2,1)S(1)}, f32[16,128]{1,0:T(8,128)S(1)}, bf16[528,128]{1,0:T(8,128)(2,1)S(1)}, bf16[528,128]{1,0:T(8,128)(2,1)S(1)}) custom-call(bf16[512,128]{1,0:T(8,128)(2,1)S(1)} %collective-permute-done.12.refs_0_, bf16[1024,2048]{1,0:T(8,128)(2,1)S(1)} %get-tuple-element.77.refs_2_.refs_3_.refs_1_, ...), custom_call_target="tpu_custom_call" | custom-call | flops 3221225472 | tf_op jit(solution)/shard_map/pallas_call | solution.py:44
  29.0 0.2 collective-permute-start.15
  29.3 0.3 collective-permute-start.16
  29.6 0.7 %shard_map.103 = f32[528,128]{1,0:T(8,128)S(1)} custom-call(bf16[1024,128]{1,0:T(8,128)(2,1)S(1)} %get-tuple-element.134.gg_ref, bf16[1024,128]{1,0:T(8,128)(2,1)S(1)} %get-tuple-element.135.gu_ref, f32[16,128]{1,0:T(8,128)S(1)} %get-tuple-element.136.sums_ref, bf16[2048,1024]{1,0:T(8,128)(2,1)S(1)} %get-tuple-element.81.refs_4_.refs_8_.gate_w.refs_6_.refs_7_, ...), custom_call_target="tpu_custom_call" | custom-call | flops 1610612736 | tf_op jit(solution)/shard_map/pallas_call | solution.py:44
  30.5 0.9 %collective-permute-start.17 = (bf16[528,128]{1,0:T(8,128)(2,1)S(1)}, bf16[528,128]{1,0:T(8,128)(2,1)S(1)}, u32[]{:S(2)}, u32[]{:S(2)}) collective-permute-start(bf16[528,128]{1,0:T(8,128)(2,1)S(1)} %convert_add_fusion.1), channel_id=1, source_target_pairs={{0,2},{1,3},{2,0},{3,1},{4,6},{5,7},{6,4},{7,5},{8,10},{9,11},{10,... | collective-permute-start | bytes 405512 | tf_op jit(solution)/shard_map/ppermute | solution.py:21
  31.4 0.7 %shard_map.104 = f32[528,128]{1,0:T(8,128)S(1)} custom-call(bf16[1024,128]{1,0:T(8,128)(2,1)S(1)} %get-tuple-element.134.gg_ref, bf16[1024,128]{1,0:T(8,128)(2,1)S(1)} %get-tuple-element.135.gu_ref, f32[16,128]{1,0:T(8,128)S(1)} %get-tuple-element.136.sums_ref, bf16[2048,1024]{1,0:T(8,128)(2,1)S(1)} %get-tuple-element.81.refs_4_.refs_8_.gate_w.refs_6_.refs_7_, ...), custom_call_target="tpu_custom_call" | custom-call | flops 1610612736 | tf_op jit(solution)/shard_map/pallas_call | solution.py:44
  32.2 0.2 shard_map.105
  32.4 3.8 %collective-permute-done.17.got = bf16[528,128]{1,0:T(8,128)(2,1)S(1)} collective-permute-done((bf16[528,128]{1,0:T(8,128)(2,1)S(1)}, bf16[528,128]{1,0:T(8,128)(2,1)S(1)}, u32[]{:S(2)}, u32[]{:S(2)}) %collective-permute-start.17) | collective-permute-done | bytes 135200 | tf_op jit(solution)/shard_map/ppermute | solution.py:21
  36.2 0.8 %shard_map.106 = bf16[128,512]{1,0:T(8,128)(2,1)} custom-call(f32[528,128]{1,0:T(8,128)S(1)} %convert_add_fusion.chip, bf16[528,128]{1,0:T(8,128)(2,1)S(1)} %collective-permute-done.17.got, bf16[512,128]{1,0:T(8,128)(2,1)S(1)} %shard_map.100.refs_0_.second, f32[512,128]{1,0:T(8,128)S(1)} %get-tuple-element.140.x, f32[512,128]{1,0:T(8,128)S(1)} %get-tuple-element.141.scale, ...), custom_call_target="tpu_custom_call" | custom-call | tf_op jit(solution)/shard_map/pallas_call | solution.py:44
  (25 shorter events, 0.8 us)
Async XLA Ops:
  0.0 3.5 %collective-permute-start.2 = (bf16[128,512]{1,0:T(8,128)(2,1)}, bf16[128,512]{1,0:T(8,128)(2,1)S(1)}, u32[]{:S(2)}, u32[]{:S(2)}) collective-permute-start(bf16[128,512]{1,0:T(8,128)(2,1)} %refs_2_.1), channel_id=1, source_target_pairs={{0,1},{1,0},{2,3},{3,2},{4,5},{5,4},{6,7},{7,6},{8,9},{9,8},{10,11... | collective-permute-start | bytes 393224 | tf_op jit(solution)/shard_map/ppermute | solution.py:21
  0.5 3.1 %collective-permute-start.3 = (bf16[128,512]{1,0:T(8,128)(2,1)}, bf16[128,512]{1,0:T(8,128)(2,1)S(1)}, u32[]{:S(2)}, u32[]{:S(2)}) collective-permute-start(bf16[128,512]{1,0:T(8,128)(2,1)} %refs_3_.1), channel_id=1, source_target_pairs={{0,1},{1,0},{2,3},{3,2},{4,5},{5,4},{6,7},{7,6},{8,9},{9,8},{10,11... | collective-permute-start | bytes 393224 | tf_op jit(solution)/shard_map/ppermute | solution.py:21
  0.5 11.9 %collective-permute-start = (bf16[128,512]{1,0:T(8,128)(2,1)}, bf16[128,512]{1,0:T(8,128)(2,1)S(1)}, u32[]{:S(2)}, u32[]{:S(2)}) collective-permute-start(bf16[128,512]{1,0:T(8,128)(2,1)} %refs_3_.1), channel_id=1, source_target_pairs={{0,2},{1,3},{2,0},{3,1},{4,6},{5,7},{6,4},{7,5},{8,10},{9,11},{10,... | collective-permute-start | bytes 393224 | tf_op jit(solution)/shard_map/ppermute | solution.py:21
  3.5 6.7 %collective-permute-start.1 = (bf16[128,512]{1,0:T(8,128)(2,1)}, bf16[128,512]{1,0:T(8,128)(2,1)S(1)}, u32[]{:S(2)}, u32[]{:S(2)}) collective-permute-start(bf16[128,512]{1,0:T(8,128)(2,1)} %refs_2_.1), channel_id=1, source_target_pairs={{0,2},{1,3},{2,0},{3,1},{4,6},{5,7},{6,4},{7,5},{8,10},{9,11},{10,... | collective-permute-start | bytes 393224 | tf_op jit(solution)/shard_map/ppermute | solution.py:21
  10.2 2.3 %collective-permute-start.5 = (bf16[128,512]{1,0:T(8,128)(2,1)S(1)}, bf16[128,512]{1,0:T(8,128)(2,1)S(1)}, u32[]{:S(2)}, u32[]{:S(2)}) collective-permute-start(bf16[128,512]{1,0:T(8,128)(2,1)S(1)} %collective-permute-done.1.refs_0_.refs_1_), channel_id=1, source_target_pairs={{0,1},{1,0},{2,3},{3,2},{4,5},{5,4},{6,7},{7,6},{8,9},{9,8},{10,11... | collective-permute-start | bytes 393224 | tf_op jit(solution)/shard_map/ppermute | solution.py:21
  10.2 9.0 %collective-permute-start.7 = (bf16[128,512]{1,0:T(8,128)(2,1)S(1)}, bf16[128,512]{1,0:T(8,128)(2,1)S(1)}, u32[]{:S(2)}, u32[]{:S(2)}) collective-permute-start(bf16[128,512]{1,0:T(8,128)(2,1)S(1)} %get-tuple-element.113.refs_0_), channel_id=1, source_target_pairs={{0,1},{1,0},{2,3},{3,2},{4,5},{5,4},{6,7},{7,6},{8,9},{9,8},{10,11... | collective-permute-start | bytes 393224 | tf_op jit(solution)/shard_map/ppermute | solution.py:21
  10.7 6.0 %collective-permute-start.8 = (bf16[128,512]{1,0:T(8,128)(2,1)S(1)}, bf16[128,512]{1,0:T(8,128)(2,1)S(1)}, u32[]{:S(2)}, u32[]{:S(2)}) collective-permute-start(bf16[128,512]{1,0:T(8,128)(2,1)S(1)} %get-tuple-element.113.refs_0_), channel_id=1, source_target_pairs={{0,2},{1,3},{2,0},{3,1},{4,6},{5,7},{6,4},{7,5},{8,10},{9,11},{10,... | collective-permute-start | bytes 393224 | tf_op jit(solution)/shard_map/ppermute | solution.py:21
  12.4 1.3 %collective-permute-start.4 = (bf16[128,512]{1,0:T(8,128)(2,1)S(1)}, bf16[128,512]{1,0:T(8,128)(2,1)S(1)}, u32[]{:S(2)}, u32[]{:S(2)}) collective-permute-start(bf16[128,512]{1,0:T(8,128)(2,1)S(1)} %collective-permute-done.refs_0_.second), channel_id=1, source_target_pairs={{0,1},{1,0},{2,3},{3,2},{4,5},{5,4},{6,7},{7,6},{8,9},{9,8},{10,11... | collective-permute-start | bytes 393224 | tf_op jit(solution)/shard_map/ppermute | solution.py:21
  15.6 1.7 %collective-permute-start.6 = (bf16[528,128]{1,0:T(8,128)(2,1)S(1)}, bf16[528,128]{1,0:T(8,128)(2,1)S(1)}, u32[]{:S(2)}, u32[]{:S(2)}) collective-permute-start(bf16[528,128]{1,0:T(8,128)(2,1)S(1)} %get-tuple-element.93), channel_id=1, source_target_pairs={{0,1},{1,0},{2,3},{3,2},{4,5},{5,4},{6,7},{7,6},{8,9},{9,8},{10,11... | collective-permute-start | bytes 405512 | tf_op jit(solution)/shard_map/ppermute | solution.py:21
  16.7 2.5 %collective-permute-start.9 = (bf16[128,512]{1,0:T(8,128)(2,1)S(1)}, bf16[128,512]{1,0:T(8,128)(2,1)S(1)}, u32[]{:S(2)}, u32[]{:S(2)}) collective-permute-start(bf16[128,512]{1,0:T(8,128)(2,1)S(1)} %collective-permute-done.8.refs_2_), channel_id=1, source_target_pairs={{0,1},{1,0},{2,3},{3,2},{4,5},{5,4},{6,7},{7,6},{8,9},{9,8},{10,11... | collective-permute-start | bytes 393224 | tf_op jit(solution)/shard_map/ppermute | solution.py:21
  17.0 2.2 %collective-permute-start.10 = (bf16[528,128]{1,0:T(8,128)(2,1)S(1)}, bf16[528,128]{1,0:T(8,128)(2,1)S(1)}, u32[]{:S(2)}, u32[]{:S(2)}) collective-permute-start(bf16[528,128]{1,0:T(8,128)(2,1)S(1)} %get-tuple-element.101), channel_id=1, source_target_pairs={{0,1},{1,0},{2,3},{3,2},{4,5},{5,4},{6,7},{7,6},{8,9},{9,8},{10,11... | collective-permute-start | bytes 405512 | tf_op jit(solution)/shard_map/ppermute | solution.py:21
  17.3 6.5 %collective-permute-start.13 = (bf16[528,128]{1,0:T(8,128)(2,1)S(1)}, bf16[528,128]{1,0:T(8,128)(2,1)S(1)}, u32[]{:S(2)}, u32[]{:S(2)}) collective-permute-start(bf16[528,128]{1,0:T(8,128)(2,1)S(1)} %get-tuple-element.143), channel_id=1, source_target_pairs={{0,2},{1,3},{2,0},{3,1},{4,6},{5,7},{6,4},{7,5},{8,10},{9,11},{10,... | collective-permute-start | bytes 405512 | tf_op jit(solution)/shard_map/ppermute | solution.py:21
  19.2 6.7 %collective-permute-start.11 = (bf16[528,128]{1,0:T(8,128)(2,1)S(1)}, bf16[528,128]{1,0:T(8,128)(2,1)S(1)}, u32[]{:S(2)}, u32[]{:S(2)}) collective-permute-start(bf16[528,128]{1,0:T(8,128)(2,1)S(1)} %convert_element_type.23), channel_id=1, source_target_pairs={{0,2},{1,3},{2,0},{3,1},{4,6},{5,7},{6,4},{7,5},{8,10},{9,11},{10,... | collective-permute-start | bytes 405512 | tf_op jit(solution)/shard_map/ppermute | solution.py:21
  23.9 2.3 %collective-permute-start.14 = (bf16[512,128]{1,0:T(8,128)(2,1)S(1)}, bf16[512,128]{1,0:T(8,128)(2,1)S(1)}, u32[]{:S(2)}, u32[]{:S(2)}) collective-permute-start(bf16[512,128]{1,0:T(8,128)(2,1)S(1)} %shard_map.100.refs_0_.second), channel_id=1, source_target_pairs={{0,1},{1,0},{2,3},{3,2},{4,5},{5,4},{6,7},{7,6},{8,9},{9,8},{10,11... | collective-permute-start | bytes 393224 | tf_op jit(solution)/shard_map/ppermute | solution.py:21
  26.1 1.4 %collective-permute-start.12 = (bf16[512,128]{1,0:T(8,128)(2,1)S(1)}, bf16[512,128]{1,0:T(8,128)(2,1)S(1)}, u32[]{:S(2)}, u32[]{:S(2)}) collective-permute-start(bf16[512,128]{1,0:T(8,128)(2,1)S(1)} %shard_map.98.refs_2_), channel_id=1, source_target_pairs={{0,1},{1,0},{2,3},{3,2},{4,5},{5,4},{6,7},{7,6},{8,9},{9,8},{10,11... | collective-permute-start | bytes 393224 | tf_op jit(solution)/shard_map/ppermute | solution.py:21
  29.0 1.4 %collective-permute-start.15 = (bf16[528,128]{1,0:T(8,128)(2,1)S(1)}, bf16[528,128]{1,0:T(8,128)(2,1)S(1)}, u32[]{:S(2)}, u32[]{:S(2)}) collective-permute-start(bf16[528,128]{1,0:T(8,128)(2,1)S(1)} %get-tuple-element.133), channel_id=1, source_target_pairs={{0,1},{1,0},{2,3},{3,2},{4,5},{5,4},{6,7},{7,6},{8,9},{9,8},{10,11... | collective-permute-start | bytes 405512 | tf_op jit(solution)/shard_map/ppermute | solution.py:21
  29.3 2.9 %collective-permute-start.16 = (bf16[528,128]{1,0:T(8,128)(2,1)S(1)}, bf16[528,128]{1,0:T(8,128)(2,1)S(1)}, u32[]{:S(2)}, u32[]{:S(2)}) collective-permute-start(bf16[528,128]{1,0:T(8,128)(2,1)S(1)} %get-tuple-element.137), channel_id=1, source_target_pairs={{0,1},{1,0},{2,3},{3,2},{4,5},{5,4},{6,7},{7,6},{8,9},{9,8},{10,11... | collective-permute-start | bytes 405512 | tf_op jit(solution)/shard_map/ppermute | solution.py:21
  30.5 5.7 %collective-permute-start.17 = (bf16[528,128]{1,0:T(8,128)(2,1)S(1)}, bf16[528,128]{1,0:T(8,128)(2,1)S(1)}, u32[]{:S(2)}, u32[]{:S(2)}) collective-permute-start(bf16[528,128]{1,0:T(8,128)(2,1)S(1)} %convert_add_fusion.1), channel_id=1, source_target_pairs={{0,2},{1,3},{2,0},{3,1},{4,6},{5,7},{6,4},{7,5},{8,10},{9,11},{10,... | collective-permute-start | bytes 405512 | tf_op jit(solution)/shard_map/ppermute | solution.py:21

commit v7 on v6

--- a/solution.py
+++ b/solution.py
@@ -352,7 +352,7 @@
         [VM(a.shape, a.dtype) for a in (*smalls, w_gate, w_up, w_down)]
         + partial_outs + [wide_units],
         *x2_mine[1:], *cot_mine[1:], *smalls, w_gate, w_up, w_down,
-        flops=3 * product, far=range(2 * top - 2, 2 * top + 7),
+        flops=product // 2, far=range(2 * top - 2, 2 * top + 7),
         scratch=semaphores(6 + 2 * (wide // PIECE) + units // PIECE),
     )
     x2_own, cot_own, x1_own, gain, router, depths, *gate_up, down = outs[:9]

time: 37.2 us -> 35.9 us (0.965)
  waiting for transfers between devices: 9.4 us -> 7.73 us
  starting transfers between devices: 10.5 us -> 10.9 us
    ppermute x18, waiting for transfers between devices: 9.4 us -> 7.73 us  [hop(): return lax.ppermute(value, 'tensor', [(j, j ^ bit) for j in range(size)])]
    ppermute x18, starting transfers between devices: 10.5 us -> 10.9 us  [hop(): return lax.ppermute(value, 'tensor', [(j, j ^ bit) for j in range(size)])]
  transfers between devices with their start and end apart: 18 -> 18, of which waited for: 7 -> 6; matrix products, arithmetic and copies ran while one was open for 0% -> 0% of each run, Pallas kernels for 39% -> 40%
where the time goes in v7:
time: 35.9 us; the launch traced here: 35.8 us
  Pallas kernels  16.8 us (47%)
  starting transfers between devices  10.9 us (30%)
  waiting for transfers between devices  7.73 us (22%)
    pallas_call x16, Pallas kernels, kernel_call(): pl.pallas_call(kernel, out_shape=list(outs) if many else outs, in_specs=[...  16.8 us
    ppermute x18, starting transfers between devices, hop(): return lax.ppermute(value, 'tensor', [(j, j ^ bit) for j in range(size)])  10.9 us
    ppermute x18, waiting for transfers between devices, hop(): return lax.ppermute(value, 'tensor', [(j, j ^ bit) for j in range(size)])  7.73 us
  transfers between devices with their start and end apart: 18, of which 6 were waited for; matrix products, arithmetic and copies ran while one was open for 0% of the time, Pallas kernels for 40%

profile of v7, /device:TPU:0, one launch (start us, length us, event | category | flops | bytes accessed | tf_op | source)
XLA Modules:
  0.0 35.8 jit_solution(9664494491715948978)
XLA Ops:
  0.0 0.5 %collective-permute-start.2 = (bf16[128,512]{1,0:T(8,128)(2,1)}, bf16[128,512]{1,0:T(8,128)(2,1)S(1)}, u32[]{:S(2)}, u32[]{:S(2)}) collective-permute-start(bf16[128,512]{1,0:T(8,128)(2,1)} %refs_2_.1), channel_id=1, source_target_pairs={{0,1},{1,0},{2,3},{3,2},{4,5},{5,4},{6,7},{7,6},{8,9},{9,8},{10,11... | collective-permute-start | bytes 393224 | tf_op jit(solution)/shard_map/ppermute | solution.py:21
  0.5 3.0 %collective-permute-start.1 = (bf16[128,512]{1,0:T(8,128)(2,1)}, bf16[128,512]{1,0:T(8,128)(2,1)S(1)}, u32[]{:S(2)}, u32[]{:S(2)}) collective-permute-start(bf16[128,512]{1,0:T(8,128)(2,1)} %refs_2_.1), channel_id=1, source_target_pairs={{0,2},{1,3},{2,0},{3,1},{4,6},{5,7},{6,4},{7,5},{8,10},{9,11},{10,... | collective-permute-start | bytes 393224 | tf_op jit(solution)/shard_map/ppermute | solution.py:21
  3.5 5.0 %shard_map.91 = (bf16[128,512]{1,0:T(8,128)(2,1)S(1)}, bf16[128,512]{1,0:T(8,128)(2,1)S(1)}, bf16[128,512]{1,0:T(8,128)(2,1)S(1)}, f32[1,2048]{1,0:T(1,128)S(1)}...) custom-call(bf16[128,512]{1,0:T(8,128)(2,1)S(1)} %collective-permute, ...), custom_call_target="tpu_custom_call" | custom-call | flops 805306368 | tf_op jit(solution)/shard_map/pallas_call | solution.py:44
  8.7 0.5 %collective-permute-start.7 = (bf16[128,512]{1,0:T(8,128)(2,1)S(1)}, bf16[128,512]{1,0:T(8,128)(2,1)S(1)}, u32[]{:S(2)}, u32[]{:S(2)}) collective-permute-start(bf16[128,512]{1,0:T(8,128)(2,1)S(1)} %get-tuple-element.113.refs_0_), channel_id=1, source_target_pairs={{0,1},{1,0},{2,3},{3,2},{4,5},{5,4},{6,7},{7,6},{8,9},{9,8},{10,11... | collective-permute-start | bytes 393224 | tf_op jit(solution)/shard_map/ppermute | solution.py:21
  9.2 2.0 %collective-permute-start.8 = (bf16[128,512]{1,0:T(8,128)(2,1)S(1)}, bf16[128,512]{1,0:T(8,128)(2,1)S(1)}, u32[]{:S(2)}, u32[]{:S(2)}) collective-permute-start(bf16[128,512]{1,0:T(8,128)(2,1)S(1)} %get-tuple-element.113.refs_0_), channel_id=1, source_target_pairs={{0,2},{1,3},{2,0},{3,1},{4,6},{5,7},{6,4},{7,5},{8,10},{9,11},{10,... | collective-permute-start | bytes 393224 | tf_op jit(solution)/shard_map/ppermute | solution.py:21
  11.2 1.1 %shard_map.92 = (f32[1024,128]{1,0:T(8,128)S(1)}, f32[1024,128]{1,0:T(8,128)S(1)}, f32[1024,128]{1,0:T(8,128)S(1)}, f32[1024,128]{1,0:T(8,128)S(1)}, f32[8,128]{1,0:T(8,128)S(1)}) custom-call(bf16[128,512]{1,0:T(8,128)(2,1)S(1)} %collective-permute-done.1.refs_0_.refs_1_, bf16[128,512]{1,0:T(8,128)(2,1)S(1)} %collective-permute-done.5.refs_1_, ...), custom_call_target="tpu_custom_call" | custom-call | flops 3221225472 | tf_op jit(solution)/shard_map/pallas_call | solution.py:44
  12.3 0.2 collective-permute-done.4.refs_1_
  12.5 1.8 %shard_map.93 = (bf16[1024,128]{1,0:T(8,128)(2,1)S(1)}, bf16[1024,128]{1,0:T(8,128)(2,1)S(1)}, f32[16,128]{1,0:T(8,128)S(1)}, bf16[528,128]{1,0:T(8,128)(2,1)S(1)}, bf16[528,128]{1,0:T(8,128)(2,1)S(1)}) custom-call(bf16[128,512]{1,0:T(8,128)(2,1)S(1)} %collective-permute-done.refs_0_.second, bf16[128,512]{1,0:T(8,128)(2,1)S(1)} %collective-permute-done.4.refs_1_, ...), custom_call_target="tpu_custom_call" | custom-call | flops 3221225472 | tf_op jit(solution)/shard_map/pallas_call | solution.py:44
  14.3 0.4 collective-permute-start.6
  14.7 0.7 %shard_map.94 = f32[528,128]{1,0:T(8,128)S(1)} custom-call(bf16[1024,128]{1,0:T(8,128)(2,1)S(1)} %get-tuple-element.98.gg_ref, bf16[1024,128]{1,0:T(8,128)(2,1)S(1)} %get-tuple-element.99.gu_ref, f32[16,128]{1,0:T(8,128)S(1)} %get-tuple-element.100.sums_ref, bf16[2048,1024]{1,0:T(8,128)(2,1)S(1)} %get-tuple-element.81.refs_4_.refs_8_.gate_w.refs_6_.refs_7_, ...), custom_call_target="tpu_custom_call" | custom-call | flops 1610612736 | tf_op jit(solution)/shard_map/pallas_call | solution.py:44
  15.4 0.3 collective-permute-start.9
  15.7 0.3 collective-permute-start.10
  16.0 1.2 %collective-permute-start.13 = (bf16[528,128]{1,0:T(8,128)(2,1)S(1)}, bf16[528,128]{1,0:T(8,128)(2,1)S(1)}, u32[]{:S(2)}, u32[]{:S(2)}) collective-permute-start(bf16[528,128]{1,0:T(8,128)(2,1)S(1)} %get-tuple-element.143), channel_id=1, source_target_pairs={{0,2},{1,3},{2,0},{3,1},{4,6},{5,7},{6,4},{7,5},{8,10},{9,11},{10,... | collective-permute-start | bytes 405512 | tf_op jit(solution)/shard_map/ppermute | solution.py:21
  17.2 0.7 %shard_map.95 = f32[528,128]{1,0:T(8,128)S(1)} custom-call(bf16[1024,128]{1,0:T(8,128)(2,1)S(1)} %get-tuple-element.98.gg_ref, bf16[1024,128]{1,0:T(8,128)(2,1)S(1)} %get-tuple-element.99.gu_ref, f32[16,128]{1,0:T(8,128)S(1)} %get-tuple-element.100.sums_ref, bf16[2048,1024]{1,0:T(8,128)(2,1)S(1)} %get-tuple-element.81.refs_4_.refs_8_.gate_w.refs_6_.refs_7_, ...), custom_call_target="tpu_custom_call" | custom-call | flops 1610612736 | tf_op jit(solution)/shard_map/pallas_call | solution.py:44
  18.0 0.9 %collective-permute-start.11 = (bf16[528,128]{1,0:T(8,128)(2,1)S(1)}, bf16[528,128]{1,0:T(8,128)(2,1)S(1)}, u32[]{:S(2)}, u32[]{:S(2)}) collective-permute-start(bf16[528,128]{1,0:T(8,128)(2,1)S(1)} %convert_element_type.23), channel_id=1, source_target_pairs={{0,2},{1,3},{2,0},{3,1},{4,6},{5,7},{6,4},{7,5},{8,10},{9,11},{10,... | collective-permute-start | bytes 405512 | tf_op jit(solution)/shard_map/ppermute | solution.py:21
  19.0 0.4 %shard_map.97 = (f32[512,128]{1,0:T(8,128)S(1)}, f32[512,128]{1,0:T(8,128)S(1)}, f32[512,128]{1,0:T(8,128)S(1)}, f32[512,128]{1,0:T(8,128)S(1)}, f32[512,128]{1,0:T(8,128)S(1)}, /*index=5*/f32[512,128]{1,0:T(8,128)S(1)}) custom-call(bf16[128,512]{1,0:T(8,128)(2,1)S(1)} %get-tuple-element.108.refs_0_, ...), custom_call_target="tpu_custom_call" | custom-call | tf_op jit(solution)/shard_map/pallas_call | solution.py:44
  19.4 1.7 %shard_map.99 = (f32[1024,128]{1,0:T(8,128)S(1)}, f32[1024,128]{1,0:T(8,128)S(1)}, f32[1024,128]{1,0:T(8,128)S(1)}, f32[1024,128]{1,0:T(8,128)S(1)}, f32[8,128]{1,0:T(8,128)S(1)}) custom-call(bf16[128,512]{1,0:T(8,128)(2,1)S(1)} %get-tuple-element.113.refs_0_, bf16[128,512]{1,0:T(8,128)(2,1)S(1)} %collective-permute-done.7.refs_1_, ...), custom_call_target="tpu_custom_call" | custom-call | tf_op jit(solution)/shard_map/pallas_call | solution.py:44
  21.1 0.1 shard_map.96
  21.2 1.3 %collective-permute-done.13.got = bf16[528,128]{1,0:T(8,128)(2,1)S(1)} collective-permute-done((bf16[528,128]{1,0:T(8,128)(2,1)S(1)}, bf16[528,128]{1,0:T(8,128)(2,1)S(1)}, u32[]{:S(2)}, u32[]{:S(2)}) %collective-permute-start.13) | collective-permute-done | bytes 135200 | tf_op jit(solution)/shard_map/ppermute | solution.py:21
  22.7 2.0 %collective-permute-done.11.got = bf16[528,128]{1,0:T(8,128)(2,1)S(1)} collective-permute-done((bf16[528,128]{1,0:T(8,128)(2,1)S(1)}, bf16[528,128]{1,0:T(8,128)(2,1)S(1)}, u32[]{:S(2)}, u32[]{:S(2)}) %collective-permute-start.11) | collective-permute-done | bytes 135200 | tf_op jit(solution)/shard_map/ppermute | solution.py:21
  24.9 1.0 %shard_map.101.refs_2_ = f32[1024,128]{1,0:T(8,128)S(1)} custom-call(bf16[512,128]{1,0:T(8,128)(2,1)S(1)} %shard_map.100.refs_0_.second, bf16[512,128]{1,0:T(8,128)(2,1)S(1)} %collective-permute-done.14.refs_1_, bf16[512,128]{1,0:T(8,128)(2,1)S(1)} %shard_map.98.refs_2_, bf16[1024,2048]{1,0:T(8,128)(2,1)S(1)} %get-tuple-element.77.refs_2_.refs_3_.refs_1_), custom_call_target="tpu_custom_call" | custom-call | flops 1610612736 | tf_op jit(solution)/shard_map/pallas_call | solution.py:44
  25.9 0.3 collective-permute-done.12.refs_0_
  26.2 1.5 %shard_map.102 = (bf16[1024,128]{1,0:T(8,128)(2,1)S(1)}, bf16[1024,128]{1,0:T(8,128)(2,1)S(1)}, f32[16,128]{1,0:T(8,128)S(1)}, bf16[528,128]{1,0:T(8,128)(2,1)S(1)}, bf16[528,128]{1,0:T(8,128)(2,1)S(1)}) custom-call(bf16[512,128]{1,0:T(8,128)(2,1)S(1)} %collective-permute-done.12.refs_0_, bf16[1024,2048]{1,0:T(8,128)(2,1)S(1)} %get-tuple-element.77.refs_2_.refs_3_.refs_1_, ...), custom_call_target="tpu_custom_call" | custom-call | flops 3221225472 | tf_op jit(solution)/shard_map/pallas_call | solution.py:44
  27.8 0.2 collective-permute-start.15
  28.0 0.3 collective-permute-start.16
  28.3 0.7 %shard_map.103 = f32[528,128]{1,0:T(8,128)S(1)} custom-call(bf16[1024,128]{1,0:T(8,128)(2,1)S(1)} %get-tuple-element.134.gg_ref, bf16[1024,128]{1,0:T(8,128)(2,1)S(1)} %get-tuple-element.135.gu_ref, f32[16,128]{1,0:T(8,128)S(1)} %get-tuple-element.136.sums_ref, bf16[2048,1024]{1,0:T(8,128)(2,1)S(1)} %get-tuple-element.81.refs_4_.refs_8_.gate_w.refs_6_.refs_7_, ...), custom_call_target="tpu_custom_call" | custom-call | flops 1610612736 | tf_op jit(solution)/shard_map/pallas_call | solution.py:44
  29.0 0.1 collective-permute-done.15
  29.2 1.0 %collective-permute-start.17 = (bf16[528,128]{1,0:T(8,128)(2,1)S(1)}, bf16[528,128]{1,0:T(8,128)(2,1)S(1)}, u32[]{:S(2)}, u32[]{:S(2)}) collective-permute-start(bf16[528,128]{1,0:T(8,128)(2,1)S(1)} %convert_add_fusion.1), channel_id=1, source_target_pairs={{0,2},{1,3},{2,0},{3,1},{4,6},{5,7},{6,4},{7,5},{8,10},{9,11},{10,... | collective-permute-start | bytes 405512 | tf_op jit(solution)/shard_map/ppermute | solution.py:21
  30.2 0.7 %shard_map.104 = f32[528,128]{1,0:T(8,128)S(1)} custom-call(bf16[1024,128]{1,0:T(8,128)(2,1)S(1)} %get-tuple-element.134.gg_ref, bf16[1024,128]{1,0:T(8,128)(2,1)S(1)} %get-tuple-element.135.gu_ref, f32[16,128]{1,0:T(8,128)S(1)} %get-tuple-element.136.sums_ref, bf16[2048,1024]{1,0:T(8,128)(2,1)S(1)} %get-tuple-element.81.refs_4_.refs_8_.gate_w.refs_6_.refs_7_, ...), custom_call_target="tpu_custom_call" | custom-call | flops 1610612736 | tf_op jit(solution)/shard_map/pallas_call | solution.py:44
  31.0 0.2 shard_map.105
  31.2 3.7 %collective-permute-done.17.got = bf16[528,128]{1,0:T(8,128)(2,1)S(1)} collective-permute-done((bf16[528,128]{1,0:T(8,128)(2,1)S(1)}, bf16[528,128]{1,0:T(8,128)(2,1)S(1)}, u32[]{:S(2)}, u32[]{:S(2)}) %collective-permute-start.17) | collective-permute-done | bytes 135200 | tf_op jit(solution)/shard_map/ppermute | solution.py:21
  34.9 0.8 %shard_map.106 = bf16[128,512]{1,0:T(8,128)(2,1)} custom-call(f32[528,128]{1,0:T(8,128)S(1)} %convert_add_fusion.chip, bf16[528,128]{1,0:T(8,128)(2,1)S(1)} %collective-permute-done.17.got, bf16[512,128]{1,0:T(8,128)(2,1)S(1)} %shard_map.100.refs_0_.second, f32[512,128]{1,0:T(8,128)S(1)} %get-tuple-element.140.x, f32[512,128]{1,0:T(8,128)S(1)} %get-tuple-element.141.scale, ...), custom_call_target="tpu_custom_call" | custom-call | tf_op jit(solution)/shard_map/pallas_call | solution.py:44
  (25 shorter events, 0.7 us)
Async XLA Ops:
  0.0 3.5 %collective-permute-start.2 = (bf16[128,512]{1,0:T(8,128)(2,1)}, bf16[128,512]{1,0:T(8,128)(2,1)S(1)}, u32[]{:S(2)}, u32[]{:S(2)}) collective-permute-start(bf16[128,512]{1,0:T(8,128)(2,1)} %refs_2_.1), channel_id=1, source_target_pairs={{0,1},{1,0},{2,3},{3,2},{4,5},{5,4},{6,7},{7,6},{8,9},{9,8},{10,11... | collective-permute-start | bytes 393224 | tf_op jit(solution)/shard_map/ppermute | solution.py:21
  0.5 3.1 %collective-permute-start.3 = (bf16[128,512]{1,0:T(8,128)(2,1)}, bf16[128,512]{1,0:T(8,128)(2,1)S(1)}, u32[]{:S(2)}, u32[]{:S(2)}) collective-permute-start(bf16[128,512]{1,0:T(8,128)(2,1)} %refs_3_.1), channel_id=1, source_target_pairs={{0,1},{1,0},{2,3},{3,2},{4,5},{5,4},{6,7},{7,6},{8,9},{9,8},{10,11... | collective-permute-start | bytes 393224 | tf_op jit(solution)/shard_map/ppermute | solution.py:21
  0.5 8.1 %collective-permute-start.1 = (bf16[128,512]{1,0:T(8,128)(2,1)}, bf16[128,512]{1,0:T(8,128)(2,1)S(1)}, u32[]{:S(2)}, u32[]{:S(2)}) collective-permute-start(bf16[128,512]{1,0:T(8,128)(2,1)} %refs_2_.1), channel_id=1, source_target_pairs={{0,2},{1,3},{2,0},{3,1},{4,6},{5,7},{6,4},{7,5},{8,10},{9,11},{10,... | collective-permute-start | bytes 393224 | tf_op jit(solution)/shard_map/ppermute | solution.py:21
  3.5 7.7 %collective-permute-start = (bf16[128,512]{1,0:T(8,128)(2,1)}, bf16[128,512]{1,0:T(8,128)(2,1)S(1)}, u32[]{:S(2)}, u32[]{:S(2)}) collective-permute-start(bf16[128,512]{1,0:T(8,128)(2,1)} %refs_3_.1), channel_id=1, source_target_pairs={{0,2},{1,3},{2,0},{3,1},{4,6},{5,7},{6,4},{7,5},{8,10},{9,11},{10,... | collective-permute-start | bytes 393224 | tf_op jit(solution)/shard_map/ppermute | solution.py:21
  8.6 2.6 %collective-permute-start.5 = (bf16[128,512]{1,0:T(8,128)(2,1)S(1)}, bf16[128,512]{1,0:T(8,128)(2,1)S(1)}, u32[]{:S(2)}, u32[]{:S(2)}) collective-permute-start(bf16[128,512]{1,0:T(8,128)(2,1)S(1)} %collective-permute-done.1.refs_0_.refs_1_), channel_id=1, source_target_pairs={{0,1},{1,0},{2,3},{3,2},{4,5},{5,4},{6,7},{7,6},{8,9},{9,8},{10,11... | collective-permute-start | bytes 393224 | tf_op jit(solution)/shard_map/ppermute | solution.py:21
  8.7 9.4 %collective-permute-start.7 = (bf16[128,512]{1,0:T(8,128)(2,1)S(1)}, bf16[128,512]{1,0:T(8,128)(2,1)S(1)}, u32[]{:S(2)}, u32[]{:S(2)}) collective-permute-start(bf16[128,512]{1,0:T(8,128)(2,1)S(1)} %get-tuple-element.113.refs_0_), channel_id=1, source_target_pairs={{0,1},{1,0},{2,3},{3,2},{4,5},{5,4},{6,7},{7,6},{8,9},{9,8},{10,11... | collective-permute-start | bytes 393224 | tf_op jit(solution)/shard_map/ppermute | solution.py:21
  9.2 6.2 %collective-permute-start.8 = (bf16[128,512]{1,0:T(8,128)(2,1)S(1)}, bf16[128,512]{1,0:T(8,128)(2,1)S(1)}, u32[]{:S(2)}, u32[]{:S(2)}) collective-permute-start(bf16[128,512]{1,0:T(8,128)(2,1)S(1)} %get-tuple-element.113.refs_0_), channel_id=1, source_target_pairs={{0,2},{1,3},{2,0},{3,1},{4,6},{5,7},{6,4},{7,5},{8,10},{9,11},{10,... | collective-permute-start | bytes 393224 | tf_op jit(solution)/shard_map/ppermute | solution.py:21
  11.1 1.3 %collective-permute-start.4 = (bf16[128,512]{1,0:T(8,128)(2,1)S(1)}, bf16[128,512]{1,0:T(8,128)(2,1)S(1)}, u32[]{:S(2)}, u32[]{:S(2)}) collective-permute-start(bf16[128,512]{1,0:T(8,128)(2,1)S(1)} %collective-permute-done.refs_0_.second), channel_id=1, source_target_pairs={{0,1},{1,0},{2,3},{3,2},{4,5},{5,4},{6,7},{7,6},{8,9},{9,8},{10,11... | collective-permute-start | bytes 393224 | tf_op jit(solution)/shard_map/ppermute | solution.py:21
  14.3 1.7 %collective-permute-start.6 = (bf16[528,128]{1,0:T(8,128)(2,1)S(1)}, bf16[528,128]{1,0:T(8,128)(2,1)S(1)}, u32[]{:S(2)}, u32[]{:S(2)}) collective-permute-start(bf16[528,128]{1,0:T(8,128)(2,1)S(1)} %get-tuple-element.93), channel_id=1, source_target_pairs={{0,1},{1,0},{2,3},{3,2},{4,5},{5,4},{6,7},{7,6},{8,9},{9,8},{10,11... | collective-permute-start | bytes 405512 | tf_op jit(solution)/shard_map/ppermute | solution.py:21
  15.4 2.6 %collective-permute-start.9 = (bf16[128,512]{1,0:T(8,128)(2,1)S(1)}, bf16[128,512]{1,0:T(8,128)(2,1)S(1)}, u32[]{:S(2)}, u32[]{:S(2)}) collective-permute-start(bf16[128,512]{1,0:T(8,128)(2,1)S(1)} %collective-permute-done.8.refs_2_), channel_id=1, source_target_pairs={{0,1},{1,0},{2,3},{3,2},{4,5},{5,4},{6,7},{7,6},{8,9},{9,8},{10,11... | collective-permute-start | bytes 393224 | tf_op jit(solution)/shard_map/ppermute | solution.py:21
  15.7 2.3 %collective-permute-start.10 = (bf16[528,128]{1,0:T(8,128)(2,1)S(1)}, bf16[528,128]{1,0:T(8,128)(2,1)S(1)}, u32[]{:S(2)}, u32[]{:S(2)}) collective-permute-start(bf16[528,128]{1,0:T(8,128)(2,1)S(1)} %get-tuple-element.101), channel_id=1, source_target_pairs={{0,1},{1,0},{2,3},{3,2},{4,5},{5,4},{6,7},{7,6},{8,9},{9,8},{10,11... | collective-permute-start | bytes 405512 | tf_op jit(solution)/shard_map/ppermute | solution.py:21
  16.0 6.5 %collective-permute-start.13 = (bf16[528,128]{1,0:T(8,128)(2,1)S(1)}, bf16[528,128]{1,0:T(8,128)(2,1)S(1)}, u32[]{:S(2)}, u32[]{:S(2)}) collective-permute-start(bf16[528,128]{1,0:T(8,128)(2,1)S(1)} %get-tuple-element.143), channel_id=1, source_target_pairs={{0,2},{1,3},{2,0},{3,1},{4,6},{5,7},{6,4},{7,5},{8,10},{9,11},{10,... | collective-permute-start | bytes 405512 | tf_op jit(solution)/shard_map/ppermute | solution.py:21
  18.0 6.6 %collective-permute-start.11 = (bf16[528,128]{1,0:T(8,128)(2,1)S(1)}, bf16[528,128]{1,0:T(8,128)(2,1)S(1)}, u32[]{:S(2)}, u32[]{:S(2)}) collective-permute-start(bf16[528,128]{1,0:T(8,128)(2,1)S(1)} %convert_element_type.23), channel_id=1, source_target_pairs={{0,2},{1,3},{2,0},{3,1},{4,6},{5,7},{6,4},{7,5},{8,10},{9,11},{10,... | collective-permute-start | bytes 405512 | tf_op jit(solution)/shard_map/ppermute | solution.py:21
  22.6 2.3 %collective-permute-start.14 = (bf16[512,128]{1,0:T(8,128)(2,1)S(1)}, bf16[512,128]{1,0:T(8,128)(2,1)S(1)}, u32[]{:S(2)}, u32[]{:S(2)}) collective-permute-start(bf16[512,128]{1,0:T(8,128)(2,1)S(1)} %shard_map.100.refs_0_.second), channel_id=1, source_target_pairs={{0,1},{1,0},{2,3},{3,2},{4,5},{5,4},{6,7},{7,6},{8,9},{9,8},{10,11... | collective-permute-start | bytes 393224 | tf_op jit(solution)/shard_map/ppermute | solution.py:21
  24.8 1.4 %collective-permute-start.12 = (bf16[512,128]{1,0:T(8,128)(2,1)S(1)}, bf16[512,128]{1,0:T(8,128)(2,1)S(1)}, u32[]{:S(2)}, u32[]{:S(2)}) collective-permute-start(bf16[512,128]{1,0:T(8,128)(2,1)S(1)} %shard_map.98.refs_2_), channel_id=1, source_target_pairs={{0,1},{1,0},{2,3},{3,2},{4,5},{5,4},{6,7},{7,6},{8,9},{9,8},{10,11... | collective-permute-start | bytes 393224 | tf_op jit(solution)/shard_map/ppermute | solution.py:21
  27.8 1.4 %collective-permute-start.15 = (bf16[528,128]{1,0:T(8,128)(2,1)S(1)}, bf16[528,128]{1,0:T(8,128)(2,1)S(1)}, u32[]{:S(2)}, u32[]{:S(2)}) collective-permute-start(bf16[528,128]{1,0:T(8,128)(2,1)S(1)} %get-tuple-element.133), channel_id=1, source_target_pairs={{0,1},{1,0},{2,3},{3,2},{4,5},{5,4},{6,7},{7,6},{8,9},{9,8},{10,11... | collective-permute-start | bytes 405512 | tf_op jit(solution)/shard_map/ppermute | solution.py:21
  28.0 2.9 %collective-permute-start.16 = (bf16[528,128]{1,0:T(8,128)(2,1)S(1)}, bf16[528,128]{1,0:T(8,128)(2,1)S(1)}, u32[]{:S(2)}, u32[]{:S(2)}) collective-permute-start(bf16[528,128]{1,0:T(8,128)(2,1)S(1)} %get-tuple-element.137), channel_id=1, source_target_pairs={{0,1},{1,0},{2,3},{3,2},{4,5},{5,4},{6,7},{7,6},{8,9},{9,8},{10,11... | collective-permute-start | bytes 405512 | tf_op jit(solution)/shard_map/ppermute | solution.py:21
  29.2 5.7 %collective-permute-start.17 = (bf16[528,128]{1,0:T(8,128)(2,1)S(1)}, bf16[528,128]{1,0:T(8,128)(2,1)S(1)}, u32[]{:S(2)}, u32[]{:S(2)}) collective-permute-start(bf16[528,128]{1,0:T(8,128)(2,1)S(1)} %convert_add_fusion.1), channel_id=1, source_target_pairs={{0,2},{1,3},{2,0},{3,1},{4,6},{5,7},{6,4},{7,5},{8,10},{9,11},{10,... | collective-permute-start | bytes 405512 | tf_op jit(solution)/shard_map/ppermute | solution.py:21

commit v8 on v7

--- a/solution.py
+++ b/solution.py
@@ -33,7 +33,7 @@
     return [parts[key] for key in range(len(parts))]
 
 
-def kernel_call(kernel, outs, *args, flops=0, far=(), scratch=()):
+def kernel_call(kernel, outs, *args, flops=0, far=(), scratch=(), out_far=False):
     many = isinstance(outs, (list, tuple))
     args = [
         pltpu.with_memory_space_constraint(a, pltpu.HBM) if n in far else a
@@ -45,7 +45,7 @@
         kernel,
         out_shape=list(outs) if many else outs,
         in_specs=[away if n in far else near for n in range(len(args))],
-        out_specs=[near] * len(outs) if many else near,
+        out_specs=[near] * len(outs) if many else away if out_far else near,
         scratch_shapes=list(scratch),
         compiler_params=pltpu.CompilerParams(vmem_limit_bytes=8 * 2**20),
         cost_estimate=pl.CostEstimate(flops=6 * flops, bytes_accessed=0, transcendentals=0),
@@ -284,14 +284,22 @@
     out_ref[...] = (cot[...].astype(F32) + delta).astype(out_ref.dtype)
 
 
-def last_kernel(wide, chip, got, second, x, scale, router, rows_ref, out_ref):
-    feat = out_ref.shape[1]
-    total = chip[...] + got[...].astype(F32)
-    coef, logit = row_factors(total[feat : feat + 2, :], rows_ref[...], wide)
-    delta = scale[...] * total[0:feat, :] - x[...] * coef + router[...] * logit
-    result = second[...].astype(F32) + delta
-    for k in range(0, feat, LANES):
-        out_ref[:, k : k + LANES] = result[k : k + LANES, :].T.astype(out_ref.dtype)
+def last_kernel(wide, chip, got, second, x, scale, router, rows_ref, out_far, near, sems):
+    feat = near.shape[1]
+    sums = chip[feat : feat + 2, :] + got[feat : feat + 2, :].astype(F32)
+    coef, logit = row_factors(sums, rows_ref[...], wide)
+    copies = []
+    for n, k in enumerate(range(0, feat, LANES)):
+        rows = slice(k, k + LANES)
+        total = chip[rows, :] + got[rows, :].astype(F32)
+        delta = scale[rows, :] * total - x[rows, :] * coef + router[rows, :] * logit
+        result = second[rows, :].astype(F32) + delta
+        near[:, rows] = result.T.astype(near.dtype)
+        copy = pltpu.make_async_copy(near.at[:, rows], out_far.at[:, rows], sems.at[n])
+        copy.start()
+        copies.append(copy)
+    for copy in copies:
+        copy.wait()
 
 
 def body(hidden_first, hidden_second, cotangent, depths, norm_gain, router, w_gate, w_up, w_down):
@@ -373,7 +381,6 @@
     got_mine = hop(chip_theirs.astype(BF16), top)
     *grads, chip_theirs = lax.optimization_barrier((*grads, chip_theirs))
     chip_mine, _ = reduce(0, grads, to_mine)
-    x1_mine, x1_theirs, chip_mine = lax.optimization_barrier((x1_mine, x1_theirs, chip_mine))
 
     rows2, chip_mine = lax.optimization_barrier((rows2, chip_mine))
     columns2 = kernel_call(
@@ -420,6 +427,7 @@
         functools.partial(last_kernel, wide),
         jax.ShapeDtypeStruct((tokens, feat), BF16),
         chip_mine, got, own_second, *columns1, rows1,
+        scratch=[VM((tokens, feat), BF16)] + semaphores(feat // LANES), out_far=True,
     )
 
 

time: 35.9 us -> 35.9 us (level)
  no operation moved by 1% of the time
where the time goes in v8:
time: 35.9 us; the launch traced here: 35.8 us
  Pallas kernels  16.8 us (47%)
  starting transfers between devices  10.9 us (30%)
  waiting for transfers between devices  7.74 us (22%)
    pallas_call x16, Pallas kernels, kernel_call(): pl.pallas_call(kernel, out_shape=list(outs) if many else outs, in_specs=[...  16.8 us
    ppermute x18, starting transfers between devices, hop(): return lax.ppermute(value, 'tensor', [(j, j ^ bit) for j in range(size)])  10.9 us
    ppermute x18, waiting for transfers between devices, hop(): return lax.ppermute(value, 'tensor', [(j, j ^ bit) for j in range(size)])  7.74 us
  transfers between devices with their start and end apart: 18, of which 6 were waited for; matrix products, arithmetic and copies ran while one was open for 0% of the time, Pallas kernels for 40%

profile of v8, /device:TPU:0, one launch (start us, length us, event | category | flops | bytes accessed | tf_op | source)
XLA Modules:
  0.0 35.8 jit_solution(16324659305071599314)
XLA Ops:
  0.0 0.5 %collective-permute-start.2 = (bf16[128,512]{1,0:T(8,128)(2,1)}, bf16[128,512]{1,0:T(8,128)(2,1)S(1)}, u32[]{:S(2)}, u32[]{:S(2)}) collective-permute-start(bf16[128,512]{1,0:T(8,128)(2,1)} %refs_2_.1), channel_id=1, source_target_pairs={{0,1},{1,0},{2,3},{3,2},{4,5},{5,4},{6,7},{7,6},{8,9},{9,8},{10,11... | collective-permute-start | bytes 393224 | tf_op jit(solution)/shard_map/ppermute | solution.py:21
  0.5 3.0 %collective-permute-start.1 = (bf16[128,512]{1,0:T(8,128)(2,1)}, bf16[128,512]{1,0:T(8,128)(2,1)S(1)}, u32[]{:S(2)}, u32[]{:S(2)}) collective-permute-start(bf16[128,512]{1,0:T(8,128)(2,1)} %refs_2_.1), channel_id=1, source_target_pairs={{0,2},{1,3},{2,0},{3,1},{4,6},{5,7},{6,4},{7,5},{8,10},{9,11},{10,... | collective-permute-start | bytes 393224 | tf_op jit(solution)/shard_map/ppermute | solution.py:21
  3.5 5.0 %shard_map.91 = (bf16[128,512]{1,0:T(8,128)(2,1)S(1)}, bf16[128,512]{1,0:T(8,128)(2,1)S(1)}, bf16[128,512]{1,0:T(8,128)(2,1)S(1)}, f32[1,2048]{1,0:T(1,128)S(1)}...) custom-call(bf16[128,512]{1,0:T(8,128)(2,1)S(1)} %collective-permute, ...), custom_call_target="tpu_custom_call" | custom-call | flops 805306368 | tf_op jit(solution)/shard_map/pallas_call | solution.py:44
  8.7 0.5 %collective-permute-start.11 = (bf16[128,512]{1,0:T(8,128)(2,1)S(1)}, bf16[128,512]{1,0:T(8,128)(2,1)S(1)}, u32[]{:S(2)}, u32[]{:S(2)}) collective-permute-start(bf16[128,512]{1,0:T(8,128)(2,1)S(1)} %get-tuple-element.105.refs_0_), channel_id=1, source_target_pairs={{0,1},{1,0},{2,3},{3,2},{4,5},{5,4},{6,7},{7,6},{8,9},{9,8},{10,11... | collective-permute-start | bytes 393224 | tf_op jit(solution)/shard_map/ppermute | solution.py:21
  9.2 2.0 %collective-permute-start.12 = (bf16[128,512]{1,0:T(8,128)(2,1)S(1)}, bf16[128,512]{1,0:T(8,128)(2,1)S(1)}, u32[]{:S(2)}, u32[]{:S(2)}) collective-permute-start(bf16[128,512]{1,0:T(8,128)(2,1)S(1)} %get-tuple-element.105.refs_0_), channel_id=1, source_target_pairs={{0,2},{1,3},{2,0},{3,1},{4,6},{5,7},{6,4},{7,5},{8,10},{9,11},{10,... | collective-permute-start | bytes 393224 | tf_op jit(solution)/shard_map/ppermute | solution.py:21
  11.2 1.1 %shard_map.92 = (f32[1024,128]{1,0:T(8,128)S(1)}, f32[1024,128]{1,0:T(8,128)S(1)}, f32[1024,128]{1,0:T(8,128)S(1)}, f32[1024,128]{1,0:T(8,128)S(1)}, f32[8,128]{1,0:T(8,128)S(1)}) custom-call(bf16[128,512]{1,0:T(8,128)(2,1)S(1)} %collective-permute-done.1.refs_0_.refs_1_, bf16[128,512]{1,0:T(8,128)(2,1)S(1)} %collective-permute-done.5.refs_1_, ...), custom_call_target="tpu_custom_call" | custom-call | flops 3221225472 | tf_op jit(solution)/shard_map/pallas_call | solution.py:44
  12.3 0.2 collective-permute-done.4.refs_1_
  12.5 1.8 %shard_map.93 = (bf16[1024,128]{1,0:T(8,128)(2,1)S(1)}, bf16[1024,128]{1,0:T(8,128)(2,1)S(1)}, f32[16,128]{1,0:T(8,128)S(1)}, bf16[528,128]{1,0:T(8,128)(2,1)S(1)}, bf16[528,128]{1,0:T(8,128)(2,1)S(1)}) custom-call(bf16[128,512]{1,0:T(8,128)(2,1)S(1)} %collective-permute-done.refs_0_.second, bf16[128,512]{1,0:T(8,128)(2,1)S(1)} %collective-permute-done.4.refs_1_, ...), custom_call_target="tpu_custom_call" | custom-call | flops 3221225472 | tf_op jit(solution)/shard_map/pallas_call | solution.py:44
  14.3 0.4 collective-permute-start.6
  14.7 0.2 collective-permute-start.7
  14.9 0.7 %shard_map.94 = f32[528,128]{1,0:T(8,128)S(1)} custom-call(bf16[1024,128]{1,0:T(8,128)(2,1)S(1)} %get-tuple-element.91.gg_ref, bf16[1024,128]{1,0:T(8,128)(2,1)S(1)} %get-tuple-element.92.gu_ref, f32[16,128]{1,0:T(8,128)S(1)} %get-tuple-element.93.sums_ref, bf16[2048,1024]{1,0:T(8,128)(2,1)S(1)} %get-tuple-element.76.refs_4_.refs_8_.gate_w.refs_6_.refs_7_, ...), custom_call_target="tpu_custom_call" | custom-call | flops 1610612736 | tf_op jit(solution)/shard_map/pallas_call | solution.py:44
  15.6 0.4 collective-permute-start.13
  16.0 0.8 %collective-permute-start.10 = (bf16[528,128]{1,0:T(8,128)(2,1)S(1)}, bf16[528,128]{1,0:T(8,128)(2,1)S(1)}, u32[]{:S(2)}, u32[]{:S(2)}) collective-permute-start(bf16[528,128]{1,0:T(8,128)(2,1)S(1)} %get-tuple-element.133), channel_id=1, source_target_pairs={{0,2},{1,3},{2,0},{3,1},{4,6},{5,7},{6,4},{7,5},{8,10},{9,11},{10,... | collective-permute-start | bytes 405512 | tf_op jit(solution)/shard_map/ppermute | solution.py:21
  16.8 0.7 %shard_map.95 = f32[528,128]{1,0:T(8,128)S(1)} custom-call(bf16[1024,128]{1,0:T(8,128)(2,1)S(1)} %get-tuple-element.91.gg_ref, bf16[1024,128]{1,0:T(8,128)(2,1)S(1)} %get-tuple-element.92.gu_ref, f32[16,128]{1,0:T(8,128)S(1)} %get-tuple-element.93.sums_ref, bf16[2048,1024]{1,0:T(8,128)(2,1)S(1)} %get-tuple-element.76.refs_4_.refs_8_.gate_w.refs_6_.refs_7_, ...), custom_call_target="tpu_custom_call" | custom-call | flops 1610612736 | tf_op jit(solution)/shard_map/pallas_call | solution.py:44
  17.6 1.3 %collective-permute-start.8 = (bf16[528,128]{1,0:T(8,128)(2,1)S(1)}, bf16[528,128]{1,0:T(8,128)(2,1)S(1)}, u32[]{:S(2)}, u32[]{:S(2)}) collective-permute-start(bf16[528,128]{1,0:T(8,128)(2,1)S(1)} %convert_element_type.23), channel_id=1, source_target_pairs={{0,2},{1,3},{2,0},{3,1},{4,6},{5,7},{6,4},{7,5},{8,10},{9,11},{10,... | collective-permute-start | bytes 405512 | tf_op jit(solution)/shard_map/ppermute | solution.py:21
  19.0 1.7 %shard_map.99 = (f32[1024,128]{1,0:T(8,128)S(1)}, f32[1024,128]{1,0:T(8,128)S(1)}, f32[1024,128]{1,0:T(8,128)S(1)}, f32[1024,128]{1,0:T(8,128)S(1)}, f32[8,128]{1,0:T(8,128)S(1)}) custom-call(bf16[128,512]{1,0:T(8,128)(2,1)S(1)} %get-tuple-element.105.refs_0_, bf16[128,512]{1,0:T(8,128)(2,1)S(1)} %collective-permute-done.11.refs_1_, ...), custom_call_target="tpu_custom_call" | custom-call | tf_op jit(solution)/shard_map/pallas_call | solution.py:44
  20.6 0.4 %shard_map.97 = (f32[512,128]{1,0:T(8,128)S(1)}, f32[512,128]{1,0:T(8,128)S(1)}, f32[512,128]{1,0:T(8,128)S(1)}, f32[512,128]{1,0:T(8,128)S(1)}, f32[512,128]{1,0:T(8,128)S(1)}, /*index=5*/f32[512,128]{1,0:T(8,128)S(1)}) custom-call(bf16[128,512]{1,0:T(8,128)(2,1)S(1)} %get-tuple-element.100.refs_0_, ...), custom_call_target="tpu_custom_call" | custom-call | tf_op jit(solution)/shard_map/pallas_call | solution.py:44
  21.0 0.1 shard_map.96
  21.2 1.3 %collective-permute-done.10.got = bf16[528,128]{1,0:T(8,128)(2,1)S(1)} collective-permute-done((bf16[528,128]{1,0:T(8,128)(2,1)S(1)}, bf16[528,128]{1,0:T(8,128)(2,1)S(1)}, u32[]{:S(2)}, u32[]{:S(2)}) %collective-permute-start.10) | collective-permute-done | bytes 135200 | tf_op jit(solution)/shard_map/ppermute | solution.py:21
  22.7 2.0 %collective-permute-done.8.got = bf16[528,128]{1,0:T(8,128)(2,1)S(1)} collective-permute-done((bf16[528,128]{1,0:T(8,128)(2,1)S(1)}, bf16[528,128]{1,0:T(8,128)(2,1)S(1)}, u32[]{:S(2)}, u32[]{:S(2)}) %collective-permute-start.8) | collective-permute-done | bytes 135200 | tf_op jit(solution)/shard_map/ppermute | solution.py:21
  24.9 1.0 %shard_map.101.refs_2_ = f32[1024,128]{1,0:T(8,128)S(1)} custom-call(bf16[512,128]{1,0:T(8,128)(2,1)S(1)} %shard_map.100.refs_0_.second, bf16[512,128]{1,0:T(8,128)(2,1)S(1)} %collective-permute-done.14.refs_1_, bf16[512,128]{1,0:T(8,128)(2,1)S(1)} %shard_map.98.refs_2_, bf16[1024,2048]{1,0:T(8,128)(2,1)S(1)} %get-tuple-element.72.refs_2_.refs_3_.refs_1_), custom_call_target="tpu_custom_call" | custom-call | flops 1610612736 | tf_op jit(solution)/shard_map/pallas_call | solution.py:44
  25.9 0.3 collective-permute-done.9.refs_0_
  26.2 1.5 %shard_map.102 = (bf16[1024,128]{1,0:T(8,128)(2,1)S(1)}, bf16[1024,128]{1,0:T(8,128)(2,1)S(1)}, f32[16,128]{1,0:T(8,128)S(1)}, bf16[528,128]{1,0:T(8,128)(2,1)S(1)}, bf16[528,128]{1,0:T(8,128)(2,1)S(1)}) custom-call(bf16[512,128]{1,0:T(8,128)(2,1)S(1)} %collective-permute-done.9.refs_0_, bf16[1024,2048]{1,0:T(8,128)(2,1)S(1)} %get-tuple-element.72.refs_2_.refs_3_.refs_1_, ...), custom_call_target="tpu_custom_call" | custom-call | flops 3221225472 | tf_op jit(solution)/shard_map/pallas_call | solution.py:44
  27.7 0.2 collective-permute-start.15
  28.0 0.3 collective-permute-start.16
  28.3 0.7 %shard_map.103 = f32[528,128]{1,0:T(8,128)S(1)} custom-call(bf16[1024,128]{1,0:T(8,128)(2,1)S(1)} %get-tuple-element.124.gg_ref, bf16[1024,128]{1,0:T(8,128)(2,1)S(1)} %get-tuple-element.125.gu_ref, f32[16,128]{1,0:T(8,128)S(1)} %get-tuple-element.126.sums_ref, bf16[2048,1024]{1,0:T(8,128)(2,1)S(1)} %get-tuple-element.76.refs_4_.refs_8_.gate_w.refs_6_.refs_7_, ...), custom_call_target="tpu_custom_call" | custom-call | flops 1610612736 | tf_op jit(solution)/shard_map/pallas_call | solution.py:44
  29.0 0.1 collective-permute-done.15
  29.2 1.0 %collective-permute-start.17 = (bf16[528,128]{1,0:T(8,128)(2,1)S(1)}, bf16[528,128]{1,0:T(8,128)(2,1)S(1)}, u32[]{:S(2)}, u32[]{:S(2)}) collective-permute-start(bf16[528,128]{1,0:T(8,128)(2,1)S(1)} %convert_add_fusion.1), channel_id=1, source_target_pairs={{0,2},{1,3},{2,0},{3,1},{4,6},{5,7},{6,4},{7,5},{8,10},{9,11},{10,... | collective-permute-start | bytes 405512 | tf_op jit(solution)/shard_map/ppermute | solution.py:21
  30.2 0.7 %shard_map.104 = f32[528,128]{1,0:T(8,128)S(1)} custom-call(bf16[1024,128]{1,0:T(8,128)(2,1)S(1)} %get-tuple-element.124.gg_ref, bf16[1024,128]{1,0:T(8,128)(2,1)S(1)} %get-tuple-element.125.gu_ref, f32[16,128]{1,0:T(8,128)S(1)} %get-tuple-element.126.sums_ref, bf16[2048,1024]{1,0:T(8,128)(2,1)S(1)} %get-tuple-element.76.refs_4_.refs_8_.gate_w.refs_6_.refs_7_, ...), custom_call_target="tpu_custom_call" | custom-call | flops 1610612736 | tf_op jit(solution)/shard_map/pallas_call | solution.py:44
  31.0 0.2 shard_map.105
  31.2 3.7 %collective-permute-done.17.got = bf16[528,128]{1,0:T(8,128)(2,1)S(1)} collective-permute-done((bf16[528,128]{1,0:T(8,128)(2,1)S(1)}, bf16[528,128]{1,0:T(8,128)(2,1)S(1)}, u32[]{:S(2)}, u32[]{:S(2)}) %collective-permute-start.17) | collective-permute-done | bytes 135200 | tf_op jit(solution)/shard_map/ppermute | solution.py:21
  34.9 0.8 %shard_map.106 = bf16[128,512]{1,0:T(8,128)(2,1)} custom-call(f32[528,128]{1,0:T(8,128)S(1)} %convert_add_fusion.chip, bf16[528,128]{1,0:T(8,128)(2,1)S(1)} %collective-permute-done.17.got, bf16[512,128]{1,0:T(8,128)(2,1)S(1)} %shard_map.100.refs_0_.second, f32[512,128]{1,0:T(8,128)S(1)} %get-tuple-element.130.x, f32[512,128]{1,0:T(8,128)S(1)} %get-tuple-element.131.scale, ...), custom_call_target="tpu_custom_call" | custom-call | tf_op jit(solution)/shard_map/pallas_call | solution.py:44
  (25 shorter events, 0.7 us)
Async XLA Ops:
  0.0 3.5 %collective-permute-start.2 = (bf16[128,512]{1,0:T(8,128)(2,1)}, bf16[128,512]{1,0:T(8,128)(2,1)S(1)}, u32[]{:S(2)}, u32[]{:S(2)}) collective-permute-start(bf16[128,512]{1,0:T(8,128)(2,1)} %refs_2_.1), channel_id=1, source_target_pairs={{0,1},{1,0},{2,3},{3,2},{4,5},{5,4},{6,7},{7,6},{8,9},{9,8},{10,11... | collective-permute-start | bytes 393224 | tf_op jit(solution)/shard_map/ppermute | solution.py:21
  0.5 3.1 %collective-permute-start.3 = (bf16[128,512]{1,0:T(8,128)(2,1)}, bf16[128,512]{1,0:T(8,128)(2,1)S(1)}, u32[]{:S(2)}, u32[]{:S(2)}) collective-permute-start(bf16[128,512]{1,0:T(8,128)(2,1)} %refs_3_.1), channel_id=1, source_target_pairs={{0,1},{1,0},{2,3},{3,2},{4,5},{5,4},{6,7},{7,6},{8,9},{9,8},{10,11... | collective-permute-start | bytes 393224 | tf_op jit(solution)/shard_map/ppermute | solution.py:21
  0.5 8.1 %collective-permute-start.1 = (bf16[128,512]{1,0:T(8,128)(2,1)}, bf16[128,512]{1,0:T(8,128)(2,1)S(1)}, u32[]{:S(2)}, u32[]{:S(2)}) collective-permute-start(bf16[128,512]{1,0:T(8,128)(2,1)} %refs_2_.1), channel_id=1, source_target_pairs={{0,2},{1,3},{2,0},{3,1},{4,6},{5,7},{6,4},{7,5},{8,10},{9,11},{10,... | collective-permute-start | bytes 393224 | tf_op jit(solution)/shard_map/ppermute | solution.py:21
  3.5 7.7 %collective-permute-start = (bf16[128,512]{1,0:T(8,128)(2,1)}, bf16[128,512]{1,0:T(8,128)(2,1)S(1)}, u32[]{:S(2)}, u32[]{:S(2)}) collective-permute-start(bf16[128,512]{1,0:T(8,128)(2,1)} %refs_3_.1), channel_id=1, source_target_pairs={{0,2},{1,3},{2,0},{3,1},{4,6},{5,7},{6,4},{7,5},{8,10},{9,11},{10,... | collective-permute-start | bytes 393224 | tf_op jit(solution)/shard_map/ppermute | solution.py:21
  8.6 2.6 %collective-permute-start.5 = (bf16[128,512]{1,0:T(8,128)(2,1)S(1)}, bf16[128,512]{1,0:T(8,128)(2,1)S(1)}, u32[]{:S(2)}, u32[]{:S(2)}) collective-permute-start(bf16[128,512]{1,0:T(8,128)(2,1)S(1)} %collective-permute-done.1.refs_0_.refs_1_), channel_id=1, source_target_pairs={{0,1},{1,0},{2,3},{3,2},{4,5},{5,4},{6,7},{7,6},{8,9},{9,8},{10,11... | collective-permute-start | bytes 393224 | tf_op jit(solution)/shard_map/ppermute | solution.py:21
  8.7 10.3 %collective-permute-start.11 = (bf16[128,512]{1,0:T(8,128)(2,1)S(1)}, bf16[128,512]{1,0:T(8,128)(2,1)S(1)}, u32[]{:S(2)}, u32[]{:S(2)}) collective-permute-start(bf16[128,512]{1,0:T(8,128)(2,1)S(1)} %get-tuple-element.105.refs_0_), channel_id=1, source_target_pairs={{0,1},{1,0},{2,3},{3,2},{4,5},{5,4},{6,7},{7,6},{8,9},{9,8},{10,11... | collective-permute-start | bytes 393224 | tf_op jit(solution)/shard_map/ppermute | solution.py:21
  9.2 6.5 %collective-permute-start.12 = (bf16[128,512]{1,0:T(8,128)(2,1)S(1)}, bf16[128,512]{1,0:T(8,128)(2,1)S(1)}, u32[]{:S(2)}, u32[]{:S(2)}) collective-permute-start(bf16[128,512]{1,0:T(8,128)(2,1)S(1)} %get-tuple-element.105.refs_0_), channel_id=1, source_target_pairs={{0,2},{1,3},{2,0},{3,1},{4,6},{5,7},{6,4},{7,5},{8,10},{9,11},{10,... | collective-permute-start | bytes 393224 | tf_op jit(solution)/shard_map/ppermute | solution.py:21
  11.1 1.3 %collective-permute-start.4 = (bf16[128,512]{1,0:T(8,128)(2,1)S(1)}, bf16[128,512]{1,0:T(8,128)(2,1)S(1)}, u32[]{:S(2)}, u32[]{:S(2)}) collective-permute-start(bf16[128,512]{1,0:T(8,128)(2,1)S(1)} %collective-permute-done.refs_0_.second), channel_id=1, source_target_pairs={{0,1},{1,0},{2,3},{3,2},{4,5},{5,4},{6,7},{7,6},{8,9},{9,8},{10,11... | collective-permute-start | bytes 393224 | tf_op jit(solution)/shard_map/ppermute | solution.py:21
  14.3 1.7 %collective-permute-start.6 = (bf16[528,128]{1,0:T(8,128)(2,1)S(1)}, bf16[528,128]{1,0:T(8,128)(2,1)S(1)}, u32[]{:S(2)}, u32[]{:S(2)}) collective-permute-start(bf16[528,128]{1,0:T(8,128)(2,1)S(1)} %get-tuple-element.88), channel_id=1, source_target_pairs={{0,1},{1,0},{2,3},{3,2},{4,5},{5,4},{6,7},{7,6},{8,9},{9,8},{10,11... | collective-permute-start | bytes 405512 | tf_op jit(solution)/shard_map/ppermute | solution.py:21
  14.7 2.9 %collective-permute-start.7 = (bf16[528,128]{1,0:T(8,128)(2,1)S(1)}, bf16[528,128]{1,0:T(8,128)(2,1)S(1)}, u32[]{:S(2)}, u32[]{:S(2)}) collective-permute-start(bf16[528,128]{1,0:T(8,128)(2,1)S(1)} %get-tuple-element.94), channel_id=1, source_target_pairs={{0,1},{1,0},{2,3},{3,2},{4,5},{5,4},{6,7},{7,6},{8,9},{9,8},{10,11... | collective-permute-start | bytes 405512 | tf_op jit(solution)/shard_map/ppermute | solution.py:21
  15.6 3.3 %collective-permute-start.13 = (bf16[128,512]{1,0:T(8,128)(2,1)S(1)}, bf16[128,512]{1,0:T(8,128)(2,1)S(1)}, u32[]{:S(2)}, u32[]{:S(2)}) collective-permute-start(bf16[128,512]{1,0:T(8,128)(2,1)S(1)} %collective-permute-done.12.refs_2_), channel_id=1, source_target_pairs={{0,1},{1,0},{2,3},{3,2},{4,5},{5,4},{6,7},{7,6},{8,9},{9,8},{10,11... | collective-permute-start | bytes 393224 | tf_op jit(solution)/shard_map/ppermute | solution.py:21
  16.0 6.5 %collective-permute-start.10 = (bf16[528,128]{1,0:T(8,128)(2,1)S(1)}, bf16[528,128]{1,0:T(8,128)(2,1)S(1)}, u32[]{:S(2)}, u32[]{:S(2)}) collective-permute-start(bf16[528,128]{1,0:T(8,128)(2,1)S(1)} %get-tuple-element.133), channel_id=1, source_target_pairs={{0,2},{1,3},{2,0},{3,1},{4,6},{5,7},{6,4},{7,5},{8,10},{9,11},{10,... | collective-permute-start | bytes 405512 | tf_op jit(solution)/shard_map/ppermute | solution.py:21
  17.6 7.1 %collective-permute-start.8 = (bf16[528,128]{1,0:T(8,128)(2,1)S(1)}, bf16[528,128]{1,0:T(8,128)(2,1)S(1)}, u32[]{:S(2)}, u32[]{:S(2)}) collective-permute-start(bf16[528,128]{1,0:T(8,128)(2,1)S(1)} %convert_element_type.23), channel_id=1, source_target_pairs={{0,2},{1,3},{2,0},{3,1},{4,6},{5,7},{6,4},{7,5},{8,10},{9,11},{10,... | collective-permute-start | bytes 405512 | tf_op jit(solution)/shard_map/ppermute | solution.py:21
  22.6 2.3 %collective-permute-start.14 = (bf16[512,128]{1,0:T(8,128)(2,1)S(1)}, bf16[512,128]{1,0:T(8,128)(2,1)S(1)}, u32[]{:S(2)}, u32[]{:S(2)}) collective-permute-start(bf16[512,128]{1,0:T(8,128)(2,1)S(1)} %shard_map.100.refs_0_.second), channel_id=1, source_target_pairs={{0,1},{1,0},{2,3},{3,2},{4,5},{5,4},{6,7},{7,6},{8,9},{9,8},{10,11... | collective-permute-start | bytes 393224 | tf_op jit(solution)/shard_map/ppermute | solution.py:21
  24.8 1.4 %collective-permute-start.9 = (bf16[512,128]{1,0:T(8,128)(2,1)S(1)}, bf16[512,128]{1,0:T(8,128)(2,1)S(1)}, u32[]{:S(2)}, u32[]{:S(2)}) collective-permute-start(bf16[512,128]{1,0:T(8,128)(2,1)S(1)} %shard_map.98.refs_2_), channel_id=1, source_target_pairs={{0,1},{1,0},{2,3},{3,2},{4,5},{5,4},{6,7},{7,6},{8,9},{9,8},{10,11... | collective-permute-start | bytes 393224 | tf_op jit(solution)/shard_map/ppermute | solution.py:21
  27.7 1.4 %collective-permute-start.15 = (bf16[528,128]{1,0:T(8,128)(2,1)S(1)}, bf16[528,128]{1,0:T(8,128)(2,1)S(1)}, u32[]{:S(2)}, u32[]{:S(2)}) collective-permute-start(bf16[528,128]{1,0:T(8,128)(2,1)S(1)} %get-tuple-element.123), channel_id=1, source_target_pairs={{0,1},{1,0},{2,3},{3,2},{4,5},{5,4},{6,7},{7,6},{8,9},{9,8},{10,11... | collective-permute-start | bytes 405512 | tf_op jit(solution)/shard_map/ppermute | solution.py:21
  28.0 3.0 %collective-permute-start.16 = (bf16[528,128]{1,0:T(8,128)(2,1)S(1)}, bf16[528,128]{1,0:T(8,128)(2,1)S(1)}, u32[]{:S(2)}, u32[]{:S(2)}) collective-permute-start(bf16[528,128]{1,0:T(8,128)(2,1)S(1)} %get-tuple-element.127), channel_id=1, source_target_pairs={{0,1},{1,0},{2,3},{3,2},{4,5},{5,4},{6,7},{7,6},{8,9},{9,8},{10,11... | collective-permute-start | bytes 405512 | tf_op jit(solution)/shard_map/ppermute | solution.py:21
  29.2 5.7 %collective-permute-start.17 = (bf16[528,128]{1,0:T(8,128)(2,1)S(1)}, bf16[528,128]{1,0:T(8,128)(2,1)S(1)}, u32[]{:S(2)}, u32[]{:S(2)}) collective-permute-start(bf16[528,128]{1,0:T(8,128)(2,1)S(1)} %convert_add_fusion.1), channel_id=1, source_target_pairs={{0,2},{1,3},{2,0},{3,1},{4,6},{5,7},{6,4},{7,5},{8,10},{9,11},{10,... | collective-permute-start | bytes 405512 | tf_op jit(solution)/shard_map/ppermute | solution.py:21

commit v9 on v8

--- a/solution.py
+++ b/solution.py
@@ -377,10 +377,11 @@
     grads, to_theirs, to_mine = back_call(across, True, cot_theirs, back_mine, factors2)
     chip_theirs, part = reduce(top, grads, to_theirs)
     x1_cross, part = lax.optimization_barrier((x1_cross, part))
-    x1_mine, x1_theirs = spread(x1_own, low), spread(x1_cross, low)
+    x1_mine = spread(x1_own, low)
     got_mine = hop(chip_theirs.astype(BF16), top)
     *grads, chip_theirs = lax.optimization_barrier((*grads, chip_theirs))
-    chip_mine, _ = reduce(0, grads, to_mine)
+    chip_mine, part = reduce(0, grads, to_mine)
+    x1_theirs = spread(after(x1_cross, part), low)
 
     rows2, chip_mine = lax.optimization_barrier((rows2, chip_mine))
     columns2 = kernel_call(

time: 35.9 us -> 35.8 us (level)
  starting transfers between devices: 10.9 us -> 10.4 us
    ppermute x18, starting transfers between devices: 10.9 us -> 10.4 us  [hop(): return lax.ppermute(value, 'tensor', [(j, j ^ bit) for j in range(size)])]
  transfers between devices with their start and end apart: 18 -> 18, of which waited for: 6 -> 7; matrix products, arithmetic and copies ran while one was open for 0% -> 0% of each run, Pallas kernels for 40% -> 41%
where the time goes in v9:
time: 35.8 us; the launch traced here: 35.6 us
  Pallas kernels  16.8 us (47%)
  starting transfers between devices  10.4 us (29%)
  waiting for transfers between devices  8.03 us (22%)
    pallas_call x16, Pallas kernels, kernel_call(): pl.pallas_call(kernel, out_shape=list(outs) if many else outs, in_specs=[...  16.8 us
    ppermute x18, starting transfers between devices, hop(): return lax.ppermute(value, 'tensor', [(j, j ^ bit) for j in range(size)])  10.4 us
    ppermute x18, waiting for transfers between devices, hop(): return lax.ppermute(value, 'tensor', [(j, j ^ bit) for j in range(size)])  8.03 us
  transfers between devices with their start and end apart: 18, of which 7 were waited for; matrix products, arithmetic and copies ran while one was open for 0% of the time, Pallas kernels for 41%

profile of v9, /device:TPU:0, one launch (start us, length us, event | category | flops | bytes accessed | tf_op | source)
XLA Modules:
  0.0 35.6 jit_solution(16406882277962829149)
XLA Ops:
  0.0 0.5 %collective-permute-start.2 = (bf16[128,512]{1,0:T(8,128)(2,1)}, bf16[128,512]{1,0:T(8,128)(2,1)S(1)}, u32[]{:S(2)}, u32[]{:S(2)}) collective-permute-start(bf16[128,512]{1,0:T(8,128)(2,1)} %refs_2_.1), channel_id=1, source_target_pairs={{0,1},{1,0},{2,3},{3,2},{4,5},{5,4},{6,7},{7,6},{8,9},{9,8},{10,11... | collective-permute-start | bytes 393224 | tf_op jit(solution)/shard_map/ppermute | solution.py:21
  0.5 3.0 %collective-permute-start.1 = (bf16[128,512]{1,0:T(8,128)(2,1)}, bf16[128,512]{1,0:T(8,128)(2,1)S(1)}, u32[]{:S(2)}, u32[]{:S(2)}) collective-permute-start(bf16[128,512]{1,0:T(8,128)(2,1)} %refs_2_.1), channel_id=1, source_target_pairs={{0,2},{1,3},{2,0},{3,1},{4,6},{5,7},{6,4},{7,5},{8,10},{9,11},{10,... | collective-permute-start | bytes 393224 | tf_op jit(solution)/shard_map/ppermute | solution.py:21
  3.5 5.0 %shard_map.91 = (bf16[128,512]{1,0:T(8,128)(2,1)S(1)}, bf16[128,512]{1,0:T(8,128)(2,1)S(1)}, bf16[128,512]{1,0:T(8,128)(2,1)S(1)}, f32[1,2048]{1,0:T(1,128)S(1)}...) custom-call(bf16[128,512]{1,0:T(8,128)(2,1)S(1)} %collective-permute, ...), custom_call_target="tpu_custom_call" | custom-call | flops 805306368 | tf_op jit(solution)/shard_map/pallas_call | solution.py:44
  8.7 0.5 %collective-permute-start.11 = (bf16[128,512]{1,0:T(8,128)(2,1)S(1)}, bf16[128,512]{1,0:T(8,128)(2,1)S(1)}, u32[]{:S(2)}, u32[]{:S(2)}) collective-permute-start(bf16[128,512]{1,0:T(8,128)(2,1)S(1)} %get-tuple-element.106.refs_0_), channel_id=1, source_target_pairs={{0,1},{1,0},{2,3},{3,2},{4,5},{5,4},{6,7},{7,6},{8,9},{9,8},{10,11... | collective-permute-start | bytes 393224 | tf_op jit(solution)/shard_map/ppermute | solution.py:21
  9.2 2.0 %collective-permute-start.12 = (bf16[128,512]{1,0:T(8,128)(2,1)S(1)}, bf16[128,512]{1,0:T(8,128)(2,1)S(1)}, u32[]{:S(2)}, u32[]{:S(2)}) collective-permute-start(bf16[128,512]{1,0:T(8,128)(2,1)S(1)} %get-tuple-element.106.refs_0_), channel_id=1, source_target_pairs={{0,2},{1,3},{2,0},{3,1},{4,6},{5,7},{6,4},{7,5},{8,10},{9,11},{10,... | collective-permute-start | bytes 393224 | tf_op jit(solution)/shard_map/ppermute | solution.py:21
  11.2 1.1 %shard_map.92 = (f32[1024,128]{1,0:T(8,128)S(1)}, f32[1024,128]{1,0:T(8,128)S(1)}, f32[1024,128]{1,0:T(8,128)S(1)}, f32[1024,128]{1,0:T(8,128)S(1)}, f32[8,128]{1,0:T(8,128)S(1)}) custom-call(bf16[128,512]{1,0:T(8,128)(2,1)S(1)} %collective-permute-done.1.refs_0_.refs_1_, bf16[128,512]{1,0:T(8,128)(2,1)S(1)} %collective-permute-done.5.refs_1_, ...), custom_call_target="tpu_custom_call" | custom-call | flops 3221225472 | tf_op jit(solution)/shard_map/pallas_call | solution.py:44
  12.3 0.2 collective-permute-done.4.refs_1_
  12.5 1.8 %shard_map.93 = (bf16[1024,128]{1,0:T(8,128)(2,1)S(1)}, bf16[1024,128]{1,0:T(8,128)(2,1)S(1)}, f32[16,128]{1,0:T(8,128)S(1)}, bf16[528,128]{1,0:T(8,128)(2,1)S(1)}, bf16[528,128]{1,0:T(8,128)(2,1)S(1)}) custom-call(bf16[128,512]{1,0:T(8,128)(2,1)S(1)} %collective-permute-done.refs_0_.second, bf16[128,512]{1,0:T(8,128)(2,1)S(1)} %collective-permute-done.4.refs_1_, ...), custom_call_target="tpu_custom_call" | custom-call | flops 3221225472 | tf_op jit(solution)/shard_map/pallas_call | solution.py:44
  14.3 0.4 %collective-permute-start.6 = (bf16[528,128]{1,0:T(8,128)(2,1)S(1)}, bf16[528,128]{1,0:T(8,128)(2,1)S(1)}, u32[]{:S(2)}, u32[]{:S(2)}) collective-permute-start(bf16[528,128]{1,0:T(8,128)(2,1)S(1)} %get-tuple-element.89), channel_id=1, source_target_pairs={{0,1},{1,0},{2,3},{3,2},{4,5},{5,4},{6,7},{7,6},{8,9},{9,8},{10,11... | collective-permute-start | bytes 405512 | tf_op jit(solution)/shard_map/ppermute | solution.py:21
  14.7 0.2 collective-permute-start.7
  14.9 0.7 %shard_map.94 = f32[528,128]{1,0:T(8,128)S(1)} custom-call(bf16[1024,128]{1,0:T(8,128)(2,1)S(1)} %get-tuple-element.92.gg_ref, bf16[1024,128]{1,0:T(8,128)(2,1)S(1)} %get-tuple-element.93.gu_ref, f32[16,128]{1,0:T(8,128)S(1)} %get-tuple-element.94.sums_ref, bf16[2048,1024]{1,0:T(8,128)(2,1)S(1)} %get-tuple-element.77.refs_4_.refs_8_.gate_w.refs_6_.refs_7_, ...), custom_call_target="tpu_custom_call" | custom-call | flops 1610612736 | tf_op jit(solution)/shard_map/pallas_call | solution.py:44
  15.8 1.0 %collective-permute-start.10 = (bf16[528,128]{1,0:T(8,128)(2,1)S(1)}, bf16[528,128]{1,0:T(8,128)(2,1)S(1)}, u32[]{:S(2)}, u32[]{:S(2)}) collective-permute-start(bf16[528,128]{1,0:T(8,128)(2,1)S(1)} %get-tuple-element.135), channel_id=1, source_target_pairs={{0,2},{1,3},{2,0},{3,1},{4,6},{5,7},{6,4},{7,5},{8,10},{9,11},{10,... | collective-permute-start | bytes 405512 | tf_op jit(solution)/shard_map/ppermute | solution.py:21
  16.7 0.7 %shard_map.95 = f32[528,128]{1,0:T(8,128)S(1)} custom-call(bf16[1024,128]{1,0:T(8,128)(2,1)S(1)} %get-tuple-element.92.gg_ref, bf16[1024,128]{1,0:T(8,128)(2,1)S(1)} %get-tuple-element.93.gu_ref, f32[16,128]{1,0:T(8,128)S(1)} %get-tuple-element.94.sums_ref, bf16[2048,1024]{1,0:T(8,128)(2,1)S(1)} %get-tuple-element.77.refs_4_.refs_8_.gate_w.refs_6_.refs_7_, ...), custom_call_target="tpu_custom_call" | custom-call | flops 1610612736 | tf_op jit(solution)/shard_map/pallas_call | solution.py:44
  17.6 1.2 %collective-permute-start.8 = (bf16[528,128]{1,0:T(8,128)(2,1)S(1)}, bf16[528,128]{1,0:T(8,128)(2,1)S(1)}, u32[]{:S(2)}, u32[]{:S(2)}) collective-permute-start(bf16[528,128]{1,0:T(8,128)(2,1)S(1)} %convert_element_type.23), channel_id=1, source_target_pairs={{0,2},{1,3},{2,0},{3,1},{4,6},{5,7},{6,4},{7,5},{8,10},{9,11},{10,... | collective-permute-start | bytes 405512 | tf_op jit(solution)/shard_map/ppermute | solution.py:21
  18.8 0.4 %shard_map.97 = (f32[512,128]{1,0:T(8,128)S(1)}, f32[512,128]{1,0:T(8,128)S(1)}, f32[512,128]{1,0:T(8,128)S(1)}, f32[512,128]{1,0:T(8,128)S(1)}, f32[512,128]{1,0:T(8,128)S(1)}, /*index=5*/f32[512,128]{1,0:T(8,128)S(1)}) custom-call(bf16[128,512]{1,0:T(8,128)(2,1)S(1)} %get-tuple-element.101.refs_0_, ...), custom_call_target="tpu_custom_call" | custom-call | tf_op jit(solution)/shard_map/pallas_call | solution.py:44
  19.2 0.1 shard_map.96
  19.4 1.7 %shard_map.99 = (f32[1024,128]{1,0:T(8,128)S(1)}, f32[1024,128]{1,0:T(8,128)S(1)}, f32[1024,128]{1,0:T(8,128)S(1)}, f32[1024,128]{1,0:T(8,128)S(1)}, f32[8,128]{1,0:T(8,128)S(1)}) custom-call(bf16[128,512]{1,0:T(8,128)(2,1)S(1)} %get-tuple-element.106.refs_0_, bf16[128,512]{1,0:T(8,128)(2,1)S(1)} %collective-permute-done.11.refs_1_, ...), custom_call_target="tpu_custom_call" | custom-call | tf_op jit(solution)/shard_map/pallas_call | solution.py:44
  21.0 1.2 %collective-permute-done.10.got = bf16[528,128]{1,0:T(8,128)(2,1)S(1)} collective-permute-done((bf16[528,128]{1,0:T(8,128)(2,1)S(1)}, bf16[528,128]{1,0:T(8,128)(2,1)S(1)}, u32[]{:S(2)}, u32[]{:S(2)}) %collective-permute-start.10) | collective-permute-done | bytes 135200 | tf_op jit(solution)/shard_map/ppermute | solution.py:21
  22.3 0.1 shard_map.100.refs_0_.second
  22.5 2.1 %collective-permute-done.8.got = bf16[528,128]{1,0:T(8,128)(2,1)S(1)} collective-permute-done((bf16[528,128]{1,0:T(8,128)(2,1)S(1)}, bf16[528,128]{1,0:T(8,128)(2,1)S(1)}, u32[]{:S(2)}, u32[]{:S(2)}) %collective-permute-start.8) | collective-permute-done | bytes 135200 | tf_op jit(solution)/shard_map/ppermute | solution.py:21
  24.7 1.0 %shard_map.101.refs_2_ = f32[1024,128]{1,0:T(8,128)S(1)} custom-call(bf16[512,128]{1,0:T(8,128)(2,1)S(1)} %shard_map.100.refs_0_.second, bf16[512,128]{1,0:T(8,128)(2,1)S(1)} %collective-permute-done.14.refs_1_, bf16[512,128]{1,0:T(8,128)(2,1)S(1)} %shard_map.98.refs_2_, bf16[1024,2048]{1,0:T(8,128)(2,1)S(1)} %get-tuple-element.73.refs_2_.refs_3_.refs_1_), custom_call_target="tpu_custom_call" | custom-call | flops 1610612736 | tf_op jit(solution)/shard_map/pallas_call | solution.py:44
  25.7 0.3 collective-permute-done.9.refs_0_
  26.1 1.5 %shard_map.102 = (bf16[1024,128]{1,0:T(8,128)(2,1)S(1)}, bf16[1024,128]{1,0:T(8,128)(2,1)S(1)}, f32[16,128]{1,0:T(8,128)S(1)}, bf16[528,128]{1,0:T(8,128)(2,1)S(1)}, bf16[528,128]{1,0:T(8,128)(2,1)S(1)}) custom-call(bf16[512,128]{1,0:T(8,128)(2,1)S(1)} %collective-permute-done.9.refs_0_, bf16[1024,2048]{1,0:T(8,128)(2,1)S(1)} %get-tuple-element.73.refs_2_.refs_3_.refs_1_, ...), custom_call_target="tpu_custom_call" | custom-call | flops 3221225472 | tf_op jit(solution)/shard_map/pallas_call | solution.py:44
  27.6 0.2 collective-permute-start.15
  27.8 0.3 collective-permute-start.16
  28.2 0.7 %shard_map.103 = f32[528,128]{1,0:T(8,128)S(1)} custom-call(bf16[1024,128]{1,0:T(8,128)(2,1)S(1)} %get-tuple-element.126.gg_ref, bf16[1024,128]{1,0:T(8,128)(2,1)S(1)} %get-tuple-element.127.gu_ref, f32[16,128]{1,0:T(8,128)S(1)} %get-tuple-element.128.sums_ref, bf16[2048,1024]{1,0:T(8,128)(2,1)S(1)} %get-tuple-element.77.refs_4_.refs_8_.gate_w.refs_6_.refs_7_, ...), custom_call_target="tpu_custom_call" | custom-call | flops 1610612736 | tf_op jit(solution)/shard_map/pallas_call | solution.py:44
  28.9 0.1 collective-permute-done.15
  29.0 0.8 %collective-permute-start.17 = (bf16[528,128]{1,0:T(8,128)(2,1)S(1)}, bf16[528,128]{1,0:T(8,128)(2,1)S(1)}, u32[]{:S(2)}, u32[]{:S(2)}) collective-permute-start(bf16[528,128]{1,0:T(8,128)(2,1)S(1)} %convert_add_fusion.1), channel_id=1, source_target_pairs={{0,2},{1,3},{2,0},{3,1},{4,6},{5,7},{6,4},{7,5},{8,10},{9,11},{10,... | collective-permute-start | bytes 405512 | tf_op jit(solution)/shard_map/ppermute | solution.py:21
  29.9 0.7 %shard_map.104 = f32[528,128]{1,0:T(8,128)S(1)} custom-call(bf16[1024,128]{1,0:T(8,128)(2,1)S(1)} %get-tuple-element.126.gg_ref, bf16[1024,128]{1,0:T(8,128)(2,1)S(1)} %get-tuple-element.127.gu_ref, f32[16,128]{1,0:T(8,128)S(1)} %get-tuple-element.128.sums_ref, bf16[2048,1024]{1,0:T(8,128)(2,1)S(1)} %get-tuple-element.77.refs_4_.refs_8_.gate_w.refs_6_.refs_7_, ...), custom_call_target="tpu_custom_call" | custom-call | flops 1610612736 | tf_op jit(solution)/shard_map/pallas_call | solution.py:44
  30.6 0.2 shard_map.105
  30.9 3.9 %collective-permute-done.17.got = bf16[528,128]{1,0:T(8,128)(2,1)S(1)} collective-permute-done((bf16[528,128]{1,0:T(8,128)(2,1)S(1)}, bf16[528,128]{1,0:T(8,128)(2,1)S(1)}, u32[]{:S(2)}, u32[]{:S(2)}) %collective-permute-start.17) | collective-permute-done | bytes 135200 | tf_op jit(solution)/shard_map/ppermute | solution.py:21
  34.8 0.8 %shard_map.106 = bf16[128,512]{1,0:T(8,128)(2,1)} custom-call(f32[528,128]{1,0:T(8,128)S(1)} %convert_add_fusion.chip, bf16[528,128]{1,0:T(8,128)(2,1)S(1)} %collective-permute-done.17.got, bf16[512,128]{1,0:T(8,128)(2,1)S(1)} %shard_map.100.refs_0_.second, f32[512,128]{1,0:T(8,128)S(1)} %get-tuple-element.132.x, f32[512,128]{1,0:T(8,128)S(1)} %get-tuple-element.133.scale, ...), custom_call_target="tpu_custom_call" | custom-call | tf_op jit(solution)/shard_map/pallas_call | solution.py:44
  (25 shorter events, 0.8 us)
Async XLA Ops:
  0.0 3.5 %collective-permute-start.2 = (bf16[128,512]{1,0:T(8,128)(2,1)}, bf16[128,512]{1,0:T(8,128)(2,1)S(1)}, u32[]{:S(2)}, u32[]{:S(2)}) collective-permute-start(bf16[128,512]{1,0:T(8,128)(2,1)} %refs_2_.1), channel_id=1, source_target_pairs={{0,1},{1,0},{2,3},{3,2},{4,5},{5,4},{6,7},{7,6},{8,9},{9,8},{10,11... | collective-permute-start | bytes 393224 | tf_op jit(solution)/shard_map/ppermute | solution.py:21
  0.5 3.1 %collective-permute-start.3 = (bf16[128,512]{1,0:T(8,128)(2,1)}, bf16[128,512]{1,0:T(8,128)(2,1)S(1)}, u32[]{:S(2)}, u32[]{:S(2)}) collective-permute-start(bf16[128,512]{1,0:T(8,128)(2,1)} %refs_3_.1), channel_id=1, source_target_pairs={{0,1},{1,0},{2,3},{3,2},{4,5},{5,4},{6,7},{7,6},{8,9},{9,8},{10,11... | collective-permute-start | bytes 393224 | tf_op jit(solution)/shard_map/ppermute | solution.py:21
  0.5 8.1 %collective-permute-start.1 = (bf16[128,512]{1,0:T(8,128)(2,1)}, bf16[128,512]{1,0:T(8,128)(2,1)S(1)}, u32[]{:S(2)}, u32[]{:S(2)}) collective-permute-start(bf16[128,512]{1,0:T(8,128)(2,1)} %refs_2_.1), channel_id=1, source_target_pairs={{0,2},{1,3},{2,0},{3,1},{4,6},{5,7},{6,4},{7,5},{8,10},{9,11},{10,... | collective-permute-start | bytes 393224 | tf_op jit(solution)/shard_map/ppermute | solution.py:21
  3.5 7.7 %collective-permute-start = (bf16[128,512]{1,0:T(8,128)(2,1)}, bf16[128,512]{1,0:T(8,128)(2,1)S(1)}, u32[]{:S(2)}, u32[]{:S(2)}) collective-permute-start(bf16[128,512]{1,0:T(8,128)(2,1)} %refs_3_.1), channel_id=1, source_target_pairs={{0,2},{1,3},{2,0},{3,1},{4,6},{5,7},{6,4},{7,5},{8,10},{9,11},{10,... | collective-permute-start | bytes 393224 | tf_op jit(solution)/shard_map/ppermute | solution.py:21
  8.6 2.6 %collective-permute-start.5 = (bf16[128,512]{1,0:T(8,128)(2,1)S(1)}, bf16[128,512]{1,0:T(8,128)(2,1)S(1)}, u32[]{:S(2)}, u32[]{:S(2)}) collective-permute-start(bf16[128,512]{1,0:T(8,128)(2,1)S(1)} %collective-permute-done.1.refs_0_.refs_1_), channel_id=1, source_target_pairs={{0,1},{1,0},{2,3},{3,2},{4,5},{5,4},{6,7},{7,6},{8,9},{9,8},{10,11... | collective-permute-start | bytes 393224 | tf_op jit(solution)/shard_map/ppermute | solution.py:21
  8.7 10.7 %collective-permute-start.11 = (bf16[128,512]{1,0:T(8,128)(2,1)S(1)}, bf16[128,512]{1,0:T(8,128)(2,1)S(1)}, u32[]{:S(2)}, u32[]{:S(2)}) collective-permute-start(bf16[128,512]{1,0:T(8,128)(2,1)S(1)} %get-tuple-element.106.refs_0_), channel_id=1, source_target_pairs={{0,1},{1,0},{2,3},{3,2},{4,5},{5,4},{6,7},{7,6},{8,9},{9,8},{10,11... | collective-permute-start | bytes 393224 | tf_op jit(solution)/shard_map/ppermute | solution.py:21
  9.2 6.5 %collective-permute-start.12 = (bf16[128,512]{1,0:T(8,128)(2,1)S(1)}, bf16[128,512]{1,0:T(8,128)(2,1)S(1)}, u32[]{:S(2)}, u32[]{:S(2)}) collective-permute-start(bf16[128,512]{1,0:T(8,128)(2,1)S(1)} %get-tuple-element.106.refs_0_), channel_id=1, source_target_pairs={{0,2},{1,3},{2,0},{3,1},{4,6},{5,7},{6,4},{7,5},{8,10},{9,11},{10,... | collective-permute-start | bytes 393224 | tf_op jit(solution)/shard_map/ppermute | solution.py:21
  11.1 1.3 %collective-permute-start.4 = (bf16[128,512]{1,0:T(8,128)(2,1)S(1)}, bf16[128,512]{1,0:T(8,128)(2,1)S(1)}, u32[]{:S(2)}, u32[]{:S(2)}) collective-permute-start(bf16[128,512]{1,0:T(8,128)(2,1)S(1)} %collective-permute-done.refs_0_.second), channel_id=1, source_target_pairs={{0,1},{1,0},{2,3},{3,2},{4,5},{5,4},{6,7},{7,6},{8,9},{9,8},{10,11... | collective-permute-start | bytes 393224 | tf_op jit(solution)/shard_map/ppermute | solution.py:21
  14.3 1.4 %collective-permute-start.6 = (bf16[528,128]{1,0:T(8,128)(2,1)S(1)}, bf16[528,128]{1,0:T(8,128)(2,1)S(1)}, u32[]{:S(2)}, u32[]{:S(2)}) collective-permute-start(bf16[528,128]{1,0:T(8,128)(2,1)S(1)} %get-tuple-element.89), channel_id=1, source_target_pairs={{0,1},{1,0},{2,3},{3,2},{4,5},{5,4},{6,7},{7,6},{8,9},{9,8},{10,11... | collective-permute-start | bytes 405512 | tf_op jit(solution)/shard_map/ppermute | solution.py:21
  14.7 2.9 %collective-permute-start.7 = (bf16[528,128]{1,0:T(8,128)(2,1)S(1)}, bf16[528,128]{1,0:T(8,128)(2,1)S(1)}, u32[]{:S(2)}, u32[]{:S(2)}) collective-permute-start(bf16[528,128]{1,0:T(8,128)(2,1)S(1)} %get-tuple-element.95), channel_id=1, source_target_pairs={{0,1},{1,0},{2,3},{3,2},{4,5},{5,4},{6,7},{7,6},{8,9},{9,8},{10,11... | collective-permute-start | bytes 405512 | tf_op jit(solution)/shard_map/ppermute | solution.py:21
  15.8 6.5 %collective-permute-start.10 = (bf16[528,128]{1,0:T(8,128)(2,1)S(1)}, bf16[528,128]{1,0:T(8,128)(2,1)S(1)}, u32[]{:S(2)}, u32[]{:S(2)}) collective-permute-start(bf16[528,128]{1,0:T(8,128)(2,1)S(1)} %get-tuple-element.135), channel_id=1, source_target_pairs={{0,2},{1,3},{2,0},{3,1},{4,6},{5,7},{6,4},{7,5},{8,10},{9,11},{10,... | collective-permute-start | bytes 405512 | tf_op jit(solution)/shard_map/ppermute | solution.py:21
  17.4 1.9 %collective-permute-start.13 = (bf16[128,512]{1,0:T(8,128)(2,1)S(1)}, bf16[128,512]{1,0:T(8,128)(2,1)S(1)}, u32[]{:S(2)}, u32[]{:S(2)}) collective-permute-start(bf16[128,512]{1,0:T(8,128)(2,1)S(1)} %collective-permute-done.12.refs_2_), channel_id=1, source_target_pairs={{0,1},{1,0},{2,3},{3,2},{4,5},{5,4},{6,7},{7,6},{8,9},{9,8},{10,11... | collective-permute-start | bytes 393224 | tf_op jit(solution)/shard_map/ppermute | solution.py:21
  17.6 6.9 %collective-permute-start.8 = (bf16[528,128]{1,0:T(8,128)(2,1)S(1)}, bf16[528,128]{1,0:T(8,128)(2,1)S(1)}, u32[]{:S(2)}, u32[]{:S(2)}) collective-permute-start(bf16[528,128]{1,0:T(8,128)(2,1)S(1)} %convert_element_type.23), channel_id=1, source_target_pairs={{0,2},{1,3},{2,0},{3,1},{4,6},{5,7},{6,4},{7,5},{8,10},{9,11},{10,... | collective-permute-start | bytes 405512 | tf_op jit(solution)/shard_map/ppermute | solution.py:21
  22.4 2.3 %collective-permute-start.14 = (bf16[512,128]{1,0:T(8,128)(2,1)S(1)}, bf16[512,128]{1,0:T(8,128)(2,1)S(1)}, u32[]{:S(2)}, u32[]{:S(2)}) collective-permute-start(bf16[512,128]{1,0:T(8,128)(2,1)S(1)} %shard_map.100.refs_0_.second), channel_id=1, source_target_pairs={{0,1},{1,0},{2,3},{3,2},{4,5},{5,4},{6,7},{7,6},{8,9},{9,8},{10,11... | collective-permute-start | bytes 393224 | tf_op jit(solution)/shard_map/ppermute | solution.py:21
  24.6 1.4 %collective-permute-start.9 = (bf16[512,128]{1,0:T(8,128)(2,1)S(1)}, bf16[512,128]{1,0:T(8,128)(2,1)S(1)}, u32[]{:S(2)}, u32[]{:S(2)}) collective-permute-start(bf16[512,128]{1,0:T(8,128)(2,1)S(1)} %shard_map.98.refs_2_), channel_id=1, source_target_pairs={{0,1},{1,0},{2,3},{3,2},{4,5},{5,4},{6,7},{7,6},{8,9},{9,8},{10,11... | collective-permute-start | bytes 393224 | tf_op jit(solution)/shard_map/ppermute | solution.py:21
  27.6 1.4 %collective-permute-start.15 = (bf16[528,128]{1,0:T(8,128)(2,1)S(1)}, bf16[528,128]{1,0:T(8,128)(2,1)S(1)}, u32[]{:S(2)}, u32[]{:S(2)}) collective-permute-start(bf16[528,128]{1,0:T(8,128)(2,1)S(1)} %get-tuple-element.125), channel_id=1, source_target_pairs={{0,1},{1,0},{2,3},{3,2},{4,5},{5,4},{6,7},{7,6},{8,9},{9,8},{10,11... | collective-permute-start | bytes 405512 | tf_op jit(solution)/shard_map/ppermute | solution.py:21
  27.8 2.8 %collective-permute-start.16 = (bf16[528,128]{1,0:T(8,128)(2,1)S(1)}, bf16[528,128]{1,0:T(8,128)(2,1)S(1)}, u32[]{:S(2)}, u32[]{:S(2)}) collective-permute-start(bf16[528,128]{1,0:T(8,128)(2,1)S(1)} %get-tuple-element.129), channel_id=1, source_target_pairs={{0,1},{1,0},{2,3},{3,2},{4,5},{5,4},{6,7},{7,6},{8,9},{9,8},{10,11... | collective-permute-start | bytes 405512 | tf_op jit(solution)/shard_map/ppermute | solution.py:21
  29.0 5.7 %collective-permute-start.17 = (bf16[528,128]{1,0:T(8,128)(2,1)S(1)}, bf16[528,128]{1,0:T(8,128)(2,1)S(1)}, u32[]{:S(2)}, u32[]{:S(2)}) collective-permute-start(bf16[528,128]{1,0:T(8,128)(2,1)S(1)} %convert_add_fusion.1), channel_id=1, source_target_pairs={{0,2},{1,3},{2,0},{3,1},{4,6},{5,7},{6,4},{7,5},{8,10},{9,11},{10,... | collective-permute-start | bytes 405512 | tf_op jit(solution)/shard_map/ppermute | solution.py:21

commit v10 on v9

--- a/solution.py
+++ b/solution.py
@@ -10,7 +10,7 @@
 epsilon = 1e-06
 LANES = 128
 EXTRA = 16
-PIECE = 256
+PIECE = 512
 VM = pltpu.VMEM
 F32 = jnp.float32
 BF16 = jnp.bfloat16

time: 35.8 us -> 35.7 us (level)
  transfers between devices with their start and end apart: 18 -> 18, of which waited for: 7 -> 7; matrix products, arithmetic and copies ran while one was open for 0% -> 0% of each run, Pallas kernels for 41% -> 40%
where the time goes in v10:
time: 35.7 us; the launch traced here: 35.6 us
  Pallas kernels  16.8 us (47%)
  starting transfers between devices  10.5 us (29%)
  waiting for transfers between devices  7.98 us (22%)
    pallas_call x16, Pallas kernels, kernel_call(): pl.pallas_call(kernel, out_shape=list(outs) if many else outs, in_specs=[...  16.8 us
    ppermute x18, starting transfers between devices, hop(): return lax.ppermute(value, 'tensor', [(j, j ^ bit) for j in range(size)])  10.5 us
    ppermute x18, waiting for transfers between devices, hop(): return lax.ppermute(value, 'tensor', [(j, j ^ bit) for j in range(size)])  7.98 us
  transfers between devices with their start and end apart: 18, of which 7 were waited for; matrix products, arithmetic and copies ran while one was open for 0% of the time, Pallas kernels for 40%

profile of v10, /device:TPU:0, one launch (start us, length us, event | category | flops | bytes accessed | tf_op | source)
XLA Modules:
  0.0 35.6 jit_solution(14289502452286791083)
XLA Ops:
  0.0 0.5 %collective-permute-start.2 = (bf16[128,512]{1,0:T(8,128)(2,1)}, bf16[128,512]{1,0:T(8,128)(2,1)S(1)}, u32[]{:S(2)}, u32[]{:S(2)}) collective-permute-start(bf16[128,512]{1,0:T(8,128)(2,1)} %refs_2_.1), channel_id=1, source_target_pairs={{0,1},{1,0},{2,3},{3,2},{4,5},{5,4},{6,7},{7,6},{8,9},{9,8},{10,11... | collective-permute-start | bytes 393224 | tf_op jit(solution)/shard_map/ppermute | solution.py:21
  0.5 3.0 %collective-permute-start.1 = (bf16[128,512]{1,0:T(8,128)(2,1)}, bf16[128,512]{1,0:T(8,128)(2,1)S(1)}, u32[]{:S(2)}, u32[]{:S(2)}) collective-permute-start(bf16[128,512]{1,0:T(8,128)(2,1)} %refs_2_.1), channel_id=1, source_target_pairs={{0,2},{1,3},{2,0},{3,1},{4,6},{5,7},{6,4},{7,5},{8,10},{9,11},{10,... | collective-permute-start | bytes 393224 | tf_op jit(solution)/shard_map/ppermute | solution.py:21
  3.5 5.0 %shard_map.91 = (bf16[128,512]{1,0:T(8,128)(2,1)S(1)}, bf16[128,512]{1,0:T(8,128)(2,1)S(1)}, bf16[128,512]{1,0:T(8,128)(2,1)S(1)}, f32[1,2048]{1,0:T(1,128)S(1)}...) custom-call(bf16[128,512]{1,0:T(8,128)(2,1)S(1)} %collective-permute, ...), custom_call_target="tpu_custom_call" | custom-call | flops 805306368 | tf_op jit(solution)/shard_map/pallas_call | solution.py:44
  8.6 0.5 %collective-permute-start.11 = (bf16[128,512]{1,0:T(8,128)(2,1)S(1)}, bf16[128,512]{1,0:T(8,128)(2,1)S(1)}, u32[]{:S(2)}, u32[]{:S(2)}) collective-permute-start(bf16[128,512]{1,0:T(8,128)(2,1)S(1)} %get-tuple-element.106.refs_0_), channel_id=1, source_target_pairs={{0,1},{1,0},{2,3},{3,2},{4,5},{5,4},{6,7},{7,6},{8,9},{9,8},{10,11... | collective-permute-start | bytes 393224 | tf_op jit(solution)/shard_map/ppermute | solution.py:21
  9.1 2.0 %collective-permute-start.12 = (bf16[128,512]{1,0:T(8,128)(2,1)S(1)}, bf16[128,512]{1,0:T(8,128)(2,1)S(1)}, u32[]{:S(2)}, u32[]{:S(2)}) collective-permute-start(bf16[128,512]{1,0:T(8,128)(2,1)S(1)} %get-tuple-element.106.refs_0_), channel_id=1, source_target_pairs={{0,2},{1,3},{2,0},{3,1},{4,6},{5,7},{6,4},{7,5},{8,10},{9,11},{10,... | collective-permute-start | bytes 393224 | tf_op jit(solution)/shard_map/ppermute | solution.py:21
  11.1 1.1 %shard_map.92 = (f32[1024,128]{1,0:T(8,128)S(1)}, f32[1024,128]{1,0:T(8,128)S(1)}, f32[1024,128]{1,0:T(8,128)S(1)}, f32[1024,128]{1,0:T(8,128)S(1)}, f32[8,128]{1,0:T(8,128)S(1)}) custom-call(bf16[128,512]{1,0:T(8,128)(2,1)S(1)} %collective-permute-done.1.refs_0_.refs_1_, bf16[128,512]{1,0:T(8,128)(2,1)S(1)} %collective-permute-done.5.refs_1_, ...), custom_call_target="tpu_custom_call" | custom-call | flops 3221225472 | tf_op jit(solution)/shard_map/pallas_call | solution.py:44
  12.2 0.2 collective-permute-done.4.refs_1_
  12.4 1.8 %shard_map.93 = (bf16[1024,128]{1,0:T(8,128)(2,1)S(1)}, bf16[1024,128]{1,0:T(8,128)(2,1)S(1)}, f32[16,128]{1,0:T(8,128)S(1)}, bf16[528,128]{1,0:T(8,128)(2,1)S(1)}, bf16[528,128]{1,0:T(8,128)(2,1)S(1)}) custom-call(bf16[128,512]{1,0:T(8,128)(2,1)S(1)} %collective-permute-done.refs_0_.second, bf16[128,512]{1,0:T(8,128)(2,1)S(1)} %collective-permute-done.4.refs_1_, ...), custom_call_target="tpu_custom_call" | custom-call | flops 3221225472 | tf_op jit(solution)/shard_map/pallas_call | solution.py:44
  14.3 0.4 %collective-permute-start.6 = (bf16[528,128]{1,0:T(8,128)(2,1)S(1)}, bf16[528,128]{1,0:T(8,128)(2,1)S(1)}, u32[]{:S(2)}, u32[]{:S(2)}) collective-permute-start(bf16[528,128]{1,0:T(8,128)(2,1)S(1)} %get-tuple-element.89), channel_id=1, source_target_pairs={{0,1},{1,0},{2,3},{3,2},{4,5},{5,4},{6,7},{7,6},{8,9},{9,8},{10,11... | collective-permute-start | bytes 405512 | tf_op jit(solution)/shard_map/ppermute | solution.py:21
  14.6 0.2 collective-permute-start.7
  14.8 0.7 %shard_map.94 = f32[528,128]{1,0:T(8,128)S(1)} custom-call(bf16[1024,128]{1,0:T(8,128)(2,1)S(1)} %get-tuple-element.92.gg_ref, bf16[1024,128]{1,0:T(8,128)(2,1)S(1)} %get-tuple-element.93.gu_ref, f32[16,128]{1,0:T(8,128)S(1)} %get-tuple-element.94.sums_ref, bf16[2048,1024]{1,0:T(8,128)(2,1)S(1)} %get-tuple-element.77.refs_4_.refs_8_.gate_w.refs_6_.refs_7_, ...), custom_call_target="tpu_custom_call" | custom-call | flops 1610612736 | tf_op jit(solution)/shard_map/pallas_call | solution.py:44
  15.6 0.1 collective-permute-done.6
  15.7 1.0 %collective-permute-start.10 = (bf16[528,128]{1,0:T(8,128)(2,1)S(1)}, bf16[528,128]{1,0:T(8,128)(2,1)S(1)}, u32[]{:S(2)}, u32[]{:S(2)}) collective-permute-start(bf16[528,128]{1,0:T(8,128)(2,1)S(1)} %get-tuple-element.135), channel_id=1, source_target_pairs={{0,2},{1,3},{2,0},{3,1},{4,6},{5,7},{6,4},{7,5},{8,10},{9,11},{10,... | collective-permute-start | bytes 405512 | tf_op jit(solution)/shard_map/ppermute | solution.py:21
  16.7 0.7 %shard_map.95 = f32[528,128]{1,0:T(8,128)S(1)} custom-call(bf16[1024,128]{1,0:T(8,128)(2,1)S(1)} %get-tuple-element.92.gg_ref, bf16[1024,128]{1,0:T(8,128)(2,1)S(1)} %get-tuple-element.93.gu_ref, f32[16,128]{1,0:T(8,128)S(1)} %get-tuple-element.94.sums_ref, bf16[2048,1024]{1,0:T(8,128)(2,1)S(1)} %get-tuple-element.77.refs_4_.refs_8_.gate_w.refs_6_.refs_7_, ...), custom_call_target="tpu_custom_call" | custom-call | flops 1610612736 | tf_op jit(solution)/shard_map/pallas_call | solution.py:44
  17.5 1.2 %collective-permute-start.8 = (bf16[528,128]{1,0:T(8,128)(2,1)S(1)}, bf16[528,128]{1,0:T(8,128)(2,1)S(1)}, u32[]{:S(2)}, u32[]{:S(2)}) collective-permute-start(bf16[528,128]{1,0:T(8,128)(2,1)S(1)} %convert_element_type.23), channel_id=1, source_target_pairs={{0,2},{1,3},{2,0},{3,1},{4,6},{5,7},{6,4},{7,5},{8,10},{9,11},{10,... | collective-permute-start | bytes 405512 | tf_op jit(solution)/shard_map/ppermute | solution.py:21
  18.7 0.4 %shard_map.97 = (f32[512,128]{1,0:T(8,128)S(1)}, f32[512,128]{1,0:T(8,128)S(1)}, f32[512,128]{1,0:T(8,128)S(1)}, f32[512,128]{1,0:T(8,128)S(1)}, f32[512,128]{1,0:T(8,128)S(1)}, /*index=5*/f32[512,128]{1,0:T(8,128)S(1)}) custom-call(bf16[128,512]{1,0:T(8,128)(2,1)S(1)} %get-tuple-element.101.refs_0_, ...), custom_call_target="tpu_custom_call" | custom-call | tf_op jit(solution)/shard_map/pallas_call | solution.py:44
  19.2 0.1 shard_map.96
  19.3 1.7 %shard_map.99 = (f32[1024,128]{1,0:T(8,128)S(1)}, f32[1024,128]{1,0:T(8,128)S(1)}, f32[1024,128]{1,0:T(8,128)S(1)}, f32[1024,128]{1,0:T(8,128)S(1)}, f32[8,128]{1,0:T(8,128)S(1)}) custom-call(bf16[128,512]{1,0:T(8,128)(2,1)S(1)} %get-tuple-element.106.refs_0_, bf16[128,512]{1,0:T(8,128)(2,1)S(1)} %collective-permute-done.11.refs_1_, ...), custom_call_target="tpu_custom_call" | custom-call | tf_op jit(solution)/shard_map/pallas_call | solution.py:44
  21.0 1.2 %collective-permute-done.10.got = bf16[528,128]{1,0:T(8,128)(2,1)S(1)} collective-permute-done((bf16[528,128]{1,0:T(8,128)(2,1)S(1)}, bf16[528,128]{1,0:T(8,128)(2,1)S(1)}, u32[]{:S(2)}, u32[]{:S(2)}) %collective-permute-start.10) | collective-permute-done | bytes 135200 | tf_op jit(solution)/shard_map/ppermute | solution.py:21
  22.4 2.1 %collective-permute-done.8.got = bf16[528,128]{1,0:T(8,128)(2,1)S(1)} collective-permute-done((bf16[528,128]{1,0:T(8,128)(2,1)S(1)}, bf16[528,128]{1,0:T(8,128)(2,1)S(1)}, u32[]{:S(2)}, u32[]{:S(2)}) %collective-permute-start.8) | collective-permute-done | bytes 135200 | tf_op jit(solution)/shard_map/ppermute | solution.py:21
  24.7 1.0 %shard_map.101.refs_2_ = f32[1024,128]{1,0:T(8,128)S(1)} custom-call(bf16[512,128]{1,0:T(8,128)(2,1)S(1)} %shard_map.100.refs_0_.second, bf16[512,128]{1,0:T(8,128)(2,1)S(1)} %collective-permute-done.14.refs_1_, bf16[512,128]{1,0:T(8,128)(2,1)S(1)} %shard_map.98.refs_2_, bf16[1024,2048]{1,0:T(8,128)(2,1)S(1)} %get-tuple-element.73.refs_2_.refs_3_.refs_1_), custom_call_target="tpu_custom_call" | custom-call | flops 1610612736 | tf_op jit(solution)/shard_map/pallas_call | solution.py:44
  25.7 0.3 collective-permute-done.9.refs_0_
  26.0 1.5 %shard_map.102 = (bf16[1024,128]{1,0:T(8,128)(2,1)S(1)}, bf16[1024,128]{1,0:T(8,128)(2,1)S(1)}, f32[16,128]{1,0:T(8,128)S(1)}, bf16[528,128]{1,0:T(8,128)(2,1)S(1)}, bf16[528,128]{1,0:T(8,128)(2,1)S(1)}) custom-call(bf16[512,128]{1,0:T(8,128)(2,1)S(1)} %collective-permute-done.9.refs_0_, bf16[1024,2048]{1,0:T(8,128)(2,1)S(1)} %get-tuple-element.73.refs_2_.refs_3_.refs_1_, ...), custom_call_target="tpu_custom_call" | custom-call | flops 3221225472 | tf_op jit(solution)/shard_map/pallas_call | solution.py:44
  27.5 0.2 collective-permute-start.15
  27.8 0.3 collective-permute-start.16
  28.1 0.7 %shard_map.103 = f32[528,128]{1,0:T(8,128)S(1)} custom-call(bf16[1024,128]{1,0:T(8,128)(2,1)S(1)} %get-tuple-element.126.gg_ref, bf16[1024,128]{1,0:T(8,128)(2,1)S(1)} %get-tuple-element.127.gu_ref, f32[16,128]{1,0:T(8,128)S(1)} %get-tuple-element.128.sums_ref, bf16[2048,1024]{1,0:T(8,128)(2,1)S(1)} %get-tuple-element.77.refs_4_.refs_8_.gate_w.refs_6_.refs_7_, ...), custom_call_target="tpu_custom_call" | custom-call | flops 1610612736 | tf_op jit(solution)/shard_map/pallas_call | solution.py:44
  28.8 0.1 collective-permute-done.15
  29.0 0.9 %collective-permute-start.17 = (bf16[528,128]{1,0:T(8,128)(2,1)S(1)}, bf16[528,128]{1,0:T(8,128)(2,1)S(1)}, u32[]{:S(2)}, u32[]{:S(2)}) collective-permute-start(bf16[528,128]{1,0:T(8,128)(2,1)S(1)} %convert_add_fusion.1), channel_id=1, source_target_pairs={{0,2},{1,3},{2,0},{3,1},{4,6},{5,7},{6,4},{7,5},{8,10},{9,11},{10,... | collective-permute-start | bytes 405512 | tf_op jit(solution)/shard_map/ppermute | solution.py:21
  29.9 0.7 %shard_map.104 = f32[528,128]{1,0:T(8,128)S(1)} custom-call(bf16[1024,128]{1,0:T(8,128)(2,1)S(1)} %get-tuple-element.126.gg_ref, bf16[1024,128]{1,0:T(8,128)(2,1)S(1)} %get-tuple-element.127.gu_ref, f32[16,128]{1,0:T(8,128)S(1)} %get-tuple-element.128.sums_ref, bf16[2048,1024]{1,0:T(8,128)(2,1)S(1)} %get-tuple-element.77.refs_4_.refs_8_.gate_w.refs_6_.refs_7_, ...), custom_call_target="tpu_custom_call" | custom-call | flops 1610612736 | tf_op jit(solution)/shard_map/pallas_call | solution.py:44
  30.6 0.2 shard_map.105
  30.9 3.9 %collective-permute-done.17.got = bf16[528,128]{1,0:T(8,128)(2,1)S(1)} collective-permute-done((bf16[528,128]{1,0:T(8,128)(2,1)S(1)}, bf16[528,128]{1,0:T(8,128)(2,1)S(1)}, u32[]{:S(2)}, u32[]{:S(2)}) %collective-permute-start.17) | collective-permute-done | bytes 135200 | tf_op jit(solution)/shard_map/ppermute | solution.py:21
  34.7 0.8 %shard_map.106 = bf16[128,512]{1,0:T(8,128)(2,1)} custom-call(f32[528,128]{1,0:T(8,128)S(1)} %convert_add_fusion.chip, bf16[528,128]{1,0:T(8,128)(2,1)S(1)} %collective-permute-done.17.got, bf16[512,128]{1,0:T(8,128)(2,1)S(1)} %shard_map.100.refs_0_.second, f32[512,128]{1,0:T(8,128)S(1)} %get-tuple-element.132.x, f32[512,128]{1,0:T(8,128)S(1)} %get-tuple-element.133.scale, ...), custom_call_target="tpu_custom_call" | custom-call | tf_op jit(solution)/shard_map/pallas_call | solution.py:44
  (25 shorter events, 0.8 us)
Async XLA Ops:
  0.0 3.5 %collective-permute-start.2 = (bf16[128,512]{1,0:T(8,128)(2,1)}, bf16[128,512]{1,0:T(8,128)(2,1)S(1)}, u32[]{:S(2)}, u32[]{:S(2)}) collective-permute-start(bf16[128,512]{1,0:T(8,128)(2,1)} %refs_2_.1), channel_id=1, source_target_pairs={{0,1},{1,0},{2,3},{3,2},{4,5},{5,4},{6,7},{7,6},{8,9},{9,8},{10,11... | collective-permute-start | bytes 393224 | tf_op jit(solution)/shard_map/ppermute | solution.py:21
  0.5 3.1 %collective-permute-start.3 = (bf16[128,512]{1,0:T(8,128)(2,1)}, bf16[128,512]{1,0:T(8,128)(2,1)S(1)}, u32[]{:S(2)}, u32[]{:S(2)}) collective-permute-start(bf16[128,512]{1,0:T(8,128)(2,1)} %refs_3_.1), channel_id=1, source_target_pairs={{0,1},{1,0},{2,3},{3,2},{4,5},{5,4},{6,7},{7,6},{8,9},{9,8},{10,11... | collective-permute-start | bytes 393224 | tf_op jit(solution)/shard_map/ppermute | solution.py:21
  0.5 8.0 %collective-permute-start.1 = (bf16[128,512]{1,0:T(8,128)(2,1)}, bf16[128,512]{1,0:T(8,128)(2,1)S(1)}, u32[]{:S(2)}, u32[]{:S(2)}) collective-permute-start(bf16[128,512]{1,0:T(8,128)(2,1)} %refs_2_.1), channel_id=1, source_target_pairs={{0,2},{1,3},{2,0},{3,1},{4,6},{5,7},{6,4},{7,5},{8,10},{9,11},{10,... | collective-permute-start | bytes 393224 | tf_op jit(solution)/shard_map/ppermute | solution.py:21
  3.5 7.6 %collective-permute-start = (bf16[128,512]{1,0:T(8,128)(2,1)}, bf16[128,512]{1,0:T(8,128)(2,1)S(1)}, u32[]{:S(2)}, u32[]{:S(2)}) collective-permute-start(bf16[128,512]{1,0:T(8,128)(2,1)} %refs_3_.1), channel_id=1, source_target_pairs={{0,2},{1,3},{2,0},{3,1},{4,6},{5,7},{6,4},{7,5},{8,10},{9,11},{10,... | collective-permute-start | bytes 393224 | tf_op jit(solution)/shard_map/ppermute | solution.py:21
  8.5 2.6 %collective-permute-start.5 = (bf16[128,512]{1,0:T(8,128)(2,1)S(1)}, bf16[128,512]{1,0:T(8,128)(2,1)S(1)}, u32[]{:S(2)}, u32[]{:S(2)}) collective-permute-start(bf16[128,512]{1,0:T(8,128)(2,1)S(1)} %collective-permute-done.1.refs_0_.refs_1_), channel_id=1, source_target_pairs={{0,1},{1,0},{2,3},{3,2},{4,5},{5,4},{6,7},{7,6},{8,9},{9,8},{10,11... | collective-permute-start | bytes 393224 | tf_op jit(solution)/shard_map/ppermute | solution.py:21
  8.6 10.7 %collective-permute-start.11 = (bf16[128,512]{1,0:T(8,128)(2,1)S(1)}, bf16[128,512]{1,0:T(8,128)(2,1)S(1)}, u32[]{:S(2)}, u32[]{:S(2)}) collective-permute-start(bf16[128,512]{1,0:T(8,128)(2,1)S(1)} %get-tuple-element.106.refs_0_), channel_id=1, source_target_pairs={{0,1},{1,0},{2,3},{3,2},{4,5},{5,4},{6,7},{7,6},{8,9},{9,8},{10,11... | collective-permute-start | bytes 393224 | tf_op jit(solution)/shard_map/ppermute | solution.py:21
  9.1 6.5 %collective-permute-start.12 = (bf16[128,512]{1,0:T(8,128)(2,1)S(1)}, bf16[128,512]{1,0:T(8,128)(2,1)S(1)}, u32[]{:S(2)}, u32[]{:S(2)}) collective-permute-start(bf16[128,512]{1,0:T(8,128)(2,1)S(1)} %get-tuple-element.106.refs_0_), channel_id=1, source_target_pairs={{0,2},{1,3},{2,0},{3,1},{4,6},{5,7},{6,4},{7,5},{8,10},{9,11},{10,... | collective-permute-start | bytes 393224 | tf_op jit(solution)/shard_map/ppermute | solution.py:21
  11.1 1.3 %collective-permute-start.4 = (bf16[128,512]{1,0:T(8,128)(2,1)S(1)}, bf16[128,512]{1,0:T(8,128)(2,1)S(1)}, u32[]{:S(2)}, u32[]{:S(2)}) collective-permute-start(bf16[128,512]{1,0:T(8,128)(2,1)S(1)} %collective-permute-done.refs_0_.second), channel_id=1, source_target_pairs={{0,1},{1,0},{2,3},{3,2},{4,5},{5,4},{6,7},{7,6},{8,9},{9,8},{10,11... | collective-permute-start | bytes 393224 | tf_op jit(solution)/shard_map/ppermute | solution.py:21
  14.3 1.4 %collective-permute-start.6 = (bf16[528,128]{1,0:T(8,128)(2,1)S(1)}, bf16[528,128]{1,0:T(8,128)(2,1)S(1)}, u32[]{:S(2)}, u32[]{:S(2)}) collective-permute-start(bf16[528,128]{1,0:T(8,128)(2,1)S(1)} %get-tuple-element.89), channel_id=1, source_target_pairs={{0,1},{1,0},{2,3},{3,2},{4,5},{5,4},{6,7},{7,6},{8,9},{9,8},{10,11... | collective-permute-start | bytes 405512 | tf_op jit(solution)/shard_map/ppermute | solution.py:21
  14.6 2.8 %collective-permute-start.7 = (bf16[528,128]{1,0:T(8,128)(2,1)S(1)}, bf16[528,128]{1,0:T(8,128)(2,1)S(1)}, u32[]{:S(2)}, u32[]{:S(2)}) collective-permute-start(bf16[528,128]{1,0:T(8,128)(2,1)S(1)} %get-tuple-element.95), channel_id=1, source_target_pairs={{0,1},{1,0},{2,3},{3,2},{4,5},{5,4},{6,7},{7,6},{8,9},{9,8},{10,11... | collective-permute-start | bytes 405512 | tf_op jit(solution)/shard_map/ppermute | solution.py:21
  15.7 6.5 %collective-permute-start.10 = (bf16[528,128]{1,0:T(8,128)(2,1)S(1)}, bf16[528,128]{1,0:T(8,128)(2,1)S(1)}, u32[]{:S(2)}, u32[]{:S(2)}) collective-permute-start(bf16[528,128]{1,0:T(8,128)(2,1)S(1)} %get-tuple-element.135), channel_id=1, source_target_pairs={{0,2},{1,3},{2,0},{3,1},{4,6},{5,7},{6,4},{7,5},{8,10},{9,11},{10,... | collective-permute-start | bytes 405512 | tf_op jit(solution)/shard_map/ppermute | solution.py:21
  17.4 1.9 %collective-permute-start.13 = (bf16[128,512]{1,0:T(8,128)(2,1)S(1)}, bf16[128,512]{1,0:T(8,128)(2,1)S(1)}, u32[]{:S(2)}, u32[]{:S(2)}) collective-permute-start(bf16[128,512]{1,0:T(8,128)(2,1)S(1)} %collective-permute-done.12.refs_2_), channel_id=1, source_target_pairs={{0,1},{1,0},{2,3},{3,2},{4,5},{5,4},{6,7},{7,6},{8,9},{9,8},{10,11... | collective-permute-start | bytes 393224 | tf_op jit(solution)/shard_map/ppermute | solution.py:21
  17.5 6.9 %collective-permute-start.8 = (bf16[528,128]{1,0:T(8,128)(2,1)S(1)}, bf16[528,128]{1,0:T(8,128)(2,1)S(1)}, u32[]{:S(2)}, u32[]{:S(2)}) collective-permute-start(bf16[528,128]{1,0:T(8,128)(2,1)S(1)} %convert_element_type.23), channel_id=1, source_target_pairs={{0,2},{1,3},{2,0},{3,1},{4,6},{5,7},{6,4},{7,5},{8,10},{9,11},{10,... | collective-permute-start | bytes 405512 | tf_op jit(solution)/shard_map/ppermute | solution.py:21
  22.3 2.3 %collective-permute-start.14 = (bf16[512,128]{1,0:T(8,128)(2,1)S(1)}, bf16[512,128]{1,0:T(8,128)(2,1)S(1)}, u32[]{:S(2)}, u32[]{:S(2)}) collective-permute-start(bf16[512,128]{1,0:T(8,128)(2,1)S(1)} %shard_map.100.refs_0_.second), channel_id=1, source_target_pairs={{0,1},{1,0},{2,3},{3,2},{4,5},{5,4},{6,7},{7,6},{8,9},{9,8},{10,11... | collective-permute-start | bytes 393224 | tf_op jit(solution)/shard_map/ppermute | solution.py:21
  24.6 1.4 %collective-permute-start.9 = (bf16[512,128]{1,0:T(8,128)(2,1)S(1)}, bf16[512,128]{1,0:T(8,128)(2,1)S(1)}, u32[]{:S(2)}, u32[]{:S(2)}) collective-permute-start(bf16[512,128]{1,0:T(8,128)(2,1)S(1)} %shard_map.98.refs_2_), channel_id=1, source_target_pairs={{0,1},{1,0},{2,3},{3,2},{4,5},{5,4},{6,7},{7,6},{8,9},{9,8},{10,11... | collective-permute-start | bytes 393224 | tf_op jit(solution)/shard_map/ppermute | solution.py:21
  27.5 1.4 %collective-permute-start.15 = (bf16[528,128]{1,0:T(8,128)(2,1)S(1)}, bf16[528,128]{1,0:T(8,128)(2,1)S(1)}, u32[]{:S(2)}, u32[]{:S(2)}) collective-permute-start(bf16[528,128]{1,0:T(8,128)(2,1)S(1)} %get-tuple-element.125), channel_id=1, source_target_pairs={{0,1},{1,0},{2,3},{3,2},{4,5},{5,4},{6,7},{7,6},{8,9},{9,8},{10,11... | collective-permute-start | bytes 405512 | tf_op jit(solution)/shard_map/ppermute | solution.py:21
  27.8 2.8 %collective-permute-start.16 = (bf16[528,128]{1,0:T(8,128)(2,1)S(1)}, bf16[528,128]{1,0:T(8,128)(2,1)S(1)}, u32[]{:S(2)}, u32[]{:S(2)}) collective-permute-start(bf16[528,128]{1,0:T(8,128)(2,1)S(1)} %get-tuple-element.129), channel_id=1, source_target_pairs={{0,1},{1,0},{2,3},{3,2},{4,5},{5,4},{6,7},{7,6},{8,9},{9,8},{10,11... | collective-permute-start | bytes 405512 | tf_op jit(solution)/shard_map/ppermute | solution.py:21
  29.0 5.7 %collective-permute-start.17 = (bf16[528,128]{1,0:T(8,128)(2,1)S(1)}, bf16[528,128]{1,0:T(8,128)(2,1)S(1)}, u32[]{:S(2)}, u32[]{:S(2)}) collective-permute-start(bf16[528,128]{1,0:T(8,128)(2,1)S(1)} %convert_add_fusion.1), channel_id=1, source_target_pairs={{0,2},{1,3},{2,0},{3,1},{4,6},{5,7},{6,4},{7,5},{8,10},{9,11},{10,... | collective-permute-start | bytes 405512 | tf_op jit(solution)/shard_map/ppermute | solution.py:21
